TPU v7x, 32 devices: a whole 2x2x4 slice. The times are simulated.
32 devices in a mesh: seq: 4 (over z), fsdp: 8 (over y, x, core).
Axes of the slice: x: 2, y: 2, z: 4, core: 2. Of those that a mesh axis runs over, the one named last changes fastest.
Arguments:
- inputs: bfloat16 [16, 1024, 1024], P('fsdp', 'seq'), may hold values from -6 to 6
- lengths: int32 [16], P('fsdp'), may hold values from 512 to 1024, as said below
- ffn_in: bfloat16 [2, 1024, 4096], P(None, 'fsdp'), may hold values from -0.1875 to 0.1875
- ffn_in_bias: bfloat16 [2, 4096], P(None, 'fsdp'), may hold values from -3 to 3
- ffn_out: bfloat16 [2, 4096, 1024], P(None, 'fsdp'), may hold values from -0.09375 to 0.09375
- qkv: bfloat16 [3, 1024, 1024], P(None, 'fsdp'), may hold values from -0.1875 to 0.1875
- attn_out: bfloat16 [1024, 1024], P('fsdp'), may hold values from -0.75 to 0.75
- conv_in: bfloat16 [1024, 2048], P('fsdp'), may hold values from -0.1875 to 0.1875
- conv_out: bfloat16 [1024, 1024], P('fsdp'), may hold values from -0.1875 to 0.1875
- depthwise: bfloat16 [31, 1024], P(None, 'fsdp'), may hold values from -1 to 1
- gains: bfloat16 [6, 1024], P(None, 'fsdp'), may hold values from 0.099609375 to 1.8984375
- shifts: bfloat16 [15, 1024], P(None, 'fsdp'), may hold values from -2 to 2
- distance: bfloat16 [73, 64], replicated, may hold values from -6 to 6
- grad_out: bfloat16 [16, 1024, 1024], P('fsdp', 'seq'), may hold values from -6 to 6
Outputs:
- outputs: bfloat16 [16, 1024, 1024], P('fsdp', 'seq')
- grad_inputs: bfloat16 [16, 1024, 1024], P('fsdp', 'seq')
- grad_ffn_in: float32 [2, 1024, 4096], P(None, 'fsdp')
- grad_ffn_in_bias: float32 [2, 4096], P(None, 'fsdp')
- grad_ffn_out: float32 [2, 4096, 1024], P(None, 'fsdp')
- grad_qkv: float32 [3, 1024, 1024], P(None, 'fsdp')
- grad_attn_out: float32 [1024, 1024], P('fsdp')
- grad_conv_in: float32 [1024, 2048], P('fsdp')
- grad_conv_out: float32 [1024, 1024], P('fsdp')
- grad_depthwise: float32 [31, 1024], P(None, 'fsdp')
- grad_gains: float32 [6, 1024], P(None, 'fsdp')
- grad_shifts: float32 [15, 1024], P(None, 'fsdp')
- grad_distance: float32 [73, 64], replicated
Inputs may be any that keep to these rules, and one draw needn't show every extreme that they name: `lengths`: in each group of 2 sequences held by one index of fsdp, one sequence, drawn from the seed, has all 1024 tokens.
All inputs are finite; a program needn't handle non-finite values.
Results may differ from a plain program's by a relative error of at most 0.024.
Values may be sent and summed in bfloat16 or wider, within the bound.
A program may use at most 376 MiB of HBM per device.

v0:
```python
import jax
import jax.numpy as jnp
from jax import lax
from jax.sharding import PartitionSpec as P

HEAD_DIM = 64
LEFT = 64
RIGHT = 8


PRECISION = lax.Precision.DEFAULT
EPSILON = 1e-05


def from_behind(block, axis, distance):
    devices = range(lax.axis_size(axis))
    route = [(i - distance, i) for i in devices if i - distance in devices]
    return lax.ppermute(block, axis, route)


def shortened(shard):

    def short(part):
        return part.astype(jnp.bfloat16) if part.dtype == jnp.float32 else part

    return jax.tree.map(short, shard)


def plain_round(v):
    return lax.optimization_barrier(v.astype(jnp.bfloat16)).astype(jnp.float32)


def plain_same(v):
    return v


def value_keep(v):
    return (plain_round(v), None)


def value_pass(kept, grad):
    return (grad,)


def grad_keep(v):
    return (v, None)


def grad_lower(kept, grad):
    return (plain_round(grad),)


def round_value(v):
    wrapped = jax.custom_vjp(plain_round)
    wrapped.defvjp(value_keep, value_pass)
    return wrapped(v)


def round_grad(v):
    wrapped = jax.custom_vjp(plain_same)
    wrapped.defvjp(grad_keep, grad_lower)
    return wrapped(v)


def product(left, right):
    return jnp.einsum("...d,df->...f", left, right, precision=PRECISION)


def layer_norm(values, gain, shift):
    centred = values - jnp.mean(values, axis=-1, keepdims=True)
    spread = jnp.mean(centred * centred, axis=-1, keepdims=True)
    return centred * lax.rsqrt(spread + EPSILON) * gain + shift


def feed_forward(values, w_inner, b_inner, w_outer, b_outer, gain, shift):
    normed = round_value(layer_norm(values, gain, shift))
    inner = round_grad(product(normed, w_inner) + b_inner)
    active = round_value(jax.nn.silu(inner))
    return round_grad(product(active, w_outer) + b_outer)


def front_part(tokens, w_inner, b_inner, w_outer, projections, gain_rows, shift_rows):
    first_sum = tokens + 0.5 * feed_forward(
        tokens, w_inner, b_inner, w_outer, shift_rows[6], gain_rows[0], shift_rows[0]
    )
    normed = round_value(layer_norm(first_sum, gain_rows[1], shift_rows[1]))
    query = round_value(round_grad(product(normed, projections[0]) + shift_rows[8]))
    key_rows = round_value(round_grad(product(normed, projections[1])))
    value = round_value(round_grad(product(normed, projections[2]) + shift_rows[9]))
    return (first_sum, query, key_rows, value)


def place_band(relative, start, block_rows, token_count):
    heads_here = relative.shape[0]
    row_width = token_count + block_rows - 1
    wide = jnp.zeros((heads_here, block_rows, row_width + LEFT + RIGHT), jnp.float32)
    wide = lax.dynamic_update_slice(
        wide, relative, (jnp.int32(0), jnp.int32(0), (start + block_rows - 1).astype(jnp.int32))
    )
    rows = wide[:, :, LEFT : LEFT + row_width]
    flat = rows.reshape(heads_here, block_rows * row_width)
    skewed = flat[:, block_rows - 1 : block_rows - 1 + block_rows * (row_width - 1)]
    return skewed.reshape(heads_here, block_rows, row_width - 1)[:, :, :token_count]


def attend(query, key_rows, value, table, length):
    token_count = query.shape[0]
    heads_here = query.shape[1] // HEAD_DIM
    query_heads = query.reshape(token_count, heads_here, HEAD_DIM)
    key_heads = key_rows.reshape(token_count, heads_here, HEAD_DIM)
    value_heads = value.reshape(token_count, heads_here, HEAD_DIM)
    block_rows = min(512, token_count)
    positions = jnp.arange(token_count, dtype=jnp.int32)
    key_valid = positions < length

    def one_block(start):
        rows_query = lax.dynamic_slice_in_dim(query_heads, start, block_rows, 0)
        row_index = start + jnp.arange(block_rows, dtype=jnp.int32)
        apart = positions[None, :] - row_index[:, None]
        scores = jnp.einsum("bhd,nhd->hbn", rows_query, key_heads, precision=PRECISION)
        relative = jnp.einsum("bhd,rd->hbr", rows_query, table, precision=PRECISION)
        band = place_band(relative, start, block_rows, token_count)
        placed = jnp.where(
            apart[None] <= -LEFT,
            relative[:, :, 0:1],
            jnp.where(apart[None] >= RIGHT, relative[:, :, LEFT + RIGHT : LEFT + RIGHT + 1], band),
        )
        scores = round_grad((scores + placed) * HEAD_DIM ** (-0.5))
        scores = jnp.where(key_valid[None, None, :], scores, -1e30)
        row_max = jnp.max(scores, axis=2, keepdims=True)
        probs = jnp.exp(scores - row_max)
        probs = probs / jnp.sum(probs, axis=2, keepdims=True)
        mixed_rows = jnp.einsum(
            "hbn,nhd->bhd", round_value(probs), value_heads, precision=PRECISION
        )
        return mixed_rows.reshape(block_rows, heads_here * HEAD_DIM)

    starts = jnp.arange(0, token_count, block_rows, dtype=jnp.int32)
    return lax.map(jax.checkpoint(one_block), starts).reshape(token_count, heads_here * HEAD_DIM)


def attention_heads(query, key_rows, value, table, lengths):
    rounded_table = round_value(table)
    mixed = lax.map(
        lambda sequence: attend(sequence[0], sequence[1], sequence[2], rounded_table, sequence[3]),
        (query, key_rows, value, lengths),
    )
    return round_value(round_grad(mixed))


def middle_part(first_sum, mixed, w_attn_out, w_conv_in, gain_rows, shift_rows):
    second_sum = first_sum + round_grad(product(mixed, w_attn_out) + shift_rows[10])
    normed = round_value(layer_norm(second_sum, gain_rows[2], shift_rows[2]))
    bias_both = jnp.concatenate([shift_rows[11], shift_rows[12]])
    inner = round_grad(product(normed, w_conv_in) + bias_both)
    width = first_sum.shape[-1]
    gated = round_value(inner[..., :width] * jax.nn.sigmoid(inner[..., width:]))
    return (second_sum, gated)


def back_part(
    second_sum, gated, halo, taps, w_conv_out, w_inner, b_inner, w_outer, gain_rows, shift_rows
):
    count = second_sum.shape[-2]
    padded = jnp.concatenate([halo, gated], axis=-2)
    conv = shift_rows[13] + taps[0] * padded[..., 0:count, :]
    for tap in range(1, taps.shape[0]):
        conv = conv + taps[tap] * padded[..., tap : tap + count, :]
    active = round_value(jax.nn.silu(layer_norm(conv, gain_rows[3], shift_rows[3])))
    third_sum = second_sum + round_grad(product(active, w_conv_out) + shift_rows[14])
    fourth_sum = third_sum + 0.5 * feed_forward(
        third_sum, w_inner, b_inner, w_outer, shift_rows[7], gain_rows[4], shift_rows[4]
    )
    return layer_norm(fourth_sum, gain_rows[5], shift_rows[5])


def widened(piece, dim, factor):
    shape = list(piece.shape)
    shape[dim] = shape[dim] * factor
    return jnp.zeros(tuple(shape), jnp.float32)


def on_device(
    inputs,
    lengths,
    ffn_in,
    ffn_in_bias,
    ffn_out,
    qkv,
    attn_out,
    conv_in,
    conv_out,
    depthwise,
    gains,
    shifts,
    distance,
    grad_out,
):
    shards = (
        ffn_in,
        ffn_in_bias,
        ffn_out,
        qkv,
        attn_out,
        conv_in,
        conv_out,
        depthwise,
        gains,
        shifts,
    )
    shard_dims = (1, 1, 1, 1, 0, 0, 0, 1, 1, 1)
    factor = lax.axis_size("fsdp")
    table = distance.astype(jnp.float32)
    reach = depthwise.shape[0] - 1

    def micro_step(totals, batch):
        tokens_half, lengths_one, cotangent = batch
        whole = (
            lax.all_gather(ffn_in, "fsdp", axis=1, tiled=True),
            lax.all_gather(ffn_in_bias, "fsdp", axis=1, tiled=True),
            lax.all_gather(ffn_out, "fsdp", axis=1, tiled=True),
            lax.all_gather(qkv, "fsdp", axis=1, tiled=True),
            lax.all_gather(attn_out, "fsdp", axis=0, tiled=True),
            lax.all_gather(conv_in, "fsdp", axis=0, tiled=True),
            lax.all_gather(conv_out, "fsdp", axis=0, tiled=True),
            lax.all_gather(depthwise, "fsdp", axis=1, tiled=True),
            lax.all_gather(gains, "fsdp", axis=1, tiled=True),
            lax.all_gather(shifts, "fsdp", axis=1, tiled=True),
        )
        weights = tuple((piece.astype(jnp.float32) for piece in whole))
        tokens = tokens_half.astype(jnp.float32)
        (first_sum, query, key_rows, value), pull_front = jax.vjp(
            front_part,
            tokens,
            weights[0][0],
            weights[1][0],
            weights[2][0],
            weights[3],
            weights[8],
            weights[9],
        )
        heads_query, heads_key, heads_value = (
            lax.all_to_all(
                query.astype(jnp.bfloat16), "seq", split_axis=2, concat_axis=1, tiled=True
            ),
            lax.all_to_all(
                key_rows.astype(jnp.bfloat16), "seq", split_axis=2, concat_axis=1, tiled=True
            ),
            lax.all_to_all(
                value.astype(jnp.bfloat16), "seq", split_axis=2, concat_axis=1, tiled=True
            ),
        )

        def mixing(query_part, key_part, value_part, table_part):
            return attention_heads(query_part, key_part, value_part, table_part, lengths_one)

        mixed_heads, pull_mix = jax.vjp(
            mixing,
            heads_query.astype(jnp.float32),
            heads_key.astype(jnp.float32),
            heads_value.astype(jnp.float32),
            table,
        )
        mixed = lax.all_to_all(
            mixed_heads.astype(jnp.bfloat16), "seq", split_axis=1, concat_axis=2, tiled=True
        ).astype(jnp.float32)
        (second_sum, gated), pull_middle = jax.vjp(
            middle_part, first_sum, mixed, weights[4], weights[5], weights[8], weights[9]
        )
        row_count = gated.shape[1]
        tail = gated[:, row_count - reach :, :].astype(jnp.bfloat16)
        halo = from_behind(tail, "seq", 1).astype(jnp.float32)
        result, pull_back = jax.vjp(
            back_part,
            second_sum,
            gated,
            halo,
            weights[7],
            weights[6],
            weights[0][1],
            weights[1][1],
            weights[2][1],
            weights[8],
            weights[9],
        )
        (
            grad_second,
            grad_gated,
            grad_halo,
            grad_taps,
            grad_conv_out,
            grad_inner_two,
            grad_bias_two,
            grad_outer_two,
            gains_back,
            shifts_back,
        ) = pull_back(cotangent.astype(jnp.float32))
        returned = jax.tree.map(
            lambda part, own: part.astype(own.dtype),
            from_behind(shortened(grad_halo), "seq", -1),
            grad_halo,
        )
        grad_gated = grad_gated.at[:, row_count - reach :, :].add(returned)
        grad_first, grad_mixed, grad_attn_out, grad_conv_in, gains_middle, shifts_middle = (
            pull_middle((grad_second, grad_gated))
        )
        grad_heads = lax.all_to_all(
            grad_mixed.astype(jnp.bfloat16), "seq", split_axis=2, concat_axis=1, tiled=True
        ).astype(jnp.float32)
        grad_query, grad_key, grad_value, grad_table = pull_mix(grad_heads)
        grad_query, grad_key, grad_value = (
            lax.all_to_all(
                grad_query.astype(jnp.bfloat16), "seq", split_axis=1, concat_axis=2, tiled=True
            ),
            lax.all_to_all(
                grad_key.astype(jnp.bfloat16), "seq", split_axis=1, concat_axis=2, tiled=True
            ),
            lax.all_to_all(
                grad_value.astype(jnp.bfloat16), "seq", split_axis=1, concat_axis=2, tiled=True
            ),
        )
        (
            grad_tokens,
            grad_inner_one,
            grad_bias_one,
            grad_outer_one,
            grad_qkv,
            gains_front,
            shifts_front,
        ) = pull_front(
            (
                grad_first,
                grad_query.astype(jnp.float32),
                grad_key.astype(jnp.float32),
                grad_value.astype(jnp.float32),
            )
        )
        local_grads = (
            jnp.stack([grad_inner_one, grad_inner_two]),
            jnp.stack([grad_bias_one, grad_bias_two]),
            jnp.stack([grad_outer_one, grad_outer_two]),
            grad_qkv,
            grad_attn_out,
            grad_conv_in,
            grad_conv_out,
            grad_taps,
            gains_front + gains_middle + gains_back,
            shifts_front + shifts_middle + shifts_back,
            grad_table,
        )
        totals = tuple((first + second for first, second in zip(totals, local_grads)))
        return (totals, (result.astype(jnp.bfloat16), grad_tokens.astype(jnp.bfloat16)))

    starting = tuple((widened(piece, dim, factor) for piece, dim in zip(shards, shard_dims))) + (
        jnp.zeros(distance.shape, jnp.float32),
    )
    totals, (results, grad_rows) = lax.scan(
        micro_step, starting, (inputs[:, None], lengths[:, None], grad_out[:, None])
    )
    outputs = results.reshape(inputs.shape)
    grad_tokens = grad_rows.reshape(inputs.shape)
    (
        share_inner,
        share_bias,
        share_outer,
        share_qkv,
        share_attn,
        share_conv_in,
        share_conv_out,
        share_taps,
        share_gains,
        share_shifts,
    ) = (
        lax.psum_scatter(totals[0], "fsdp", scatter_dimension=1, tiled=True),
        lax.psum_scatter(totals[1], "fsdp", scatter_dimension=1, tiled=True),
        lax.psum_scatter(totals[2], "fsdp", scatter_dimension=1, tiled=True),
        lax.psum_scatter(totals[3], "fsdp", scatter_dimension=1, tiled=True),
        lax.psum_scatter(totals[4], "fsdp", scatter_dimension=0, tiled=True),
        lax.psum_scatter(totals[5], "fsdp", scatter_dimension=0, tiled=True),
        lax.psum_scatter(totals[6], "fsdp", scatter_dimension=0, tiled=True),
        lax.psum_scatter(totals[7], "fsdp", scatter_dimension=1, tiled=True),
        lax.psum_scatter(totals[8], "fsdp", scatter_dimension=1, tiled=True),
        lax.psum_scatter(totals[9], "fsdp", scatter_dimension=1, tiled=True),
    )
    (
        total_inner,
        total_bias,
        total_outer,
        total_qkv,
        total_attn,
        total_conv_in,
        total_conv_out,
        total_taps,
        total_gains,
        total_shifts,
    ) = (
        lax.psum(share_inner.astype(jnp.bfloat16), "seq").astype(jnp.float32),
        lax.psum(share_bias.astype(jnp.bfloat16), "seq").astype(jnp.float32),
        lax.psum(share_outer.astype(jnp.bfloat16), "seq").astype(jnp.float32),
        lax.psum(share_qkv.astype(jnp.bfloat16), "seq").astype(jnp.float32),
        lax.psum(share_attn.astype(jnp.bfloat16), "seq").astype(jnp.float32),
        lax.psum(share_conv_in.astype(jnp.bfloat16), "seq").astype(jnp.float32),
        lax.psum(share_conv_out.astype(jnp.bfloat16), "seq").astype(jnp.float32),
        lax.psum(share_taps.astype(jnp.bfloat16), "seq").astype(jnp.float32),
        lax.psum(share_gains.astype(jnp.bfloat16), "seq").astype(jnp.float32),
        lax.psum(share_shifts.astype(jnp.bfloat16), "seq").astype(jnp.float32),
    )
    total_table = lax.psum(totals[10], ("seq", "fsdp"))
    return (
        outputs,
        grad_tokens,
        total_inner,
        total_bias,
        total_outer,
        total_qkv,
        total_attn,
        total_conv_in,
        total_conv_out,
        total_taps,
        total_gains,
        total_shifts,
        total_table,
    )


def solution(mesh):
    return jax.shard_map(
        on_device,
        mesh=mesh,
        in_specs=(
            P("fsdp", "seq", None),
            P("fsdp"),
            P(None, "fsdp", None),
            P(None, "fsdp"),
            P(None, "fsdp", None),
            P(None, "fsdp", None),
            P("fsdp", None),
            P("fsdp", None),
            P("fsdp", None),
            P(None, "fsdp"),
            P(None, "fsdp"),
            P(None, "fsdp"),
            P(),
            P("fsdp", "seq", None),
        ),
        out_specs=(
            P("fsdp", "seq", None),
            P("fsdp", "seq", None),
            P(None, "fsdp", None),
            P(None, "fsdp"),
            P(None, "fsdp", None),
            P(None, "fsdp", None),
            P("fsdp", None),
            P("fsdp", None),
            P("fsdp", None),
            P(None, "fsdp"),
            P(None, "fsdp"),
            P(None, "fsdp"),
            P(),
        ),
        check_vma=False,
    )
```

profile of v0, /device:TPU:0, one launch (start us, length us, event | category | flops | bytes accessed | tf_op | source)
XLA Modules:
  0.0 3906.0 jit_solution(1424473524945121839)
XLA Ops:
  8.1 2809.6 %while.180 = (s32[]{:T(128)}, f32[2,1024,4096]{2,1,0:T(8,128)}, f32[2,4096]{1,0:T(2,128)}, f32[2,4096,1024]{2,1,0:T(8,128)}, f32[3,1024,1024]{2,1,0:T(8,128)}, /...) while((s32[]{:T(128)}, f32[2,1024,4096]{2,1,0:T(8,128)}, ...), condition=%wide.region_93.94_spmd.clone, body=%wide.region_0.93_spmd.clone.sunk | while | flops 39355039744 | bytes 1916902272 | solution.py:357
  42.5 61.6 %all-gather.7.cloned.1.call-done = bf16[2,1024,4096]{2,1,0:T(8,128)(2,1)} async-done(((bf16[2,128,4096]{2,1,0:T(8,128)(2,1)}), bf16[2,1024,4096]{2,1,0:T(8,128)(2,1)}) %all-gather.7.cloned.1.call-update) | async-done | bytes 16777232 | tf_op jit(solution)/shard_map/while/body/eval_jaxpr/all_gather | solution.py:219
  113.0 83.0 %all-gather.9.cloned.1.call-done = bf16[2,4096,1024]{2,1,0:T(8,128)(2,1)} async-done(((bf16[2,512,1024]{2,1,0:T(8,128)(2,1)}), bf16[2,4096,1024]{2,1,0:T(8,128)(2,1)}) %all-gather.9.cloned.1.call-update) | async-done | bytes 16777232 | tf_op jit(solution)/shard_map/while/body/eval_jaxpr/all_gather | solution.py:221
  203.1 40.5 %all-gather.11.cloned.1.call-done = bf16[3,1024,1024]{2,1,0:T(8,128)(2,1)} async-done(((bf16[3,128,1024]{2,1,0:T(8,128)(2,1)}), bf16[3,1024,1024]{2,1,0:T(8,128)(2,1)}) %all-gather.11.cloned.1.call-update) | async-done | bytes 6291472 | tf_op jit(solution)/shard_map/while/body/eval_jaxpr/all_gather | solution.py:222
  316.6 239.2 %while.182 = (s32[]{:T(128)}, bf16[2,512,256]{2,1,0:T(8,128)(2,1)S(1)}, s32[2]{0:T(128)S(1)}, bf16[1024,4,64]{0,2,1:T(8,128)(2,1)S(1)}, bf16[1024,4,64]{0,2,1:T(...) while((s32[]{:T(128)}, ...), condition=%wide.region_10.10_spmd.clone, body=%wide.region_7.9_spmd.clone.sunk | while | flops 574882816 | bytes 209848512 | solution.py:139
  725.2 498.6 %while.183 = (s32[]{:T(128)}, f32[1024,4,64]{0,2,1:T(8,128)}, f32[1024,4,64]{0,2,1:T(8,128)}, f32[73,64]{0,1:T(8,128)}, f32[1024,4,64]{0,2,1:T(8,128)S(1)}, /*in...) while((s32[]{:T(128)}, f32[1024,4,64]{0,2,1:T(8,128)}, ...), condition=%wide.region_35.35_spmd.clone, body=%wide.region_27.34_spmd.clone.sunk | while | flops 1491006080 | bytes 526899392 | solution.py:139
  1432.0 60.9 %all-gather.7.cloned.1.call-done = bf16[2,1024,4096]{2,1,0:T(8,128)(2,1)} async-done(((bf16[2,128,4096]{2,1,0:T(8,128)(2,1)}), bf16[2,1024,4096]{2,1,0:T(8,128)(2,1)}) %all-gather.7.cloned.1.call-update) | async-done | bytes 16777232 | tf_op jit(solution)/shard_map/while/body/eval_jaxpr/all_gather | solution.py:219
  1501.9 83.0 %all-gather.9.cloned.1.call-done = bf16[2,4096,1024]{2,1,0:T(8,128)(2,1)} async-done(((bf16[2,512,1024]{2,1,0:T(8,128)(2,1)}), bf16[2,4096,1024]{2,1,0:T(8,128)(2,1)}) %all-gather.9.cloned.1.call-update) | async-done | bytes 16777232 | tf_op jit(solution)/shard_map/while/body/eval_jaxpr/all_gather | solution.py:221
  1592.0 40.5 %all-gather.11.cloned.1.call-done = bf16[3,1024,1024]{2,1,0:T(8,128)(2,1)} async-done(((bf16[3,128,1024]{2,1,0:T(8,128)(2,1)}), bf16[3,1024,1024]{2,1,0:T(8,128)(2,1)}) %all-gather.11.cloned.1.call-update) | async-done | bytes 6291472 | tf_op jit(solution)/shard_map/while/body/eval_jaxpr/all_gather | solution.py:222
  1705.2 239.2 %while.182 = (s32[]{:T(128)}, bf16[2,512,256]{2,1,0:T(8,128)(2,1)S(1)}, s32[2]{0:T(128)S(1)}, bf16[1024,4,64]{0,2,1:T(8,128)(2,1)S(1)}, bf16[1024,4,64]{0,2,1:T(...) while((s32[]{:T(128)}, ...), condition=%wide.region_10.10_spmd.clone, body=%wide.region_7.9_spmd.clone.sunk | while | flops 574882816 | bytes 209848512 | solution.py:139
  2115.8 498.7 %while.183 = (s32[]{:T(128)}, f32[1024,4,64]{0,2,1:T(8,128)}, f32[1024,4,64]{0,2,1:T(8,128)}, f32[73,64]{0,1:T(8,128)}, f32[1024,4,64]{0,2,1:T(8,128)S(1)}, /*in...) while((s32[]{:T(128)}, f32[1024,4,64]{0,2,1:T(8,128)}, ...), condition=%wide.region_35.35_spmd.clone, body=%wide.region_27.34_spmd.clone.sunk | while | flops 1491006080 | bytes 526899392 | solution.py:139
  2731.0 33.7 maximum_add_fusion.8
  2764.8 33.4 maximum_add_fusion.6
  2825.8 47.8 %reduce-scatter.19.cloned.1.call-done = f32[128,1024]{1,0:T(8,128)} async-done(((f32[1024,1024]{1,0:T(8,128)}), f32[128,1024]{1,0:T(8,128)}) %reduce-scatter.19.cloned.1.call-update) | async-done | bytes 524304 | tf_op jit(solution)/shard_map/reduce_scatter | solution.py:378
  2875.4 53.6 %reduce-scatter.23.cloned.1.call-done = f32[128,1024]{1,0:T(8,128)} async-done(((f32[1024,1024]{1,0:T(8,128)}), f32[128,1024]{1,0:T(8,128)}) %reduce-scatter.23.cloned.1.call-update) | async-done | bytes 524304 | tf_op jit(solution)/shard_map/reduce_scatter | solution.py:380
  2930.7 72.7 %reduce-scatter.21.cloned.1.call-done = f32[128,2048]{1,0:T(8,128)} async-done(((f32[1024,2048]{1,0:T(8,128)}), f32[128,2048]{1,0:T(8,128)}) %reduce-scatter.21.cloned.1.call-update) | async-done | bytes 1048592 | tf_op jit(solution)/shard_map/reduce_scatter | solution.py:379
  3005.6 94.0 %reduce-scatter.17.cloned.1.call-done = f32[3,128,1024]{2,1,0:T(8,128)} async-done(((f32[3,1024,1024]{2,1,0:T(8,128)}), f32[3,128,1024]{2,1,0:T(8,128)}) %reduce-scatter.17.cloned.1.call-update) | async-done | bytes 1572880 | tf_op jit(solution)/shard_map/reduce_scatter | solution.py:377
  3102.0 206.7 %reduce-scatter.13.cloned.1.call-done = f32[2,128,4096]{2,1,0:T(8,128)} async-done(((f32[2,1024,4096]{2,1,0:T(8,128)}), f32[2,128,4096]{2,1,0:T(8,128)}) %reduce-scatter.13.cloned.1.call-update) | async-done | bytes 4194320 | tf_op jit(solution)/shard_map/reduce_scatter | solution.py:374
  3312.5 204.9 %reduce-scatter.15.cloned.1.call-done = f32[2,512,1024]{2,1,0:T(8,128)} async-done(((f32[2,4096,1024]{2,1,0:T(8,128)}), f32[2,512,1024]{2,1,0:T(8,128)}) %reduce-scatter.15.cloned.1.call-update) | async-done | bytes 4194320 | tf_op jit(solution)/shard_map/reduce_scatter | solution.py:376
  3522.0 40.0 %psum.87 = f32[73,64]{0,1:T(8,128)} all-reduce(f32[73,64]{0,1:T(8,128)S(1)} %copy-done.78), channel_id=1, replica_groups=mesh['seq'=4,'fsdp'=8] {'seq','fsdp'}, use_global_device_ids=true, to_apply=%region_114.115 | all-reduce | flops 4672 | bytes 37376 | tf_op jit(solution)/shard_map/psum | solution.py:408
  3562.7 33.5 reduce-scatter.31.cloned.1.call-done
  3597.2 33.6 reduce-scatter.29.cloned.1.call-done
  3631.5 35.8 reduce-scatter.25.cloned.1.call-done
  3689.5 197.9 %all-reduce.97.cloned.1.call-done = (bf16[2,128,4096]{2,1,0:T(8,128)(2,1)}, bf16[2,512,1024]{2,1,0:T(8,128)(2,1)}, bf16[3,128,1024]{2,1,0:T(8,128)(2,1)}, bf16[1...) async-done(((bf16[2,128,4096]{2,1,0:T(8,128)(2,1)}, bf16[2,512,1024]{2,1,0:T(8,128)(2,1)}, bf16[3,128,1024]{2,1,0:T(8,128)(2,1)}, ...) | async-done | bytes 6029328 | tf_op jit(solution)/shard_map/psum | solution.py:397
  (1560 shorter events, 2412.8 us)
Async XLA Ops:
  8.4 95.6 %all-gather.7.cloned.1.call-start = ((), (), s32[]{:S(2)}) async-start(), calls=%async_computation.29 | async-start | bytes 18874368 | tf_op jit(solution)/shard_map/while/body/eval_jaxpr/all_gather | solution.py:219
  9.2 186.9 %all-gather.9.cloned.1.call-start = ((), (), s32[]{:S(2)}) async-start(), calls=%async_computation.30 | async-start | bytes 18874368 | tf_op jit(solution)/shard_map/while/body/eval_jaxpr/all_gather | solution.py:221
  9.9 233.7 %all-gather.11.cloned.1.call-start = ((), (), s32[]{:S(2)}) async-start(), calls=%async_computation.31 | async-start | bytes 7077888 | tf_op jit(solution)/shard_map/while/body/eval_jaxpr/all_gather | solution.py:222
  10.7 575.2 %all-gather.13.cloned.1.call-start = ((), (), s32[]{:S(2)}) async-start(), calls=%async_computation.32 | async-start | bytes 2359296 | tf_op jit(solution)/shard_map/while/body/eval_jaxpr/all_gather | solution.py:223
  275.4 313.6 %all-gather.17.cloned.1.call-start = ((), (), s32[]{:S(2)}) async-start(), calls=%async_computation.34 | async-start | bytes 4718592 | tf_op jit(solution)/shard_map/while/body/eval_jaxpr/all_gather | solution.py:224
  289.5 25.6 all-to-all-start
  569.0 38.4 all-gather.15.cloned.1.call-start
  1399.7 93.3 %all-gather.7.cloned.1.call-start = ((), (), s32[]{:S(2)}) async-start(), calls=%async_computation.29 | async-start | bytes 18874368 | tf_op jit(solution)/shard_map/while/body/eval_jaxpr/all_gather | solution.py:219
  1400.4 184.5 %all-gather.9.cloned.1.call-start = ((), (), s32[]{:S(2)}) async-start(), calls=%async_computation.30 | async-start | bytes 18874368 | tf_op jit(solution)/shard_map/while/body/eval_jaxpr/all_gather | solution.py:221
  1401.2 231.4 %all-gather.11.cloned.1.call-start = ((), (), s32[]{:S(2)}) async-start(), calls=%async_computation.31 | async-start | bytes 7077888 | tf_op jit(solution)/shard_map/while/body/eval_jaxpr/all_gather | solution.py:222
  1401.9 572.5 %all-gather.13.cloned.1.call-start = ((), (), s32[]{:S(2)}) async-start(), calls=%async_computation.32 | async-start | bytes 2359296 | tf_op jit(solution)/shard_map/while/body/eval_jaxpr/all_gather | solution.py:223
  1664.2 313.4 %all-gather.17.cloned.1.call-start = ((), (), s32[]{:S(2)}) async-start(), calls=%async_computation.34 | async-start | bytes 4718592 | tf_op jit(solution)/shard_map/while/body/eval_jaxpr/all_gather | solution.py:224
  1957.7 38.3 all-gather.15.cloned.1.call-start
  2817.7 55.9 %reduce-scatter.19.cloned.1.call-start = ((), (), s32[]{:S(2)}) async-start(), calls=%async_computation.21 | async-start | bytes 4718592 | tf_op jit(solution)/shard_map/reduce_scatter | solution.py:378
  2818.3 110.7 %reduce-scatter.23.cloned.1.call-start = ((), (), s32[]{:S(2)}) async-start(), calls=%async_computation.23 | async-start | bytes 4718592 | tf_op jit(solution)/shard_map/reduce_scatter | solution.py:380
  2818.9 184.6 %reduce-scatter.21.cloned.1.call-start = ((), (), s32[]{:S(2)}) async-start(), calls=%async_computation.22 | async-start | bytes 9437184 | tf_op jit(solution)/shard_map/reduce_scatter | solution.py:379
  2819.5 280.1 %reduce-scatter.17.cloned.1.call-start = ((), (), s32[]{:S(2)}) async-start(), calls=%async_computation.20 | async-start | bytes 14155776 | tf_op jit(solution)/shard_map/reduce_scatter | solution.py:377
  2820.2 488.5 %reduce-scatter.13.cloned.1.call-start = ((), (), s32[]{:S(2)}) async-start(), calls=%async_computation.18 | async-start | bytes 37748736 | tf_op jit(solution)/shard_map/reduce_scatter | solution.py:374
  2821.0 696.5 %reduce-scatter.15.cloned.1.call-start = ((), (), s32[]{:S(2)}) async-start(), calls=%async_computation.19 | async-start | bytes 37748736 | tf_op jit(solution)/shard_map/reduce_scatter | solution.py:376
  2821.7 740.3 %reduce-scatter.27.cloned.1.call-start = ((), (), s32[]{:S(2)}) async-start(), calls=%async_computation.25 | async-start | bytes 36864 | tf_op jit(solution)/shard_map/reduce_scatter | solution.py:382
  2822.3 773.8 %reduce-scatter.31.cloned.1.call-start = ((), (), s32[]{:S(2)}) async-start(), calls=%async_computation.27 | async-start | bytes 2359296
  2824.4 806.4 %reduce-scatter.29.cloned.1.call-start = ((), (), s32[]{:S(2)}) async-start(), calls=%async_computation.26 | async-start | bytes 73728 | tf_op jit(solution)/shard_map/reduce_scatter | solution.py:383
  2825.0 842.3 %reduce-scatter.25.cloned.1.call-start = ((), (), s32[]{:S(2)}) async-start(), calls=%async_computation.24 | async-start | bytes 147456 | tf_op jit(solution)/shard_map/reduce_scatter | solution.py:381
  2825.7 1061.6 %all-reduce.97.cloned.1.call-start = ((), (), s32[]{:S(2)}) async-start(), calls=%async_computation.28 | async-start | bytes 12058624 | tf_op jit(solution)/shard_map/psum | solution.py:397
  (402 other events, 4546.4 us)
Sparse Core Ops, SparseCore 0:
  11.3 92.6 all-gather.6
  106.1 89.8 all-gather.8
  198.1 45.5 all-gather.10
  245.5 27.8 all-gather.12
  278.0 37.1 all-gather.16
  571.6 28.3 all-gather.14
  1402.6 90.3 all-gather.6
  1495.0 89.8 all-gather.8
  1587.0 45.5 all-gather.10
  1634.4 27.8 all-gather.12
  1667.1 37.1 all-gather.16
  1960.3 28.3 all-gather.14
Sparse Core Ops, SparseCore 1:
  2822.1 51.4 reduce-scatter.18
  2877.8 51.1 reduce-scatter.22
  2932.3 71.1 reduce-scatter.20
  3007.4 92.1 reduce-scatter.16
  3103.6 205.1 reduce-scatter.12
  3312.3 205.1 reduce-scatter.14
  3520.6 31.2 reduce-scatter.26
  3555.0 41.0 reduce-scatter.30
  3599.3 31.4 reduce-scatter.28
  3633.8 33.4 reduce-scatter.24
  3671.3 215.9 all-reduce.96
where the time goes:
time: 3920 us; the launch traced here: 3910 us
  waiting for transfers between devices  1400 us (36%)
  local copies, waits for them, and re-layouts  1350 us (34%)
  other arithmetic  468 us (12%)
  matrix products  405 us (10%)
  blocking collectives  129 us (3%)
  starting transfers between devices  78.9 us (2%)
  loops' own time  52.2 us (1%)
    while x842, local copies, waits for them, and re-layouts  450 us
    dot_general x60, matrix products, product(): return jnp.einsum('...d,df->...f', left, right, precision=PRECISION)  270 us
    reshape x16, local copies, waits for them, and re-layouts, place_band(): flat = rows.reshape(heads_here, block_rows * row_width)  258 us
    reduce_scatter x1, waiting for transfers between devices, on_device(): lax.psum_scatter(totals[0], 'fsdp', scatter_dimension=1, tiled=True)  207 us
    reduce_scatter x1, waiting for transfers between devices, on_device(): lax.psum_scatter(totals[2], 'fsdp', scatter_dimension=1, tiled=True)  205 us
    psum x1, waiting for transfers between devices, on_device(): lax.psum(share_inner.astype(jnp.bfloat16), 'seq').astype(jnp.float32)  198 us
    reshape x12, local copies, waits for them, and re-layouts, place_band(): skewed.reshape(heads_here, block_rows, row_width - 1)[:, :, :token_count]  168 us
    all_gather x2, waiting for transfers between devices, micro_step(): lax.all_gather(ffn_out, 'fsdp', axis=1, tiled=True)  166 us
  transfers between devices with their start and end apart: 43, of which 28 were waited for; matrix products, arithmetic and copies ran while one was open for 20% of the time, Pallas kernels for 0%

commit v1 on v0

v1 whole, which is shorter than its diff:
```python
import functools

import jax
import jax.numpy as jnp
from jax import lax
from jax.experimental import pallas as pl
from jax.experimental.pallas import tpu as pltpu
from jax.sharding import PartitionSpec as P

HEAD_DIM=64; LEFT=64; RIGHT=8
F32=jnp.float32; BF=jnp.bfloat16
RB=256
PADL=128
WIN=512

def dot(a,b,ca,cb):
    return lax.dot_general(a,b,(((ca,),(cb,)),((),())),preferred_element_type=F32)

def lanes(shape):
    return lax.broadcasted_iota(jnp.int32,shape,1)

def band_offset():
    row=lax.broadcasted_iota(jnp.int32,(RB,WIN),0)
    col=lax.broadcasted_iota(jnp.int32,(RB,WIN),1)
    return col-row-LEFT

def fwd_kernel(len_ref,q_ref,k_ref,v_ref,wide_ref,ends_ref,p_ref,o_ref,s_ref,kx_ref):
    n=k_ref.shape[0]
    step=pl.program_id(1)
    i0=step*RB
    q2=q_ref[...]
    lane=lanes((RB,128))
    col=lanes((RB,128))
    t=lax.broadcasted_iota(jnp.int32,(n,128),0)
    c=lanes((n,128))
    left=(t<i0-128).astype(F32); right=(t>=i0+WIN-128).astype(F32)
    masked=jnp.where(t>=len_ref[0],-1e30,0.0)
    ext=jnp.where(c<2,left,jnp.where(c<4,right,jnp.where(c==4,masked,0.0)))
    kx_ref[...]=ext.astype(BF)
    outs=[]
    for h in range(2):
        mine=(lane<64) if h==0 else (lane>=64)
        qh=jnp.where(mine,q2,jnp.zeros_like(q2))
        ends=dot(qh,ends_ref[...],1,0)
        hi=ends.astype(BF).astype(F32)
        qx=jnp.where((col==0)|(col==2),hi,jnp.where((col==1)|(col==3),ends-hi,jnp.where(col==4,1.0,0.0))).astype(BF)
        s=dot(qh,k_ref[...],1,1)+dot(qx,kx_ref[...],1,1)
        s_ref[:,PADL:PADL+n]=s
        wide=dot(qh,wide_ref[...],1,0)
        band=pltpu.roll(wide,LEFT,1,stride=1,stride_axis=0)
        j=band_offset()
        band=jnp.where(j>=LEFT+RIGHT,wide[:,LEFT+RIGHT:LEFT+RIGHT+1],band)
        w=pl.ds(pl.multiple_of(i0,RB),WIN)
        s_ref[:,w]=s_ref[:,w]+band
        s=s_ref[:,PADL:PADL+n]
        m=jnp.max(s,axis=1,keepdims=True)
        e=jnp.exp(s-m)
        z=jnp.sum(e,axis=1,keepdims=True)
        p=(e*(1.0/z)).astype(BF)
        p_ref[h]=p
        outs.append(dot(p,v_ref[...],1,0))
    o_ref[...]=jnp.where(lane<64,outs[0],outs[1]).astype(BF)

def bwd_kernel(q_ref,k_ref,v_ref,do_ref,p_ref,wide_ref,dq_ref,dkt_ref,dvt_ref,de_ref,ds_ref,kx_ref,dka,dva,dea):
    n=k_ref.shape[0]
    step=pl.program_id(1)
    pair=pl.program_id(0)
    i0=step*RB
    q2=q_ref[...]; do2=do_ref[...]
    lane=lanes((RB,128))
    row=lax.broadcasted_iota(jnp.int32,(RB,128),0)
    t=lax.broadcasted_iota(jnp.int32,(n,128),0)
    c=lanes((n,128))
    left=(t<i0-128).astype(F32)
    kx_ref[...]=jnp.where(c==0,left,jnp.where(c==1,1.0,0.0)).astype(BF)
    @pl.when(step==0)
    def _():
        dka[...]=jnp.zeros_like(dka); dva[...]=jnp.zeros_like(dva)
    @pl.when((step==0)&(pair==0))
    def _():
        dea[...]=jnp.zeros_like(dea)
    ds_ref[:,0:PADL]=jnp.zeros((RB,PADL),F32)
    ds_ref[:,PADL+n:]=jnp.zeros((RB,ds_ref.shape[1]-PADL-n),F32)
    dqs=[]
    for h in range(2):
        mine=(lane<64) if h==0 else (lane>=64)
        doh=jnp.where(mine,do2,jnp.zeros_like(do2))
        qh=jnp.where(mine,q2,jnp.zeros_like(q2))
        p=p_ref[h]
        dp=dot(doh,v_ref[...],1,1)
        pf=p.astype(F32)
        d=jnp.sum(pf*dp,axis=1,keepdims=True)
        dsf=pf*(dp-d)
        ds=dsf.astype(BF)
        ds_ref[:,PADL:PADL+n]=ds.astype(F32)
        dva[...]+=dot(doh,p,0,0)
        dka[...]+=dot(qh,ds,0,0)
        dq=dot(ds,k_ref[...],1,0)
        sums=dot(ds,kx_ref[...],1,0)
        win=ds_ref[:,pl.ds(pl.multiple_of(i0,RB),WIN)]
        j=band_offset()
        inleft=jnp.sum(jnp.where(j<=0,win,0.0),axis=1,keepdims=True)
        drel=jnp.concatenate([win[8*g:8*g+8,LEFT+8*g:LEFT+8*g+128] for g in range(RB//8)],axis=0)
        for bit in (1,2,4):
            drel=jnp.where((row&bit)!=0,pltpu.roll(drel,128-bit,1),drel)
        drel=jnp.where((lane>0)&(lane<LEFT+RIGHT),drel,0.0)
        bandsum=jnp.sum(drel,axis=1,keepdims=True)
        l=sums[:,0:1]+inleft
        r=sums[:,1:2]-l-bandsum
        drel=jnp.where(lane==0,l,jnp.where(lane==LEFT+RIGHT,r,drel)).astype(BF)
        dq=dq+dot(drel,wide_ref[...],1,1)
        dqs.append(dq)
        dea[...]+=dot(drel,qh,0,0)
    dq_ref[...]=(jnp.where(lane<64,dqs[0],dqs[1])*HEAD_DIM**-0.5).astype(BF)
    @pl.when(step==pl.num_programs(1)-1)
    def _():
        dkt_ref[...]=jnp.transpose(dka[...]).astype(BF)
        dvt_ref[...]=jnp.transpose(dva[...]).astype(BF)
    @pl.when((step==pl.num_programs(1)-1)&(pair==pl.num_programs(0)-1))
    def _():
        de_ref[...]=dea[...]

def tables(distance):
    e=distance.T
    wide=jnp.concatenate([e,jnp.broadcast_to(e[:,72:73],(64,120)),jnp.broadcast_to(e[:,0:1],(64,WIN-193))],axis=1)
    wide=jnp.concatenate([wide,wide],axis=0)
    ends=jnp.concatenate([e[:,0:1],e[:,0:1],e[:,72:73],e[:,72:73],jnp.zeros((64,124),e.dtype)],axis=1)
    ends=jnp.concatenate([ends,ends],axis=0)
    return wide,ends

def attend(q,k,v,length,wide,ends):
    n,w=q.shape; pairs=w//128
    return pl.pallas_call(fwd_kernel,
        grid=(pairs,n//RB),
        in_specs=[pl.BlockSpec(memory_space=pltpu.SMEM),
            pl.BlockSpec((RB,128),lambda a,b:(b,a)),pl.BlockSpec((n,128),lambda a,b:(0,a)),pl.BlockSpec((n,128),lambda a,b:(0,a)),
            pl.BlockSpec((128,WIN),lambda a,b:(0,0)),pl.BlockSpec((128,128),lambda a,b:(0,0))],
        out_specs=[pl.BlockSpec((2,RB,n),lambda a,b:(a,b,0)),pl.BlockSpec((RB,128),lambda a,b:(b,a))],
        out_shape=[jax.ShapeDtypeStruct((2*pairs,n,n),BF),jax.ShapeDtypeStruct((n,w),BF)],
        scratch_shapes=[pltpu.VMEM((RB,PADL+n+256),F32),pltpu.VMEM((n,128),BF)],
        compiler_params=pltpu.CompilerParams(vmem_limit_bytes=32<<20),
        name="attend_fwd",
    )(length,q,k,v,wide,ends)

def attend_back(q,k,v,do,p,wide):
    n,w=q.shape; pairs=w//128
    rows=pl.BlockSpec((RB,128),lambda a,b:(b,a)); whole=pl.BlockSpec((n,128),lambda a,b:(0,a))
    return pl.pallas_call(bwd_kernel,
        grid=(pairs,n//RB),
        in_specs=[rows,whole,whole,rows,pl.BlockSpec((2,RB,n),lambda a,b:(a,b,0)),pl.BlockSpec((128,128),lambda a,b:(0,0))],
        out_specs=[rows,whole,whole,pl.BlockSpec((128,128),lambda a,b:(0,0))],
        out_shape=[jax.ShapeDtypeStruct((n,w),BF)]*3+[jax.ShapeDtypeStruct((128,128),F32)],
        scratch_shapes=[pltpu.VMEM((RB,PADL+n+256),F32),pltpu.VMEM((n,128),BF),pltpu.VMEM((128,n),F32),pltpu.VMEM((128,n),F32),pltpu.VMEM((128,128),F32)],
        compiler_params=pltpu.CompilerParams(vmem_limit_bytes=32<<20),
        name="attend_bwd",
    )(q,k,v,do,p,wide[:,0:128])

EPSILON = 1e-05
HALF = 0.5


def mm(a, b):
    return dot(a, b, 1, 0)


def mm_bt(a, b):
    return dot(a, b, 1, 1)


def mm_at(a, b):
    return dot(a, b, 0, 0)


def norm_stats(values):
    mean = jnp.mean(values, axis=-1, keepdims=True)
    centred = values - mean
    spread = jnp.mean(centred * centred, axis=-1, keepdims=True)
    return mean, lax.rsqrt(spread + EPSILON)


def normalized(values, stats):
    return (values - stats[0]) * stats[1]


def norm_back(dy, values, stats, gain):
    unit = normalized(values, stats)
    a = dy * gain
    dv = (a - jnp.mean(a, axis=-1, keepdims=True) - unit * jnp.mean(a * unit, axis=-1, keepdims=True)) * stats[1]
    return dv, jnp.sum(dy * unit, axis=0), jnp.sum(dy, axis=0)


def silu_slope(v):
    s = jax.nn.sigmoid(v)
    return s * (1.0 + v * (1.0 - s))


def xor_route(axis, mask):
    return [(i, i ^ mask) for i in range(lax.axis_size(axis))]


def swapped(block, axis, mask):
    return lax.ppermute(block, axis, xor_route(axis, mask))


def after(value, *marks):
    return lax.optimization_barrier((value,) + marks)[0]


class Cube:
    def __init__(self):
        self.me = lax.axis_index("fsdp")

    def gather(self, shard):
        rows = shard.shape[0]
        cut = rows // 2
        across_x = swapped(shard, "fsdp", 2)
        across_y = swapped(shard, "fsdp", 4)
        far_top = swapped(across_x[:cut], "fsdp", 4)
        far_low = swapped(across_y[cut:], "fsdp", 2)
        mine = [shard, across_x, across_y, far_top, far_low]
        other = [swapped(piece, "fsdp", 1) for piece in mine]
        return jnp.concatenate(
            [mine[0], other[0], mine[1], other[1], mine[2], other[2], mine[3], mine[4], other[3], other[4]], axis=0
        )

    def arrange(self, value):
        rows, cols = value.shape
        blocks = value.reshape(rows, 8, cols // 8)
        for bit in (1, 2, 4):
            order = [i ^ bit for i in range(8)]
            turned = jnp.stack([blocks[:, i] for i in order], axis=1)
            blocks = jnp.where((self.me & bit) != 0, turned, blocks)
        return blocks.reshape(rows, cols)

    def product_back(self, left, right):
        rows, cols = left.shape
        blocks = left.reshape(rows, 4, 2, cols // 8)
        odd = mm_at(blocks[:, :, 1].reshape(rows, cols // 2), right).astype(BF)
        even = mm_at(blocks[:, :, 0].reshape(rows, cols // 2), right)
        return odd, even

    def scatter(self, odd, even):
        size, cols = odd.shape
        rows, cut = size // 4, cols // 2
        here = (even + swapped(odd, "fsdp", 1).astype(F32)).reshape(4, rows, cols)
        one, two = here[:, :, :cut], here[:, :, cut:]
        got = swapped(one[1::2].astype(BF), "fsdp", 2)
        one = one[0::2] + got.astype(F32)
        got = swapped(two[2:].astype(BF), "fsdp", 4)
        two = two[:2] + got.astype(F32)
        one = one[0] + swapped(one[1].astype(BF), "fsdp", 4).astype(F32)
        two = two[0] + swapped(two[1].astype(BF), "fsdp", 2).astype(F32)
        return self.over_seq(jnp.concatenate([one, two], axis=1))

    def over_seq(self, part):
        rows = part.shape[0]
        place = lax.axis_index("seq")
        for mask in (1, 2):
            high = (place & mask) != 0
            half = part.shape[0] // 2
            first, second = part[:half], part[half:]
            sent = jnp.where(high, first, second).astype(BF)
            part = jnp.where(high, second, first) + swapped(sent, "seq", mask).astype(F32)
        part = part.astype(BF)
        for mask in (2, 1):
            high = (place & mask) != 0
            got = swapped(part, "seq", mask)
            part = jnp.where(high, jnp.concatenate([got, part], axis=0), jnp.concatenate([part, got], axis=0))
        return part.astype(F32)


class Plain:
    def gather(self, shard):
        return lax.all_gather(shard, "fsdp", axis=0, tiled=True)

    def arrange(self, value):
        return value

    def product_back(self, left, right):
        return None, mm_at(left, right)

    def scatter(self, odd, even):
        share = lax.psum_scatter(even.astype(BF), "fsdp", scatter_dimension=0, tiled=True)
        return lax.psum(share, "seq").astype(F32)


def to_pairs(array, place):
    one, two = array[0], array[1]
    got = lax.ppermute(jnp.where(place % 2 == 0, two, one), "seq", [(0, 2), (1, 0), (2, 3), (3, 1)])
    more = lax.ppermute(jnp.where(place == 1, two, one), "seq", [(1, 2), (2, 1)])
    first = jnp.where(place == 0, one, jnp.where(place == 1, more, got))
    second = jnp.where(place < 2, got, jnp.where(place == 2, more, two))
    return jnp.concatenate([first, second], axis=0)


def from_pairs(array, place):
    half = array.shape[0] // 2
    first, second = array[:half], array[half:]
    got = lax.ppermute(jnp.where(place < 2, second, first), "seq", [(2, 0), (0, 1), (3, 2), (1, 3)])
    more = lax.ppermute(jnp.where(place == 1, first, second), "seq", [(1, 2), (2, 1)])
    one = jnp.where(place == 0, first, jnp.where(place == 2, more, got))
    two = jnp.where(place == 3, second, jnp.where(place == 1, more, got))
    return jnp.stack([one, two])


def to_heads(array, odd):
    half = array.shape[1] // 2
    low, high = array[:, :half], array[:, half:]
    mine = jnp.where(odd, high, low)
    got = swapped(jnp.where(odd, low, high), "seq", 1)
    return jnp.concatenate([jnp.where(odd, got, mine), jnp.where(odd, mine, got)], axis=0)


def to_tokens(array, odd):
    half = array.shape[0] // 2
    low, high = array[:half], array[half:]
    mine = jnp.where(odd, high, low)
    got = swapped(jnp.where(odd, low, high), "seq", 1)
    return jnp.concatenate([jnp.where(odd, got, mine), jnp.where(odd, mine, got)], axis=1)


def on_device(
    inputs,
    lengths,
    ffn_in,
    ffn_in_bias,
    ffn_out,
    qkv,
    attn_out,
    conv_in,
    conv_out,
    depthwise,
    gains,
    shifts,
    distance,
    grad_out,
):
    shards = lax.axis_size("fsdp")
    me = lax.axis_index("fsdp")
    place = lax.axis_index("seq")
    odd = place % 2 == 1
    cube = Cube() if shards == 8 else Plain()
    reach = depthwise.shape[0] - 1
    inner_width = ffn_in.shape[2]
    width = inputs.shape[2]

    bias_rows = ffn_in_bias.shape[0] * inner_width // width
    small = jnp.concatenate(
        [gains, shifts, depthwise, ffn_in_bias.reshape(-1, width // shards)], axis=0
    )
    n_gain, n_shift, n_tap = gains.shape[0], shifts.shape[0], depthwise.shape[0]
    small = lax.all_gather(small, "fsdp", axis=0).astype(F32)
    rows = jnp.transpose(small, (1, 0, 2))
    gain = rows[:n_gain].reshape(n_gain, width)
    shift = rows[n_gain : n_gain + n_shift].reshape(n_shift, width)
    taps = rows[n_gain + n_shift : n_gain + n_shift + n_tap].reshape(n_tap, width)
    bias = small[:, n_gain + n_shift + n_tap :].reshape(shards, 2, -1).transpose(1, 0, 2).reshape(2, inner_width)

    w_in_a = cube.gather(ffn_in[0])
    w_out_a = cube.gather(ffn_out[0])
    w_qkv = cube.gather(jnp.concatenate([qkv[0], qkv[1], qkv[2]], axis=1))
    w_mid = cube.gather(jnp.concatenate([attn_out, conv_in, conv_out], axis=1))
    w_in_b = cube.gather(ffn_in[1])
    w_out_b = cube.gather(ffn_out[1])
    w_attn, w_conv_in, w_conv_out = w_mid[:, :width], w_mid[:, width : 3 * width], w_mid[:, 3 * width :]

    tokens = to_pairs(inputs, place).astype(F32)
    cotangent = to_pairs(grad_out, place)
    length = jnp.where(place < 2, lengths[0], lengths[1]).reshape(1)
    wide, ends = tables(distance)

    def prenorm(values, g):
        stats = norm_stats(values)
        unit = cube.arrange((normalized(values, stats) * gain[g] + shift[g]).astype(BF))
        return stats, unit

    def ffn(values, g, w_in, b_in, w_out, b_out):
        stats, unit = prenorm(values, g)
        inner = mm(unit, w_in) + b_in
        active = cube.arrange((inner * jax.nn.sigmoid(inner)).astype(BF))
        result = values + HALF * (mm(active, w_out) + b_out)
        return result, (stats, unit, inner.astype(BF), active)

    def ffn_back(dy, values, g, w_in, w_out, kept):
        stats, unit, inner, active = kept
        dout = (HALF * dy).astype(BF)
        d_out_w = cube.product_back(active, dout)
        dactive = cube.arrange(mm_bt(dout, w_out))
        dinner = (dactive * silu_slope(inner.astype(F32))).astype(BF)
        d_in_w = cube.product_back(unit, dinner)
        dunit = cube.arrange(mm_bt(dinner, w_in))
        dv, dgain, dshift = norm_back(dunit, values, stats, gain[g])
        return dy + dv, d_in_w, d_out_w, colsum(dinner), colsum(dout), dgain, dshift

    def colsum(v):
        return jnp.sum(v.astype(F32), axis=0)

    first, kept_a = ffn(tokens, 0, w_in_a, bias[0], w_out_a, shift[6])
    stats_1, unit_1 = prenorm(first, 1)
    query = ((mm(unit_1, w_qkv[:, :width]) + shift[8]).astype(BF) * jnp.asarray(HEAD_DIM**-0.5, BF)).astype(BF)
    key_rows = mm(unit_1, w_qkv[:, width : 2 * width]).astype(BF)
    value = (mm(unit_1, w_qkv[:, 2 * width :]) + shift[9]).astype(BF)
    query, key_rows, value = to_heads(query, odd), to_heads(key_rows, odd), to_heads(value, odd)
    probs, mixed = attend(query, key_rows, value, length, wide, ends)
    mixed = cube.arrange(to_tokens(mixed, odd))
    second = first + mm(mixed, w_attn) + shift[10]
    stats_2, unit_2 = prenorm(second, 2)
    glu = mm(unit_2, w_conv_in) + jnp.concatenate([shift[11], shift[12]])
    glu_value, glu_gate = glu[:, :width], jax.nn.sigmoid(glu[:, width:])
    gated = (glu_value * glu_gate).astype(BF)
    glu_value, glu_gate = glu_value.astype(BF), glu_gate.astype(BF)
    pairs = [(0, 1), (2, 3)]
    count = gated.shape[0]
    halo = lax.ppermute(gated[count - reach :], "seq", pairs)
    padded = jnp.concatenate([halo, gated], axis=0).astype(F32)
    conv = shift[13] + taps[0] * padded[0:count]
    for tap in range(1, n_tap):
        conv = conv + taps[tap] * padded[tap : tap + count]
    stats_3 = norm_stats(conv)
    normed = normalized(conv, stats_3) * gain[3] + shift[3]
    active_c = cube.arrange((normed * jax.nn.sigmoid(normed)).astype(BF))
    third = second + mm(active_c, w_conv_out) + shift[14]
    fourth, kept_b = ffn(third, 4, w_in_b, bias[1], w_out_b, shift[7])
    stats_5 = norm_stats(fourth)
    outputs = from_pairs((normalized(fourth, stats_5) * gain[5] + shift[5]).astype(BF), place)

    d4, dg5, db5 = norm_back(cotangent.astype(F32), fourth, stats_5, gain[5])
    d3, g_in_b, g_out_b, dbias_b, ds7, dg4, db4 = ffn_back(d4, third, 4, w_in_b, w_out_b, kept_b)
    share_out_b = cube.scatter(*g_out_b)
    share_in_b = cube.scatter(*g_in_b)
    dout = d3.astype(BF)
    ds14 = colsum(dout)
    g_conv_out = cube.product_back(active_c, dout)
    dactive = cube.arrange(mm_bt(dout, w_conv_out))
    dnormed = dactive * silu_slope(normalized(conv, stats_3) * gain[3] + shift[3])
    dconv, dg3, db3 = norm_back(dnormed, conv, stats_3, gain[3])
    ds13 = colsum(dconv)
    dtaps = jnp.stack([jnp.sum(dconv * padded[tap : tap + count], axis=0) for tap in range(n_tap)])
    follow = lax.ppermute(dconv[:reach], "seq", [(j, i) for i, j in pairs])
    dpadded = jnp.concatenate([dconv, follow], axis=0)
    dgated = taps[0] * dpadded[reach : reach + count]
    for tap in range(1, n_tap):
        dgated = dgated + taps[tap] * dpadded[reach - tap : reach - tap + count]
    val, sig = glu_value.astype(F32), glu_gate.astype(F32)
    dglu = jnp.concatenate([dgated * sig, dgated * val * sig * (1.0 - sig)], axis=1).astype(BF)
    ds11_12 = colsum(dglu)
    g_conv_in = cube.product_back(unit_2, dglu)
    dunit = cube.arrange(mm_bt(dglu, w_conv_in))
    dv, dg2, db2 = norm_back(dunit, second, stats_2, gain[2])
    d2 = d3 + dv
    dout = d2.astype(BF)
    ds10 = colsum(dout)
    g_attn = cube.product_back(mixed, dout)
    dmixed = cube.arrange(mm_bt(dout, w_attn)).astype(BF)
    dmixed = to_heads(dmixed, odd)
    dq, dk, dv_, dtable = attend_back(query, key_rows, value, dmixed, probs, wide)
    dq, dk, dv_ = to_tokens(dq, odd), to_tokens(dk, odd), to_tokens(dv_, odd)
    if shards == 8:
        g_mid = tuple(jnp.concatenate(parts, axis=1) for parts in zip(g_attn, g_conv_in, g_conv_out))
    else:
        g_mid = (None, jnp.concatenate([g_attn[1], g_conv_in[1], g_conv_out[1]], axis=1))
    share_mid = cube.scatter(*g_mid)
    ds8, ds9 = colsum(dq), colsum(dv_)
    dqkv = jnp.concatenate([dq, dk, dv_], axis=1)
    g_qkv = cube.product_back(unit_1, dqkv)
    dunit = cube.arrange(mm_bt(dqkv, w_qkv))
    dv, dg1, db1 = norm_back(dunit, first, stats_1, gain[1])
    d1 = d2 + dv
    share_qkv = cube.scatter(*g_qkv)
    d0, g_in_a, g_out_a, dbias_a, ds6, dg0, db0 = ffn_back(d1, tokens, 0, w_in_a, w_out_a, kept_a)
    share_out_a = cube.scatter(*g_out_a)
    share_in_a = cube.scatter(*g_in_a)
    grad_tokens = from_pairs(d0.astype(BF), place)

    dtable = (dtable[: distance.shape[0], :HEAD_DIM] + dtable[: distance.shape[0], HEAD_DIM:]).reshape(-1)
    pad = (-dtable.shape[0]) % width
    vectors = [dg0, dg1, dg2, dg3, dg4, dg5]
    vectors += [db0, db1, db2, db3, db4, db5, ds6, ds7, ds8, ds9, ds10, ds11_12, ds13, ds14]
    flat = jnp.concatenate(
        vectors + [dtaps.reshape(-1), dbias_a, dbias_b, dtable, jnp.zeros((pad,), F32)]
    ).reshape(-1, width)
    flat = lax.psum(flat, ("seq", "fsdp"))
    own = lax.dynamic_slice_in_dim(flat, me * (width // shards), width // shards, 1)
    at = n_gain + n_shift + n_tap
    biases = flat[at : at + bias_rows].reshape(2, inner_width)
    share_bias = lax.dynamic_slice_in_dim(biases, me * (inner_width // shards), inner_width // shards, 1)
    total_table = flat[at + bias_rows :].reshape(-1)[: distance.size].reshape(distance.shape)
    return (
        outputs,
        grad_tokens,
        jnp.stack([share_in_a, share_in_b]),
        share_bias,
        jnp.stack([share_out_a, share_out_b]),
        jnp.stack([share_qkv[:, :width], share_qkv[:, width : 2 * width], share_qkv[:, 2 * width :]]),
        share_mid[:, :width],
        share_mid[:, width : 3 * width],
        share_mid[:, 3 * width :],
        own[n_gain + n_shift : at],
        own[:n_gain],
        own[n_gain : n_gain + n_shift],
        total_table,
    )


def solution(mesh):
    return jax.shard_map(
        on_device,
        mesh=mesh,
        in_specs=(
            P("fsdp", "seq", None),
            P("fsdp"),
            P(None, "fsdp", None),
            P(None, "fsdp"),
            P(None, "fsdp", None),
            P(None, "fsdp", None),
            P("fsdp", None),
            P("fsdp", None),
            P("fsdp", None),
            P(None, "fsdp"),
            P(None, "fsdp"),
            P(None, "fsdp"),
            P(),
            P("fsdp", "seq", None),
        ),
        out_specs=(
            P("fsdp", "seq", None),
            P("fsdp", "seq", None),
            P(None, "fsdp", None),
            P(None, "fsdp"),
            P(None, "fsdp", None),
            P(None, "fsdp", None),
            P("fsdp", None),
            P("fsdp", None),
            P("fsdp", None),
            P(None, "fsdp"),
            P(None, "fsdp"),
            P(None, "fsdp"),
            P(),
        ),
        check_vma=False,
    )
```

time: 3920 us -> 1610 us (0.41)
  local copies, waits for them, and re-layouts: 1350 us -> 363 us
  waiting for transfers between devices: 1400 us -> 559 us
  matrix products: 405 us -> 154 us
  other arithmetic: 468 us -> 241 us
  blocking collectives: 129 us -> 17 us
  Pallas kernels: 0 us -> 95.8 us
  starting transfers between devices: 78.9 us -> 150 us
  loops' own time: 52.2 us -> 0 us
    reduce_scatter x9 -> x0, waiting for transfers between devices: 749 us -> none  [the longest x1 207 us: on_device(): lax.psum_scatter(totals[0], 'fsdp', scatter_dimension=1, tiled=True)]
    while x842 -> x0, local copies, waits for them, and re-layouts: 450 us -> none
    ppermute x4 -> x126, waiting for transfers between devices: 8.63 us -> 440 us  [the longest x116 432 us: swapped(): return lax.ppermute(block, axis, xor_route(axis, mask))]
    reshape x28 -> x24, local copies, waits for them, and re-layouts: 426 us -> 36.2 us  [the longest x18 34.6 us: arrange(): blocks = value.reshape(rows, 8, cols // 8)]
    all_gather x12 -> x0, waiting for transfers between devices: 370 us -> none  [the longest x2 166 us: micro_step(): lax.all_gather(ffn_out, 'fsdp', axis=1, tiled=True)]
    dot_general x100 -> x34, matrix products: 360 us -> 154 us  [dot(): lax.dot_general(a, b, (((ca,), (cb,)), ((), ())), preferred_element_type=...]
    ppermute x4 -> x126, starting transfers between devices: 5.17 us -> 150 us  [the longest x116 128 us: swapped(): return lax.ppermute(block, axis, xor_route(axis, mask))]
    add x26 -> x32, other arithmetic: 152 us -> 21.7 us  [the longest x6 6.16 us: scatter(): two = two[:2] + got.astype(F32)]
  transfers between devices with their start and end apart: 43 -> 127, of which waited for: 28 -> 46; matrix products, arithmetic and copies ran while one was open for 20% -> 30% of each run, Pallas kernels for 0% -> 6%
where the time goes in v1:
time: 1610 us; the launch traced here: 1600 us
  waiting for transfers between devices  559 us (35%)
  local copies, waits for them, and re-layouts  363 us (23%)
  other arithmetic  241 us (15%)
  matrix products  154 us (10%)
  starting transfers between devices  150 us (9%)
  Pallas kernels  95.8 us (6%)
  between operations  21.6 us (1%)
  blocking collectives  17 us (1%)
    ppermute x116, waiting for transfers between devices, swapped(): return lax.ppermute(block, axis, xor_route(axis, mask))  432 us
    dot_general x34, matrix products, dot(): lax.dot_general(a, b, (((ca,), (cb,)), ((), ())), preferred_element_type=...  154 us
    ppermute x116, starting transfers between devices, swapped(): return lax.ppermute(block, axis, xor_route(axis, mask))  128 us
    unnamed x721, local copies, waits for them, and re-layouts  122 us
    psum x1, waiting for transfers between devices, on_device(): flat = lax.psum(flat, ('seq', 'fsdp'))  119 us
    another operation x28, local copies, waits for them, and re-layouts, arrange(): turned = jnp.stack([blocks[:, i] for i in order], axis=1)  58.4 us
    pallas_call x1, Pallas kernels, attend_back(): pl.pallas_call(bwd_kernel, grid=(pairs, n // RB), in_specs=[rows, whole,...  51.7 us
    pallas_call x1, Pallas kernels, attend(): pl.pallas_call(fwd_kernel, grid=(pairs, n // RB), in_specs=[pl.BlockSpec(...  44.1 us
  transfers between devices with their start and end apart: 127, of which 46 were waited for; matrix products, arithmetic and copies ran while one was open for 30% of the time, Pallas kernels for 6%

profile of v1, /device:TPU:0, one launch (start us, length us, event | category | flops | bytes accessed | tf_op | source)
XLA Modules:
  0.0 1601.3 jit_solution(17016951947891975967)
XLA Ops:
  20.5 17.0 %all-gather.1 = bf16[8,60,128]{2,1,0:T(8,128)(2,1)S(1)} all-gather(bf16[1,60,128]{2,1,0:T(8,128)(2,1)S(1)} %maximum_bitcast_fusion.8), channel_id=2, replica_groups=mesh['seq'=4,'fsdp'=8] {'fsdp'}, dimensions={0}, use_global_device_ids=true | all-gather | bytes 138240 | tf_op jit(solution)/shard_map/all_gather | solution.py:352
  85.2 12.0 collective-permute-done.46
  101.8 21.0 %collective-permute-done.34 = bf16[128,4096]{1,0:T(8,128)(2,1)} collective-permute-done((bf16[128,4096]{1,0:T(8,128)(2,1)}, bf16[128,4096]{1,0:T(8,128)(2,1)}, u32[]{:S(2)}, u32[]{:S(2)}) %collective-permute-start.34) | collective-permute-done | bytes 1048608 | tf_op jit(solution)/shard_map/ppermute | solution.py:202
  130.7 14.5 collective-permute-done.3
  153.7 13.9 collective-permute-done.53
  210.2 13.8 collective-permute-done.8
  365.2 16.3 %collective-permute-start.31 = (bf16[512,512]{1,0:T(8,128)(2,1)S(1)}, bf16[512,512]{1,0:T(8,128)(2,1)S(1)}, u32[]{:S(2)}, u32[]{:S(2)}) collective-permute-start(bf16[512,512]{1,0:T(8,128)(2,1)S(1)} %copy-done.141), channel_id=1, source_target_pairs={{0,8},{8,0},{16,24},{24,16},{1,9},{9,1},{17,25},{25,17},{2,10},{10... | collective-permute-start | bytes 1572872 | tf_op jit(solution)/shard_map/ppermute | solution.py:202
  416.5 44.1 %attend_fwd.1 = (bf16[8,1024,1024]{2,1,0:T(8,128)(2,1)S(1)}, bf16[1024,512]{1,0:T(8,128)(2,1)S(1)}) custom-call(s32[1]{0:T(128)} %bitcast.15.len_ref, bf16[1024,512]{1,0:T(8,128)(2,1)S(1)} %pad_maximum_fusion.26.q_ref, bf16[1024,512]{1,0:T(8,128)(2,1)S(1)} %pad_maximum_fusion.27.k_ref, bf16[1024,512]{1,0:T(8,128)(2,1)S(1)} %pad_maximum_fusion.28.v_ref, ...), custom_call_target="tpu_custom_call" | custom-call | tf_op jit(solution)/shard_map/attend_fwd/pallas_call | solution.py:133
  776.7 12.2 fusion.65
  825.2 51.7 %attend_bwd.1 = (bf16[1024,512]{1,0:T(8,128)(2,1)S(1)}, bf16[1024,512]{1,0:T(8,128)(2,1)S(1)}, bf16[1024,512]{1,0:T(8,128)(2,1)S(1)}, f32[128,128]{1,0:T(8,128)S(1)}) custom-call(bf16[1024,512]{1,0:T(8,128)(2,1)S(1)} %copy-done.4, bf16[1024,512]{1,0:T(8,128)(2,1)S(1)} %copy-done.6, bf16[1024,512]{1,0:T(8,128)(2,1)S(1)} %copy-done.2, ...), custom_call_target="tpu_custom_call" | custom-call | tf_op jit(solution)/shard_map/attend_bwd/pallas_call | solution.py:148
  880.1 12.8 collective-permute-done.67
  897.7 16.2 %collective-permute-done.68 = bf16[512,512]{1,0:T(8,128)(2,1)S(1)} collective-permute-done((bf16[512,512]{1,0:T(8,128)(2,1)S(1)}, bf16[512,512]{1,0:T(8,128)(2,1)S(1)}, u32[]{:S(2)}, u32[]{:S(2)}) %collective-permute-start.68) | collective-permute-done | bytes 524320 | tf_op jit(solution)/shard_map/ppermute | solution.py:202
  1046.9 119.1 %all-reduce.2.cloned.1.call-done = f32[65,1024]{1,0:T(8,128)} async-done(((f32[65,1024]{1,0:T(8,128)}), f32[65,1024]{1,0:T(8,128)}) %all-reduce.2.cloned.1.call-update) | async-done | bytes 266256 | tf_op jit(solution)/shard_map/psum | solution.py:482
  1216.7 20.4 %collective-permute-done.111 = bf16[2,128,1536]{2,1,0:T(8,128)(2,1)} collective-permute-done((bf16[2,128,1536]{2,1,0:T(8,128)(2,1)}, bf16[2,128,1536]{2,1,0:T(8,128)(2,1)}, u32[]{:S(2)}, u32[]{:S(2)}) %collective-permute-start.111) | collective-permute-done | bytes 786464 | tf_op jit(solution)/shard_map/ppermute | solution.py:202
  1248.3 14.9 collective-permute-done.100
  1268.1 17.7 %collective-permute-done.82 = bf16[2,128,2048]{2,1,0:T(8,128)(2,1)S(1)} collective-permute-done((bf16[2,128,2048]{2,1,0:T(8,128)(2,1)S(1)}, bf16[2,128,2048]{2,1,0:T(8,128)(2,1)S(1)}, u32[]{:S(2)}, u32[]{:S(2)}) %collective-permute-start.82) | collective-permute-done | bytes 1048608 | tf_op jit(solution)/shard_map/ppermute | solution.py:202
  1341.7 28.7 %collective-permute-done.121 = bf16[128,2048]{1,0:T(8,128)(2,1)S(1)} collective-permute-done((bf16[128,2048]{1,0:T(8,128)(2,1)}, bf16[128,2048]{1,0:T(8,128)(2,1)S(1)}, u32[]{:S(2)}, u32[]{:S(2)}) %collective-permute-start.121) | collective-permute-done | bytes 524320 | tf_op jit(solution)/shard_map/ppermute | solution.py:202
  1407.7 17.5 %collective-permute-done.104 = bf16[256,1024]{1,0:T(8,128)(2,1)S(1)} collective-permute-done((bf16[256,1024]{1,0:T(8,128)(2,1)S(1)}, bf16[256,1024]{1,0:T(8,128)(2,1)S(1)}, u32[]{:S(2)}, u32[]{:S(2)}) %collective-permute-start.104) | collective-permute-done | bytes 524320 | tf_op jit(solution)/shard_map/ppermute | solution.py:202
  1432.4 13.5 collective-permute-done.122
  1466.3 12.3 collective-permute-done.88
  1478.8 14.1 collective-permute-done.106
  1502.7 22.5 %collective-permute-done.89 = bf16[64,4096]{1,0:T(8,128)(2,1)S(1)} collective-permute-done((bf16[64,4096]{1,0:T(8,128)(2,1)S(1)}, bf16[64,4096]{1,0:T(8,128)(2,1)S(1)}, u32[]{:S(2)}, u32[]{:S(2)}) %collective-permute-start.89) | collective-permute-done | bytes 524320 | tf_op jit(solution)/shard_map/ppermute | solution.py:202
  1525.4 13.8 collective-permute-done.95
  1539.6 12.0 collective-permute-done.77
  (1410 shorter events, 1027.8 us)
Async XLA Ops:
  7.2 1158.8 %all-reduce.2.cloned.1.call-start = ((), (), s32[]{:S(2)}) async-start(), calls=%async_computation | async-start | bytes 589824 | tf_op jit(solution)/shard_map/psum | solution.py:482
  9.9 64.3 %collective-permute-start.21 = (bf16[128,3072]{1,0:T(8,128)(2,1)}, bf16[128,3072]{1,0:T(8,128)(2,1)}, u32[]{:S(2)}, u32[]{:S(2)}) collective-permute-start(bf16[128,3072]{1,0:T(8,128)(2,1)} %get-tuple-element.365), channel_id=1, source_target_pairs={{0,2},{1,3},{2,0},{3,1},{4,6},{5,7},{6,4},{7,5},{8,10},{9,11},{10,... | collective-permute-start | bytes 2359304 | tf_op jit(solution)/shard_map/ppermute | solution.py:202
  12.8 65.1 %collective-permute-start.20 = (bf16[128,3072]{1,0:T(8,128)(2,1)}, bf16[128,3072]{1,0:T(8,128)(2,1)}, u32[]{:S(2)}, u32[]{:S(2)}) collective-permute-start(bf16[128,3072]{1,0:T(8,128)(2,1)} %get-tuple-element.365), channel_id=1, source_target_pairs={{0,1},{1,0},{2,3},{3,2},{4,5},{5,4},{6,7},{7,6},{8,9},{9,8},{10,11... | collective-permute-start | bytes 2359304 | tf_op jit(solution)/shard_map/ppermute | solution.py:202
  12.8 63.9 %collective-permute-start.23 = (bf16[128,3072]{1,0:T(8,128)(2,1)}, bf16[128,3072]{1,0:T(8,128)(2,1)}, u32[]{:S(2)}, u32[]{:S(2)}) collective-permute-start(bf16[128,3072]{1,0:T(8,128)(2,1)} %get-tuple-element.365), channel_id=1, source_target_pairs={{0,4},{1,5},{2,6},{3,7},{4,0},{5,1},{6,2},{7,3},{8,12},{9,13},{10,... | collective-permute-start | bytes 2359304 | tf_op jit(solution)/shard_map/ppermute | solution.py:202
  194.7 131.8 %collective-permute-start.49 = (bf16[64,4096]{1,0:T(8,128)(2,1)}, bf16[64,4096]{1,0:T(8,128)(2,1)}, u32[]{:S(2)}, u32[]{:S(2)}) collective-permute-start(bf16[64,4096]{1,0:T(8,128)(2,1)} %slice.2715), channel_id=1, source_target_pairs={{0,2},{1,3},{2,0},{3,1},{4,6},{5,7},{6,4},{7,5},{8,10},{9,11},{10,... | collective-permute-start | bytes 1572872 | tf_op jit(solution)/shard_map/ppermute | solution.py:202
  244.1 72.0 %collective-permute-start.48 = (bf16[64,4096]{1,0:T(8,128)(2,1)}, bf16[64,4096]{1,0:T(8,128)(2,1)}, u32[]{:S(2)}, u32[]{:S(2)}) collective-permute-start(bf16[64,4096]{1,0:T(8,128)(2,1)} %slice.2714), channel_id=1, source_target_pairs={{0,4},{1,5},{2,6},{3,7},{4,0},{5,1},{6,2},{7,3},{8,12},{9,13},{10,... | collective-permute-start | bytes 1572872 | tf_op jit(solution)/shard_map/ppermute | solution.py:202
  260.3 103.6 %collective-permute-start.58 = (bf16[256,1024]{1,0:T(8,128)(2,1)}, bf16[256,1024]{1,0:T(8,128)(2,1)}, u32[]{:S(2)}, u32[]{:S(2)}) collective-permute-start(bf16[256,1024]{1,0:T(8,128)(2,1)} %slice.2732), channel_id=1, source_target_pairs={{0,2},{1,3},{2,0},{3,1},{4,6},{5,7},{6,4},{7,5},{8,10},{9,11},{10,... | collective-permute-start | bytes 1572872 | tf_op jit(solution)/shard_map/ppermute | solution.py:202
  293.1 68.6 %collective-permute-start.57 = (bf16[256,1024]{1,0:T(8,128)(2,1)}, bf16[256,1024]{1,0:T(8,128)(2,1)}, u32[]{:S(2)}, u32[]{:S(2)}) collective-permute-start(bf16[256,1024]{1,0:T(8,128)(2,1)} %slice.2731), channel_id=1, source_target_pairs={{0,4},{1,5},{2,6},{3,7},{4,0},{5,1},{6,2},{7,3},{8,12},{9,13},{10,... | collective-permute-start | bytes 1572872 | tf_op jit(solution)/shard_map/ppermute | solution.py:202
  341.2 127.9 %collective-permute-start.51 = (bf16[64,4096]{1,0:T(8,128)(2,1)}, bf16[64,4096]{1,0:T(8,128)(2,1)}, u32[]{:S(2)}, u32[]{:S(2)}) collective-permute-start(bf16[64,4096]{1,0:T(8,128)(2,1)} %collective-permute-done.49), channel_id=1, source_target_pairs={{0,1},{1,0},{2,3},{3,2},{4,5},{5,4},{6,7},{7,6},{8,9},{9,8},{10,11... | collective-permute-start | bytes 1572872 | tf_op jit(solution)/shard_map/ppermute | solution.py:202
  364.1 104.2 %collective-permute-start.60 = (bf16[256,1024]{1,0:T(8,128)(2,1)}, bf16[256,1024]{1,0:T(8,128)(2,1)S(1)}, u32[]{:S(2)}, u32[]{:S(2)}) collective-permute-start(bf16[256,1024]{1,0:T(8,128)(2,1)} %collective-permute-done.58), channel_id=1, source_target_pairs={{0,1},{1,0},{2,3},{3,2},{4,5},{5,4},{6,7},{7,6},{8,9},{9,8},{10,11... | collective-permute-start | bytes 1572872 | tf_op jit(solution)/shard_map/ppermute | solution.py:202
  749.7 424.7 %collective-permute-start.99 = (bf16[2048,1024]{1,0:T(8,128)(2,1)}, bf16[2048,1024]{1,0:T(8,128)(2,1)}, u32[]{:S(2)}, u32[]{:S(2)}) collective-permute-start(bf16[2048,1024]{1,0:T(8,128)(2,1)} %convolution_convert_fusion.3), channel_id=1, source_target_pairs={{0,1},{1,0},{2,3},{3,2},{4,5},{5,4},{6,7},{7,6},{8,9},{9,8},{10,11... | collective-permute-start | bytes 12582920 | tf_op jit(solution)/shard_map/ppermute | solution.py:202
  752.2 66.6 %collective-permute-start.61 = (bf16[256,1024]{1,0:T(8,128)(2,1)}, bf16[256,1024]{1,0:T(8,128)(2,1)}, u32[]{:S(2)}, u32[]{:S(2)}) collective-permute-start(bf16[256,1024]{1,0:T(8,128)(2,1)} %get-tuple-element.326), channel_id=1, source_target_pairs={{8,16},{16,8},{9,17},{17,9},{10,18},{18,10},{11,19},{19,11},{12,20... | collective-permute-start | bytes 1572872 | tf_op jit(solution)/shard_map/ppermute | solution.py:300
  776.4 409.4 %collective-permute-start.81 = (bf16[512,4096]{1,0:T(8,128)(2,1)}, bf16[512,4096]{1,0:T(8,128)(2,1)}, u32[]{:S(2)}, u32[]{:S(2)}) collective-permute-start(bf16[512,4096]{1,0:T(8,128)(2,1)} %convolution_convert_fusion), channel_id=1, source_target_pairs={{0,1},{1,0},{2,3},{3,2},{4,5},{5,4},{6,7},{7,6},{8,9},{9,8},{10,11... | collective-permute-start | bytes 12582920 | tf_op jit(solution)/shard_map/ppermute | solution.py:202
  818.8 386.8 %collective-permute-start.117 = (bf16[512,4096]{1,0:T(8,128)(2,1)}, bf16[512,4096]{1,0:T(8,128)(2,1)}, u32[]{:S(2)}, u32[]{:S(2)}) collective-permute-start(bf16[512,4096]{1,0:T(8,128)(2,1)} %pad_maximum_fusion.6), channel_id=1, source_target_pairs={{0,1},{1,0},{2,3},{3,2},{4,5},{5,4},{6,7},{7,6},{8,9},{9,8},{10,11... | collective-permute-start | bytes 12582920 | tf_op jit(solution)/shard_map/ppermute | solution.py:202
  939.7 259.3 %collective-permute-start.108 = (bf16[512,3072]{1,0:T(8,128)(2,1)}, bf16[512,3072]{1,0:T(8,128)(2,1)}, u32[]{:S(2)}, u32[]{:S(2)}) collective-permute-start(bf16[512,3072]{1,0:T(8,128)(2,1)} %convolution_convert_fusion.2), channel_id=1, source_target_pairs={{0,1},{1,0},{2,3},{3,2},{4,5},{5,4},{6,7},{7,6},{8,9},{9,8},{10,11... | collective-permute-start | bytes 9437192 | tf_op jit(solution)/shard_map/ppermute | solution.py:202
  1041.8 131.3 %collective-permute-start.70 = (bf16[256,1024]{1,0:T(8,128)(2,1)S(1)}, bf16[256,1024]{1,0:T(8,128)(2,1)S(1)}, u32[]{:S(2)}, u32[]{:S(2)}) collective-permute-start(bf16[256,1024]{1,0:T(8,128)(2,1)S(1)} %get-tuple-element.314), channel_id=1, source_target_pairs={{8,16},{16,8},{9,17},{17,9},{10,18},{18,10},{11,19},{19,11},{12,20... | collective-permute-start | bytes 1572872 | tf_op jit(solution)/shard_map/ppermute | solution.py:300
  1173.2 115.3 %collective-permute-start.90 = (bf16[2048,1024]{1,0:T(8,128)(2,1)}, bf16[2048,1024]{1,0:T(8,128)(2,1)}, u32[]{:S(2)}, u32[]{:S(2)}) collective-permute-start(bf16[2048,1024]{1,0:T(8,128)(2,1)} %convolution_convert_fusion.4), channel_id=1, source_target_pairs={{0,1},{1,0},{2,3},{3,2},{4,5},{5,4},{6,7},{7,6},{8,9},{9,8},{10,11... | collective-permute-start | bytes 12582920 | tf_op jit(solution)/shard_map/ppermute | solution.py:202
  1174.4 123.1 %collective-permute-start.72 = (bf16[512,4096]{1,0:T(8,128)(2,1)}, bf16[512,4096]{1,0:T(8,128)(2,1)}, u32[]{:S(2)}, u32[]{:S(2)}) collective-permute-start(bf16[512,4096]{1,0:T(8,128)(2,1)} %convolution_convert_fusion.1), channel_id=1, source_target_pairs={{0,1},{1,0},{2,3},{3,2},{4,5},{5,4},{6,7},{7,6},{8,9},{9,8},{10,11... | collective-permute-start | bytes 12582920 | tf_op jit(solution)/shard_map/ppermute | solution.py:202
  1319.7 105.8 %collective-permute-start.93 = (bf16[2,512,512]{2,1,0:T(8,128)(2,1)S(1)}, bf16[2,512,512]{2,1,0:T(8,128)(2,1)S(1)}, u32[]{:S(2)}, u32[]{:S(2)}) collective-permute-start(bf16[2,512,512]{2,1,0:T(8,128)(2,1)S(1)} %copy-done.123), channel_id=1, source_target_pairs={{0,4},{1,5},{2,6},{3,7},{4,0},{5,1},{6,2},{7,3},{8,12},{9,13},{10,... | collective-permute-start | bytes 3145736 | tf_op jit(solution)/shard_map/ppermute | solution.py:202
  1328.0 100.1 %collective-permute-start.91 = (bf16[2,512,512]{2,1,0:T(8,128)(2,1)}, bf16[2,512,512]{2,1,0:T(8,128)(2,1)S(1)}, u32[]{:S(2)}, u32[]{:S(2)}) collective-permute-start(bf16[2,512,512]{2,1,0:T(8,128)(2,1)} %slice.2437), channel_id=1, source_target_pairs={{0,2},{1,3},{2,0},{3,1},{4,6},{5,7},{6,4},{7,5},{8,10},{9,11},{10,... | collective-permute-start | bytes 3145736 | tf_op jit(solution)/shard_map/ppermute | solution.py:202
  1340.7 87.9 %collective-permute-start.75 = (bf16[2,128,2048]{2,1,0:T(8,128)(2,1)S(1)}, bf16[2,128,2048]{2,1,0:T(8,128)(2,1)S(1)}, u32[]{:S(2)}, u32[]{:S(2)}) collective-permute-start(bf16[2,128,2048]{2,1,0:T(8,128)(2,1)S(1)} %copy-done.122), channel_id=1, source_target_pairs={{0,4},{1,5},{2,6},{3,7},{4,0},{5,1},{6,2},{7,3},{8,12},{9,13},{10,... | collective-permute-start | bytes 3145736 | tf_op jit(solution)/shard_map/ppermute | solution.py:202
  1431.9 61.0 %collective-permute-start.94 = (bf16[512,512]{1,0:T(8,128)(2,1)S(1)}, bf16[512,512]{1,0:T(8,128)(2,1)S(1)}, u32[]{:S(2)}, u32[]{:S(2)}) collective-permute-start(bf16[512,512]{1,0:T(8,128)(2,1)S(1)} %fusion.321), channel_id=1, source_target_pairs={{0,2},{1,3},{2,0},{3,1},{4,6},{5,7},{6,4},{7,5},{8,10},{9,11},{10,... | collective-permute-start | bytes 1572872 | tf_op jit(solution)/shard_map/ppermute | solution.py:202
  1493.0 58.9 %collective-permute-start.107 = (bf16[256,1024]{1,0:T(8,128)(2,1)S(1)}, bf16[256,1024]{1,0:T(8,128)(2,1)S(1)}, u32[]{:S(2)}, u32[]{:S(2)}) collective-permute-start(bf16[256,1024]{1,0:T(8,128)(2,1)S(1)} %maximum_select_fusion.9), channel_id=1, source_target_pairs={{0,8},{8,0},{16,24},{24,16},{1,9},{9,1},{17,25},{25,17},{2,10},{10... | collective-permute-start | bytes 1572872 | tf_op jit(solution)/shard_map/ppermute | solution.py:202
  1502.6 67.9 %collective-permute-start.125 = (bf16[64,4096]{1,0:T(8,128)(2,1)S(1)}, bf16[64,4096]{1,0:T(8,128)(2,1)S(1)}, u32[]{:S(2)}, u32[]{:S(2)}) collective-permute-start(bf16[64,4096]{1,0:T(8,128)(2,1)S(1)} %maximum_select_fusion.10), channel_id=1, source_target_pairs={{0,8},{8,0},{16,24},{24,16},{1,9},{9,1},{17,25},{25,17},{2,10},{10... | collective-permute-start | bytes 1572872 | tf_op jit(solution)/shard_map/ppermute | solution.py:202
  (381 other events, 5953.1 us)
Sparse Core Ops, SparseCore 0:
  1024.8 141.1 all-reduce.1

commit v2 on v1

v2 whole, which is shorter than its diff:
```python
import functools

import jax
import jax.numpy as jnp
from jax import lax
from jax.experimental import pallas as pl
from jax.experimental.pallas import tpu as pltpu
from jax.sharding import PartitionSpec as P

HEAD_DIM=64; LEFT=64; RIGHT=8
F32=jnp.float32; BF=jnp.bfloat16
RB=256
PADL=128
WIN=512

def dot(a,b,ca,cb):
    return lax.dot_general(a,b,(((ca,),(cb,)),((),())),preferred_element_type=F32)

def lanes(shape):
    return lax.broadcasted_iota(jnp.int32,shape,1)

def band_offset():
    row=lax.broadcasted_iota(jnp.int32,(RB,WIN),0)
    col=lax.broadcasted_iota(jnp.int32,(RB,WIN),1)
    return col-row-LEFT


MESH = pl.DeviceIdType.MESH
STEPS = 4


def pair_place():
    place = lax.axis_index("seq")
    half = lax.rem(place, jnp.int32(2))
    return half, {"seq": place + 1 - 2 * half}


def meet(partner):
    barrier = pltpu.get_barrier_semaphore()
    pl.semaphore_signal(barrier, inc=1, device_id=partner, device_id_type=MESH)
    pl.semaphore_wait(barrier, 1)


def block_at(step, half):
    return lax.rem(step + 2 * (1 - half), jnp.int32(STEPS))


def fwd_kernel(len_ref,wide_ref,ends_ref,mine_ref,other_ref,p_ref,heads_ref,mixed_ref,s_ref,kx_ref,buf,mixed,stage,in_send,in_recv,in_load,out_send,out_recv):
    n=buf.shape[2]; own=n//2
    pair=pl.program_id(0); step=pl.program_id(1)
    pairs=buf.shape[0]
    half,partner=pair_place()
    at=pl.multiple_of(half*own,own)
    def arrive(a):
        return pltpu.make_async_remote_copy(src_ref=other_ref.at[a],dst_ref=buf.at[a,:,pl.ds(at,own)],send_sem=in_send.at[a],recv_sem=in_recv.at[a],device_id=partner,device_id_type=MESH)
    def load(a):
        return pltpu.make_async_copy(mine_ref.at[a],buf.at[a,:,pl.ds(at,own)],in_load.at[a])
    def leave(a,b):
        cols=pl.ds(pl.multiple_of(half*own+a*128,128),128)
        return pltpu.make_async_remote_copy(src_ref=stage.at[a,b],dst_ref=mixed.at[pl.ds(pl.multiple_of(b*RB,RB),RB),cols],send_sem=out_send.at[a,b],recv_sem=out_recv.at[a,b],device_id=partner,device_id_type=MESH)
    @pl.when((pair==0)&(step==0))
    def _():
        meet(partner)
        for a in range(pairs):
            load(a).start()
            arrive(a).start()
    @pl.when(step==0)
    def _():
        load(pair).wait()
        arrive(pair).wait()
        heads_ref[0]=buf[pair]
        kx_ref[:,0:128]=buf[pair,1]
    i0=pl.multiple_of(block_at(step,half)*RB,RB)
    q2=buf[pair,0,pl.ds(i0,RB)]
    v2=buf[pair,2]
    lane=lanes((RB,128))
    t=lax.broadcasted_iota(jnp.int32,(n,128),0)
    c=lanes((n,128))
    left=(t<i0-128).astype(F32); right=(t>=i0+WIN-128).astype(F32)
    masked=jnp.where(t>=len_ref[0],-1e30,0.0)
    ext=jnp.where(c<2,left,jnp.where(c<4,right,jnp.where(c==4,masked,0.0)))
    kx_ref[:,128:256]=ext.astype(BF)
    outs=[]
    for h in range(2):
        head=(lane<64) if h==0 else (lane>=64)
        qh=jnp.where(head,q2,jnp.zeros_like(q2))
        ends=dot(qh,ends_ref[...],1,0)
        hi=ends.astype(BF).astype(F32)
        qx=jnp.where((lane==0)|(lane==2),hi,jnp.where((lane==1)|(lane==3),ends-hi,jnp.where(lane==4,1.0,0.0))).astype(BF)
        s_ref[:,PADL:PADL+n]=dot(jnp.concatenate([qh,qx],axis=1),kx_ref[...],1,1)
        wide=dot(qh,wide_ref[...],1,0)
        band=pltpu.roll(wide,LEFT,1,stride=1,stride_axis=0)
        j=band_offset()
        band=jnp.where(j>=LEFT+RIGHT,wide[:,LEFT+RIGHT:LEFT+RIGHT+1],band)
        w=pl.ds(i0,WIN)
        s_ref[:,w]=s_ref[:,w]+band
        s=s_ref[:,PADL:PADL+n]
        m=jnp.max(s,axis=1,keepdims=True)
        e=jnp.exp(s-m)
        z=jnp.sum(e,axis=1,keepdims=True)
        p=(e*(1.0/z)).astype(BF)
        p_ref[h]=p
        outs.append(dot(p,v2,1,0))
    out=jnp.where(lane<64,outs[0],outs[1]).astype(BF)
    @pl.when(step<2)
    def _():
        stage[pair,step]=out
        leave(pair,step).start()
    @pl.when(step>=2)
    def _():
        cols=pl.ds(pl.multiple_of(half*own+pair*128,128),128)
        mixed[pl.ds(pl.multiple_of((step-2)*RB,RB),RB),cols]=out
    @pl.when((pair==pairs-1)&(step==STEPS-1))
    def _():
        for a in range(pairs):
            for b in range(2):
                leave(a,b).wait_send()
        for a in range(pairs):
            for b in range(2):
                arrived=pltpu.make_async_remote_copy(src_ref=stage.at[a,b],dst_ref=mixed.at[pl.ds(b*RB,RB),pl.ds(pl.multiple_of((1-half)*own+a*128,128),128)],send_sem=out_send.at[a,b],recv_sem=out_recv.at[a,b],device_id=partner,device_id_type=MESH)
                arrived.wait_recv()
        mixed_ref[...]=mixed[...]


def z_line(middle,to_1,to_2,whole,near,far,z_send,z_recv):
    def copy(i,stage):
        src=(whole,near,far)[stage]; dst=(near,far,near)[stage]
        return pltpu.make_async_remote_copy(src_ref=src.at[i],dst_ref=dst.at[i],send_sem=z_send.at[i,stage],recv_sem=z_recv.at[i,stage],device_id=to_2 if stage==1 else to_1,device_id_type=MESH)
    def begin(i):
        pl.when(middle==0)(lambda: copy(i,0).start())
    def step(i,stage):
        @pl.when(middle==1)
        def _():
            if stage==0:
                copy(i,0).wait_recv()
                near[i]=(whole[i].astype(F32)+near[i].astype(F32)).astype(BF)
                copy(i,1).start()
            elif stage==1:
                copy(i,1).wait()
                far[i]=(near[i].astype(F32)+far[i].astype(F32)).astype(BF)
                copy(i,2).start()
            else:
                copy(i,2).wait_send()
        if stage!=1:
            @pl.when(middle==0)
            def _():
                if stage==0:
                    copy(i,0).wait_send()
                else:
                    copy(i,2).wait_recv()
    return begin,step


def bwd_kernel(with_part,heads_ref,p_ref,wide_ref,mine_ref,other_ref,*rest):
    if with_part:
        part_ref,dqkv_ref,de_ref,out_ref,*rest=rest
        *rest,whole,near,far,part_sem,out_sem,z_send,z_recv=rest
    else:
        dqkv_ref,de_ref,*rest=rest
    ds_ref,kx_ref,dka,dva,dea,buf,dqkv,stage_q,stage_kv,in_send,in_recv,in_load,q_send,q_recv,kv_send,kv_recv=rest
    n=heads_ref.shape[2]; own=n//2
    pair=pl.program_id(0); step=pl.program_id(1)
    pairs=buf.shape[0]
    half,partner=pair_place()
    at=pl.multiple_of(half*own,own)
    width=2*own
    def columns(t,who,a):
        return pl.ds(pl.multiple_of(t*width+who*own+a*128,128),128)
    def arrive(a):
        return pltpu.make_async_remote_copy(src_ref=other_ref.at[a],dst_ref=buf.at[a,pl.ds(at,own)],send_sem=in_send.at[a],recv_sem=in_recv.at[a],device_id=partner,device_id_type=MESH)
    def load(a):
        return pltpu.make_async_copy(mine_ref.at[a],buf.at[a,pl.ds(at,own)],in_load.at[a])
    def leave_q(a,b,who):
        return pltpu.make_async_remote_copy(src_ref=stage_q.at[a,b],dst_ref=dqkv.at[pl.ds(pl.multiple_of(b*RB,RB),RB),columns(0,who,a)],send_sem=q_send.at[a,b],recv_sem=q_recv.at[a,b],device_id=partner,device_id_type=MESH)
    def leave_kv(a,t,who):
        return pltpu.make_async_remote_copy(src_ref=stage_kv.at[a,t],dst_ref=dqkv.at[:,columns(t+1,who,a)],send_sem=kv_send.at[a,t],recv_sem=kv_recv.at[a,t],device_id=partner,device_id_type=MESH)
    if with_part:
        n_part=part_ref.shape[0]
        place=lax.axis_index("seq")
        middle=lax.rem(lax.div(place+1,jnp.int32(2)),jnp.int32(2))
        across={"seq":3-place}
        z_begin,z_step=z_line(middle,partner,across,whole,near,far,z_send,z_recv)
        def part_copy(i):
            return pltpu.make_async_copy(part_ref.at[i],whole.at[i],part_sem.at[i])
        def result_do(i,act):
            for is_middle,src in ((1,far),(0,near)):
                copy=pltpu.make_async_copy(src.at[i],out_ref.at[i],out_sem.at[i])
                pl.when(middle==is_middle)(lambda copy=copy: act(copy))
        now=pair*STEPS+step
    @pl.when((pair==0)&(step==0))
    def _():
        if with_part:
            barrier=pltpu.get_barrier_semaphore()
            for device in (partner,across):
                pl.semaphore_signal(barrier,inc=1,device_id=device,device_id_type=MESH)
            pl.semaphore_wait(barrier,2)
        else:
            meet(partner)
        for a in range(pairs):
            load(a).start()
            arrive(a).start()
        if with_part:
            for i in range(n_part):
                part_copy(i).start()
        dea[...]=jnp.zeros_like(dea)
        ds_ref[:,0:PADL]=jnp.zeros((RB,PADL),F32)
        ds_ref[:,PADL+n:]=jnp.zeros((RB,ds_ref.shape[1]-PADL-n),F32)
    @pl.when(step==0)
    def _():
        load(pair).wait()
        arrive(pair).wait()
        kx_ref[:,0:128]=heads_ref[0,1]
        dka[...]=jnp.zeros_like(dka); dva[...]=jnp.zeros_like(dva)
    if with_part:
        for i in range(n_part):
            @pl.when(now==1+2*i)
            def _(i=i):
                part_copy(i).wait()
                z_begin(i)
            for stage in range(3):
                @pl.when(now==5+2*i+2*stage)
                def _(i=i,stage=stage):
                    z_step(i,stage)
                    if stage==2:
                        result_do(i,lambda copy: copy.start())
    i0=pl.multiple_of(block_at(step,half)*RB,RB)
    q2=heads_ref[0,0,pl.ds(i0,RB)]
    v2=heads_ref[0,2]
    do2=buf[pair,pl.ds(i0,RB)]
    lane=lanes((RB,128))
    row=lax.broadcasted_iota(jnp.int32,(RB,128),0)
    t=lax.broadcasted_iota(jnp.int32,(n,128),0)
    c=lanes((n,128))
    left=(t<i0-128).astype(F32)
    kx_ref[:,128:256]=jnp.where(c==0,left,jnp.where(c==1,1.0,0.0)).astype(BF)
    dqs=[]
    for h in range(2):
        head=(lane<64) if h==0 else (lane>=64)
        doh=jnp.where(head,do2,jnp.zeros_like(do2))
        qh=jnp.where(head,q2,jnp.zeros_like(q2))
        p=p_ref[h]
        dp=dot(doh,v2,1,1)
        pf=p.astype(F32)
        d=jnp.sum(pf*dp,axis=1,keepdims=True)
        dsf=pf*(dp-d)
        ds=dsf.astype(BF)
        ds_ref[:,PADL:PADL+n]=ds.astype(F32)
        dva[...]+=dot(doh,p,0,0)
        dka[...]+=dot(qh,ds,0,0)
        dqx=dot(ds,kx_ref[...],1,0)
        dq,sums=dqx[:,0:128],dqx[:,128:256]
        win=ds_ref[:,pl.ds(i0,WIN)]
        j=band_offset()
        inleft=jnp.sum(jnp.where(j<=0,win,0.0),axis=1,keepdims=True)
        drel=jnp.concatenate([win[8*g:8*g+8,LEFT+8*g:LEFT+8*g+128] for g in range(RB//8)],axis=0)
        for bit in (1,2,4):
            drel=jnp.where((row&bit)!=0,pltpu.roll(drel,128-bit,1),drel)
        drel=jnp.where((lane>0)&(lane<LEFT+RIGHT),drel,0.0)
        bandsum=jnp.sum(drel,axis=1,keepdims=True)
        l=sums[:,0:1]+inleft
        r=sums[:,1:2]-l-bandsum
        drel=jnp.where(lane==0,l,jnp.where(lane==LEFT+RIGHT,r,drel)).astype(BF)
        dq=dq+dot(drel,wide_ref[...],1,1)
        dqs.append(dq)
        dea[...]+=dot(drel,qh,0,0)
    dq=(jnp.where(lane<64,dqs[0],dqs[1])*HEAD_DIM**-0.5).astype(BF)
    @pl.when(step<2)
    def _():
        stage_q[pair,step]=dq
        leave_q(pair,step,half).start()
    @pl.when(step>=2)
    def _():
        dqkv[pl.ds(pl.multiple_of((step-2)*RB,RB),RB),columns(0,half,pair)]=dq
    @pl.when(step==STEPS-1)
    def _():
        for i,acc in enumerate((dka,dva)):
            mine=acc[:,pl.ds(at,own)]
            theirs=acc[:,pl.ds(pl.multiple_of((1-half)*own,own),own)]
            stage_kv[pair,i]=jnp.transpose(theirs).astype(BF)
            leave_kv(pair,i,half).start()
            dqkv[:,columns(i+1,half,pair)]=jnp.transpose(mine).astype(BF)
    @pl.when((pair==pairs-1)&(step==STEPS-1))
    def _():
        for a in range(pairs):
            for b in range(2):
                leave_q(a,b,half).wait_send()
                leave_kv(a,b,half).wait_send()
        for a in range(pairs):
            for b in range(2):
                leave_q(a,b,1-half).wait_recv()
                leave_kv(a,b,1-half).wait_recv()
        dqkv_ref[...]=dqkv[...]
        de_ref[...]=dea[...]
        if with_part:
            for i in range(n_part):
                result_do(i,lambda copy: copy.wait())


def tables(distance):
    e=distance.T
    wide=jnp.concatenate([e,jnp.broadcast_to(e[:,72:73],(64,120)),jnp.broadcast_to(e[:,0:1],(64,WIN-193))],axis=1)
    wide=jnp.concatenate([wide,wide],axis=0)
    ends=jnp.concatenate([e[:,0:1],e[:,0:1],e[:,72:73],e[:,72:73],jnp.zeros((64,124),e.dtype)],axis=1)
    ends=jnp.concatenate([ends,ends],axis=0)
    return wide,ends

def attend(mine,other,length,wide,ends):
    pairs,_,own,_=mine.shape; n=2*own
    dma=pltpu.SemaphoreType.DMA
    whole=lambda *shape: pl.BlockSpec(shape,lambda a,b:(0,)*len(shape))
    anywhere=pl.BlockSpec(memory_space=pl.ANY)
    return pl.pallas_call(fwd_kernel,
        grid=(pairs,STEPS),
        in_specs=[pl.BlockSpec(memory_space=pltpu.SMEM),whole(128,WIN),whole(128,128),anywhere,anywhere],
        out_specs=[pl.BlockSpec((2,RB,n),lambda a,b:(a,b,0)),pl.BlockSpec((1,3,n,128),lambda a,b:(a,0,0,0)),whole(own,2*own)],
        out_shape=[jax.ShapeDtypeStruct((2*pairs,n,n),BF),jax.ShapeDtypeStruct((pairs,3,n,128),BF),jax.ShapeDtypeStruct((own,2*own),BF)],
        scratch_shapes=[pltpu.VMEM((RB,PADL+n+256),F32),pltpu.VMEM((n,256),BF),pltpu.VMEM((pairs,3,n,128),BF),pltpu.VMEM((own,2*own),BF),pltpu.VMEM((pairs,2,RB,128),BF),
            dma((pairs,)),dma((pairs,)),dma((pairs,)),dma((pairs,2)),dma((pairs,2))],
        compiler_params=pltpu.CompilerParams(vmem_limit_bytes=58<<20,collective_id=1,has_side_effects=True),
        cost_estimate=pl.CostEstimate(flops=40_000_000_000,bytes_accessed=120_000_000,transcendentals=0),
        name="attend_fwd",
    )(length,wide,ends,mine,other)

def attend_back(heads,p,wide,mine,other,part=None):
    pairs,_,n,_=heads.shape; own=n//2
    dma=pltpu.SemaphoreType.DMA
    whole=lambda *shape: pl.BlockSpec(shape,lambda a,b:(0,)*len(shape))
    anywhere=pl.BlockSpec(memory_space=pl.ANY)
    with_part=part is not None
    extra=[pltpu.VMEM(part.shape,BF)]*3+[dma((part.shape[0],))]*2+[dma((part.shape[0],3))]*2 if with_part else []
    return pl.pallas_call(functools.partial(bwd_kernel,with_part),
        grid=(pairs,STEPS),
        in_specs=[pl.BlockSpec((1,3,n,128),lambda a,b:(a,0,0,0)),pl.BlockSpec((2,RB,n),lambda a,b:(a,b,0)),whole(128,128),anywhere,anywhere]+[anywhere]*with_part,
        out_specs=[whole(own,6*own),whole(128,128)]+[anywhere]*with_part,
        out_shape=[jax.ShapeDtypeStruct((own,6*own),BF),jax.ShapeDtypeStruct((128,128),F32)]+([jax.ShapeDtypeStruct(part.shape,BF)] if with_part else []),
        scratch_shapes=[pltpu.VMEM((RB,PADL+n+256),F32),pltpu.VMEM((n,256),BF),pltpu.VMEM((128,n),F32),pltpu.VMEM((128,n),F32),pltpu.VMEM((128,128),F32),
            pltpu.VMEM((pairs,n,128),BF),pltpu.VMEM((own,6*own),BF),pltpu.VMEM((pairs,2,RB,128),BF),pltpu.VMEM((pairs,2,own,128),BF),
            dma((pairs,)),dma((pairs,)),dma((pairs,)),dma((pairs,2)),dma((pairs,2)),dma((pairs,2)),dma((pairs,2))]+extra,
        compiler_params=pltpu.CompilerParams(vmem_limit_bytes=58<<20,collective_id=2,has_side_effects=True),
        cost_estimate=pl.CostEstimate(flops=50_000_000_000,bytes_accessed=150_000_000,transcendentals=0),
        name="attend_bwd",
    )(heads,p,wide[:,0:128],mine,other,*([part] if with_part else []))


EPSILON = 1e-05
HALF = 0.5
CUT = 256
VMEM = 56 << 20


def flat(ref):
    value = ref[...]
    return value.reshape(-1, value.shape[-1])


def cuts(count):
    return [pl.ds(i, CUT) for i in range(0, count, CUT)]


def normal(v):
    c = v - jnp.mean(v, axis=-1, keepdims=True)
    r = lax.rsqrt(jnp.mean(c * c, axis=-1, keepdims=True) + EPSILON)
    return c * r, r


def normal_back(dy, unit, r, gain):
    a = dy * gain
    return (a - jnp.mean(a, axis=-1, keepdims=True) - unit * jnp.mean(a * unit, axis=-1, keepdims=True)) * r


def total(v):
    return jnp.sum(v, axis=0, keepdims=True)


def silu_slope(v):
    s = jax.nn.sigmoid(v)
    return s * (1.0 + v * (1.0 - s))


def call(kernel, grid, ins, outs, scratch=(), name=None, aliases=None, flops=0, moved=0):
    def spec(shape, block, where):
        if block is None:
            return pl.BlockSpec(shape, lambda *_: (0,) * len(shape))
        if block == "smem":
            return pl.BlockSpec(memory_space=pltpu.SMEM)
        if block == "any":
            return pl.BlockSpec(memory_space=pl.ANY)
        return pl.BlockSpec(block, where)

    return pl.pallas_call(
        kernel,
        grid=grid,
        in_specs=[spec(a.shape, b, w) for a, b, w in ins],
        out_specs=[spec(s, b, w) for s, _, b, w in outs],
        out_shape=[jax.ShapeDtypeStruct(s, d) for s, d, _, _ in outs],
        scratch_shapes=list(scratch),
        input_output_aliases=aliases or {},
        compiler_params=pltpu.CompilerParams(vmem_limit_bytes=VMEM),
        cost_estimate=pl.CostEstimate(flops=flops, bytes_accessed=moved, transcendentals=0),
        name=name,
    )(*[a for a, _, _ in ins])


def scr(shape, dtype):
    return pltpu.VMEM(shape, dtype)


def in_kernel(x_ref, vec_ref, bias_ref, w_ref, inner_ref, act_ref, act_t_ref, unit_t_ref, unit):
    @pl.when(pl.program_id(0) == 0)
    def _():
        for rows in cuts(x_ref.shape[0]):
            n, _ = normal(x_ref[rows, :].astype(F32))
            u = (n * vec_ref[0:1, :] + vec_ref[1:2, :]).astype(BF)
            unit[rows, :] = u
            unit_t_ref[:, rows] = u.T

    w = flat(w_ref)
    for rows in cuts(x_ref.shape[0]):
        s = dot(unit[rows, :], w, 1, 0) + bias_ref[0]
        inner_ref[rows, :] = s.astype(BF)
        a = (s * jax.nn.sigmoid(s)).astype(BF)
        act_ref[rows, :] = a
        act_t_ref[:, rows] = a.T


def ffn_in_forward(x, vec, bias, w, unit0):
    t, d = x.shape
    n, _, r, _ = w.shape
    k = bias.shape[0] // d
    bias = bias.reshape(k, 1, d)
    return call(
        in_kernel,
        (k,),
        [
            (x, None, None),
            (vec, None, None),
            (bias, (1, 1, d), lambda j: (j, 0, 0)),
            (w, (n, 1, r, d), lambda j: (0, unit0 + j, 0, 0)),
        ],
        [
            ((t, k * d), BF, (t, d), lambda j: (0, j)),
            ((t, k * d), BF, (t, d), lambda j: (0, j)),
            ((k * d, t), BF, (d, t), lambda j: (j, 0)),
            ((d, t), BF, None, None),
        ],
        [scr((t, d), BF)],
        name="ffn_in",
        flops=2 * t * d * d * k,
        moved=2 * d * d * k + 6 * t * d * k,
    )


def out_qkv_kernel(odd_ref, x_ref, act_ref, w_out_ref, w_qkv_ref, vec_ref, first_ref, unit_t_ref, mine_ref, other_ref, unit, acc):
    s = pl.program_id(0)
    t = x_ref.shape[0]

    @pl.when(s < 4)
    def _():
        w = flat(w_out_ref)
        for rows in cuts(t):
            p = dot(act_ref[rows, :], w, 1, 0)
            acc[rows, :] = p + jnp.where(s == 0, 0.0, acc[rows, :])

    @pl.when(s == 3)
    def _():
        for rows in cuts(t):
            first = x_ref[rows, :].astype(F32) + HALF * (acc[rows, :] + vec_ref[0:1, :])
            first_ref[rows, :] = first
            n, _ = normal(first)
            u = (n * vec_ref[1:2, :] + vec_ref[2:3, :]).astype(BF)
            unit[rows, :] = u
            unit_t_ref[:, rows] = u.T

    @pl.when(s >= 4)
    def _():
        w = flat(w_qkv_ref)
        odd = odd_ref[0] == 1
        half = w.shape[1] // 2
        scale = jnp.where(s == 4, HEAD_DIM**-0.5, 1.0)
        b = jnp.where(s == 4, vec_ref[3:4, :], jnp.where(s == 6, vec_ref[4:5, :], 0.0))
        for rows in cuts(t):
            y = (dot(unit[rows, :], w, 1, 0) + b) * scale
            low, high = y[:, :half], y[:, half:]
            mine = jnp.where(odd, high, low).astype(BF)
            other = jnp.where(odd, low, high).astype(BF)
            for part in range(half // 128):
                cols = slice(part * 128, part * 128 + 128)
                mine_ref[part, 0, rows, :] = mine[:, cols]
                other_ref[part, 0, rows, :] = other[:, cols]


def out_qkv_forward(odd, x, act, w, vec):
    t, d = x.shape
    n, _, r, _ = w.shape
    return call(
        out_qkv_kernel,
        (7,),
        [
            (odd, "smem", None),
            (x, None, None),
            (act, (t, d), lambda s: (0, jnp.minimum(s, 3))),
            (w, (n // 4, 4, r, d), lambda s: (jnp.minimum(s, 3), 0, 0, 0)),
            (w, (n, 1, r, d), lambda s: (0, jnp.maximum(s, 4), 0, 0)),
            (vec, None, None),
        ],
        [
            ((t, d), F32, None, None),
            ((d, t), BF, None, None),
            ((d // 256, 3, t, 128), BF, (d // 256, 1, t, 128), lambda s: (0, jnp.maximum(s - 4, 0), 0, 0)),
            ((d // 256, 3, t, 128), BF, (d // 256, 1, t, 128), lambda s: (0, jnp.maximum(s - 4, 0), 0, 0)),
        ],
        [scr((t, d), BF), scr((t, d), F32)],
        name="out_qkv",
        flops=14 * t * d * d,
        moved=14 * d * d + 20 * t * d,
    )


def mid_kernel(first_ref, mixed_ref, w_attn_ref, w_in_ref, vec_ref, second_ref, mixed_t_ref, unit_t_ref, val_ref, sig_ref, gated_ref, unit, val):
    s = pl.program_id(0)
    t = first_ref.shape[0]

    @pl.when(s == 0)
    def _():
        w = flat(w_attn_ref)
        for rows in cuts(t):
            m = mixed_ref[rows, :]
            mixed_t_ref[:, rows] = m.T
            second = first_ref[rows, :] + dot(m, w, 1, 0) + vec_ref[0:1, :]
            second_ref[rows, :] = second
            n, _ = normal(second)
            u = (n * vec_ref[1:2, :] + vec_ref[2:3, :]).astype(BF)
            unit[rows, :] = u
            unit_t_ref[:, rows] = u.T

    @pl.when(s == 1)
    def _():
        w = flat(w_in_ref)
        for rows in cuts(t):
            v = dot(unit[rows, :], w, 1, 0) + vec_ref[3:4, :]
            val[rows, :] = v
            val_ref[rows, :] = v.astype(BF)

    @pl.when(s == 2)
    def _():
        w = flat(w_in_ref)
        for rows in cuts(t):
            g = jax.nn.sigmoid(dot(unit[rows, :], w, 1, 0) + vec_ref[4:5, :])
            sig_ref[rows, :] = g.astype(BF)
            gated_ref[rows, :] = (val[rows, :] * g).astype(BF)


def mid_forward(first, mixed, w, u_attn, u_in, vec):
    t, d = first.shape
    n, _, r, _ = w.shape
    return call(
        mid_kernel,
        (3,),
        [
            (first, None, None),
            (mixed, None, None),
            (w, (n, 1, r, d), lambda s: (0, u_attn, 0, 0)),
            (w, (n, 1, r, d), lambda s: (0, u_in + jnp.maximum(s - 1, 0), 0, 0)),
            (vec, None, None),
        ],
        [((t, d), F32, None, None), ((d, t), BF, None, None), ((d, t), BF, None, None)]
        + [((t, d), BF, None, None)] * 3,
        [scr((t, d), BF), scr((t, d), F32)],
        name="mid",
        flops=6 * t * d * d,
        moved=6 * d * d + 20 * t * d,
    )


ROWS = 32
COLS = 256


def shifted(window, b):
    return window if b == 0 else pltpu.roll(window, window.shape[0] - b, 0)


def fir(pad, taps, offset, count, width, start, write, turned=False):
    reach = taps.shape[0]
    for c in range(0, width, COLS):
        cols = slice(c, c + COLS)

        def body(i, _):
            base = pl.multiple_of(i * ROWS, ROWS)
            window = pad[pl.ds(base, ROWS + 32), cols]
            acc = start(cols)
            for b in range(8):
                sh = shifted(window, b)
                for a in range(0, 5):
                    m = 8 * a + b - offset
                    if 0 <= m < reach:
                        tap = reach - 1 - m if turned else m
                        acc = acc + taps[tap : tap + 1, cols] * sh[8 * a : 8 * a + ROWS]
            write(pl.ds(base, ROWS), cols, acc)
            return 0

        lax.fori_loop(0, count // ROWS, body, 0)


def conv_kernel(gated_ref, halo_ref, taps_ref, vec_ref, second_ref, w_ref, conv_ref, act_t_ref, third_ref, pad):
    t, d = gated_ref.shape
    pad[0:32, :] = halo_ref[...].astype(F32)
    for rows in cuts(t):
        pad[pl.ds(rows.start + 32, CUT), :] = gated_ref[rows, :].astype(F32)

    def write(rows, cols, acc):
        conv_ref[rows, cols] = acc

    fir(pad, taps_ref, 2, t, d, lambda cols: jnp.broadcast_to(vec_ref[0:1, cols], (ROWS, COLS)), write)
    w = flat(w_ref)
    for rows in cuts(t):
        n, _ = normal(conv_ref[rows, :])
        u = n * vec_ref[1:2, :] + vec_ref[2:3, :]
        a = (u * jax.nn.sigmoid(u)).astype(BF)
        act_t_ref[:, rows] = a.T
        third_ref[rows, :] = second_ref[rows, :] + dot(a, w, 1, 0) + vec_ref[3:4, :]


def conv_forward(gated, halo, taps, vec, second, w, unit0):
    t, d = gated.shape
    n, _, r, _ = w.shape
    return call(
        conv_kernel,
        (1,),
        [
            (gated, None, None),
            (halo, None, None),
            (taps, None, None),
            (vec, None, None),
            (second, None, None),
            (w, (n, 1, r, d), lambda s: (0, unit0, 0, 0)),
        ],
        [((t, d), F32, None, None), ((d, t), BF, None, None), ((t, d), F32, None, None)],
        [scr((t + 32, d), F32)],
        name="conv",
        flops=2 * t * d * d,
        moved=2 * d * d + 16 * t * d,
    )


def out_last_kernel(x_ref, act_ref, w_ref, cot_ref, vec_ref, out_ref, d_ref, sums_ref, acc):
    s = pl.program_id(0)
    t = x_ref.shape[0]
    w = flat(w_ref)
    for rows in cuts(t):
        p = dot(act_ref[rows, :], w, 1, 0)
        acc[rows, :] = p + jnp.where(s == 0, 0.0, acc[rows, :])

    @pl.when(s == 3)
    def _():
        sums_ref[...] = jnp.zeros_like(sums_ref)
        for rows in cuts(t):
            fourth = x_ref[rows, :] + HALF * (acc[rows, :] + vec_ref[0:1, :])
            n, r = normal(fourth)
            out_ref[rows, :] = (n * vec_ref[1:2, :] + vec_ref[2:3, :]).astype(BF)
            dy = cot_ref[rows, :].astype(F32)
            d_ref[rows, :] = normal_back(dy, n, r, vec_ref[1:2, :])
            sums_ref[0:1, :] += total(dy * n)
            sums_ref[1:2, :] += total(dy)


def out_last(x, act, w, block0, cot, vec):
    t, d = x.shape
    n, _, r, _ = w.shape
    return call(
        out_last_kernel,
        (4,),
        [
            (x, None, None),
            (act, (t, d), lambda s: (0, s)),
            (w, (n // 4, 4, r, d), lambda s: (s, block0, 0, 0)),
            (cot, None, None),
            (vec, None, None),
        ],
        [((t, d), BF, None, None), ((t, d), F32, None, None), ((8, d), F32, None, None)],
        [scr((t, d), F32)],
        name="out_last",
        flops=8 * t * d * d,
        moved=8 * d * d + 20 * t * d,
    )


def ffn_hidden_kernel(d_ref, inner_ref, w_ref, dinner_ref, dout_ref, dbias_ref, sums_ref):
    t = d_ref.shape[0]

    @pl.when(pl.program_id(0) == 0)
    def _():
        sums_ref[...] = jnp.zeros_like(sums_ref)
        for rows in cuts(t):
            v = (HALF * d_ref[rows, :]).astype(BF)
            dout_ref[rows, :] = v
            sums_ref[0:1, :] += total(v.astype(F32))

    w = flat(w_ref)
    dbias = 0.0
    for rows in cuts(t):
        da = dot(dout_ref[rows, :], w, 1, 1)
        v = (da * silu_slope(inner_ref[rows, :].astype(F32))).astype(BF)
        dinner_ref[rows, :] = v
        dbias = dbias + total(v.astype(F32))
    dbias_ref[0] = dbias


def ffn_hidden_back(dy, inner, w, block0):
    t, d = dy.shape
    n, _, r, _ = w.shape
    k = inner.shape[1] // d
    return call(
        ffn_hidden_kernel,
        (k,),
        [
            (dy, None, None),
            (inner, (t, d), lambda j: (0, j)),
            (w, (n // 4, 4, r, d), lambda j: (j, block0, 0, 0)),
        ],
        [
            ((t, k * d), BF, (t, d), lambda j: (0, j)),
            ((t, d), BF, None, None),
            ((k, 1, d), F32, (1, 1, d), lambda j: (j, 0, 0)),
            ((8, d), F32, None, None),
        ],
        name="ffn_hidden_back",
        flops=2 * t * d * d * k,
        moved=2 * d * d * k + 4 * t * d * k,
    )


def norm_input_kernel(k, dy_ref, g_ref, x_ref, w_ref, vec_ref, d_ref, sums_ref, acc):
    s = pl.program_id(0)
    t = x_ref.shape[0]
    w = flat(w_ref)
    for rows in cuts(t):
        p = dot(g_ref[rows, :], w, 1, 1)
        acc[rows, :] = p + jnp.where(s == 0, 0.0, acc[rows, :])

    @pl.when(s == k - 1)
    def _():
        sums_ref[...] = jnp.zeros_like(sums_ref)
        for rows in cuts(t):
            n, r = normal(x_ref[rows, :].astype(F32))
            du = acc[rows, :]
            d_ref[rows, :] = (dy_ref[rows, :] + normal_back(du, n, r, vec_ref[0:1, :])).astype(d_ref.dtype)
            sums_ref[0:1, :] += total(du * n)
            sums_ref[1:2, :] += total(du)


def norm_input_back(dy, g, x, w, unit0, gain, out_type=F32):
    t, d = dy.shape
    n, _, r, _ = w.shape
    k = g.shape[1] // d
    return call(
        functools.partial(norm_input_kernel, k),
        (k,),
        [
            (dy, None, None),
            (g, (t, d), lambda j: (0, j)),
            (x, None, None),
            (w, (n, 1, r, d), lambda j: (0, unit0 + j, 0, 0)),
            (gain, None, None),
        ],
        [((t, d), out_type, None, None), ((8, d), F32, None, None)],
        [scr((t, d), F32)],
        name="norm_input_back",
        flops=2 * t * d * d * k,
        moved=2 * d * d * k + 2 * t * d * k + 12 * t * d,
    )


def weight_kernel(left_ref, right_ref, *rest):
    out_ref = rest[-1]
    rows, d = left_ref.shape[0], out_ref.shape[-1]
    a, b, r, _ = out_ref.shape
    step = max(256, 4 * r)
    for i in range(0, rows, step):
        value = dot(left_ref[i : i + step, :], right_ref[...], 1, 0).astype(BF)
        if b == 1:
            out_ref[pl.ds(i // r, step // r), 0] = value.reshape(step // r, r, d)
        else:
            out_ref[pl.ds(i // (4 * r), step // (4 * r))] = value.reshape(step // (4 * r), 4, r, d)


def weight_grad(left_t, right, n, units, at, by_rows, into=None):
    d = 1024
    t = left_t.shape[1]
    r = d // n
    if by_rows:
        k = left_t.shape[0] // d
        ins = [(left_t, (d, t), lambda j: (j, 0)), (right, None, None)]
        block, where = (n // 4, 4, r, d), lambda j: (j, at // 4, 0, 0)
    else:
        k = right.shape[1] // d
        ins = [(left_t, None, None), (right, (t, d), lambda j: (0, j))]
        block, where = (n, 1, r, d), lambda j: (0, at + j, 0, 0)
    aliases = None
    if into is not None:
        ins.append((into, "any", None))
        aliases = {2: 0}
    return call(
        weight_kernel,
        (k,),
        ins,
        [((n, units, r, d), BF, block, where)],
        name="weight_grad",
        aliases=aliases,
        flops=2 * t * d * d * k,
        moved=2 * d * d * k + 2 * t * d * (k + 1),
    )[0]


def conv_out_kernel(d_ref, conv_ref, w_ref, vec_ref, dconv_ref, dout_ref, sums_ref):
    t = d_ref.shape[0]
    sums_ref[...] = jnp.zeros_like(sums_ref)
    w = flat(w_ref)
    for rows in cuts(t):
        dout = d_ref[rows, :].astype(BF)
        dout_ref[rows, :] = dout
        da = dot(dout, w, 1, 1)
        n, r = normal(conv_ref[rows, :])
        du = da * silu_slope(n * vec_ref[0:1, :] + vec_ref[1:2, :])
        dconv = normal_back(du, n, r, vec_ref[0:1, :])
        dconv_ref[rows, :] = dconv
        sums_ref[0:1, :] += total(dout.astype(F32))
        sums_ref[1:2, :] += total(du * n)
        sums_ref[2:3, :] += total(du)
        sums_ref[3:4, :] += total(dconv)


def conv_out_back(d3, conv, w, unit0, vec):
    t, d = d3.shape
    n, _, r, _ = w.shape
    return call(
        conv_out_kernel,
        (1,),
        [
            (d3, None, None),
            (conv, None, None),
            (w, (n, 1, r, d), lambda s: (0, unit0, 0, 0)),
            (vec, None, None),
        ],
        [((t, d), F32, None, None), ((t, d), BF, None, None), ((8, d), F32, None, None)],
        name="conv_out_back",
        flops=2 * t * d * d,
        moved=2 * d * d + 16 * t * d,
    )


def mid_back_kernel(odd_ref, dconv_ref, follow_ref, taps_ref, val_ref, sig_ref, second_ref, d3_ref, w_in_ref, w_attn_ref, vec_ref, d2_ref, dout_ref, dglu_ref, mine_ref, other_ref, sums_ref, pad, acc):
    s = pl.program_id(0)
    t, d = dconv_ref.shape

    @pl.when(s == 0)
    def _():
        for rows in cuts(t):
            pad[rows, :] = dconv_ref[rows, :]
        pad[t : t + 32, :] = follow_ref[...]

        def write(rows, cols, dgated):
            sig = sig_ref[rows, cols].astype(F32)
            dval = dgated * sig
            dglu_ref[rows, cols] = dval.astype(BF)
            dgate = dval * val_ref[rows, cols].astype(F32) * (1.0 - sig)
            dglu_ref[rows, cols.start + d : cols.stop + d] = dgate.astype(BF)

        fir(pad, taps_ref, 0, t, d, lambda cols: jnp.zeros((ROWS, COLS), F32), write, turned=True)
        sums_ref[...] = jnp.zeros_like(sums_ref)
        for rows in cuts(t):
            sums_ref[0:1, :] += total(dglu_ref[rows, :d].astype(F32))
            sums_ref[1:2, :] += total(dglu_ref[rows, d:].astype(F32))
        w = flat(w_in_ref)
        for rows in cuts(t):
            acc[rows, :] = dot(dglu_ref[rows, :d], w, 1, 1)

    @pl.when(s == 1)
    def _():
        w = flat(w_in_ref)
        w_attn = flat(w_attn_ref)
        odd = odd_ref[0] == 1
        half = d // 2
        for rows in cuts(t):
            du = acc[rows, :] + dot(dglu_ref[rows, d:], w, 1, 1)
            n, r = normal(second_ref[rows, :])
            d2 = d3_ref[rows, :] + normal_back(du, n, r, vec_ref[0:1, :])
            sums_ref[2:3, :] += total(du * n)
            sums_ref[3:4, :] += total(du)
            d2_ref[rows, :] = d2
            dout = d2.astype(BF)
            dout_ref[rows, :] = dout
            sums_ref[4:5, :] += total(dout.astype(F32))
            dm = dot(dout, w_attn, 1, 1)
            low, high = dm[:, :half], dm[:, half:]
            mine = jnp.where(odd, high, low).astype(BF)
            other = jnp.where(odd, low, high).astype(BF)
            for part in range(half // 128):
                cols = slice(part * 128, part * 128 + 128)
                mine_ref[part, rows, :] = mine[:, cols]
                other_ref[part, rows, :] = other[:, cols]


def mid_back(odd, dconv, follow, taps, val, sig, second, d3, w, u_attn, u_in, gain):
    t, d = d3.shape
    n, _, r, _ = w.shape
    return call(
        mid_back_kernel,
        (2,),
        [
            (odd, "smem", None),
            (dconv, None, None),
            (follow, None, None),
            (taps, None, None),
            (val, None, None),
            (sig, None, None),
            (second, None, None),
            (d3, None, None),
            (w, (n, 1, r, d), lambda s: (0, u_in + s, 0, 0)),
            (w, (n, 1, r, d), lambda s: (0, u_attn, 0, 0)),
            (gain, None, None),
        ],
        [
            ((t, d), F32, None, None),
            ((t, d), BF, None, None),
            ((t, 2 * d), BF, None, None),
            ((d // 256, t, 128), BF, None, None),
            ((d // 256, t, 128), BF, None, None),
            ((8, d), F32, None, None),
        ],
        [scr((t + 32, d), F32), scr((t, d), F32)],
        name="mid_back",
        flops=6 * t * d * d,
        moved=6 * d * d + 24 * t * d,
    )


def taps_kernel(dconv_ref, gated_ref, halo_ref, out_ref, pad, part):
    t, d = dconv_ref.shape
    reach = out_ref.shape[0]
    pad[0:32, :] = halo_ref[...].astype(F32)
    for rows in cuts(t):
        pad[pl.ds(rows.start + 32, CUT), :] = gated_ref[rows, :].astype(F32)
    part[...] = jnp.zeros_like(part)
    for c in range(0, d, COLS):
        cols = slice(c, c + COLS)

        def body(i, _):
            base = pl.multiple_of(i * ROWS, ROWS)
            window = pad[pl.ds(base, ROWS + 32), cols]
            here = dconv_ref[pl.ds(base, ROWS), cols]
            for b in range(8):
                sh = shifted(window, b)
                for a in range(0, 5):
                    m = 8 * a + b - 2
                    if 0 <= m < reach:
                        v = here * sh[8 * a : 8 * a + ROWS]
                        v = (v[0:8] + v[8:16]) + (v[16:24] + v[24:32])
                        part[8 * m : 8 * m + 8, cols] += v
            return 0

        lax.fori_loop(0, t // ROWS, body, 0)
    for m in range(reach):
        out_ref[m : m + 1, :] = total(part[8 * m : 8 * m + 8, :])


def taps_grad(dconv, gated, halo, reach):
    t, d = dconv.shape
    return call(
        taps_kernel,
        (1,),
        [(dconv, None, None), (gated, None, None), (halo, None, None)],
        [((reach, d), F32, None, None)],
        [scr((t + 32, d), F32), scr((8 * reach, d), F32)],
        name="taps_grad",
        flops=2 * t * d * reach,
        moved=6 * t * d,
    )[0]


ORDER = [
    ("q", 0), ("q", 1), ("q", 2), ("m", 0), ("m", 1), ("in", 0), ("m", 2), ("in", 1), ("m", 3),
    ("in", 2), ("out", 0), ("in", 3), ("out", 1), ("out", 2), ("out", 3),
]
N_CHUNK = len(ORDER)
FIRST_IN = 5
LAST_IN = 11
AHEAD = 2
HELD = 6


def flipped_bit(index, mask):
    return index + mask - 2 * mask * lax.rem(lax.div(index, jnp.int32(mask)), jnp.int32(2))


def thin(count):
    return [pl.ds(i, 128) for i in range(0, count, 128)]


def last_kernel(
    gain_ref, table_ref, sums_2_ref, sums_3_ref, sums_4_ref, sums_5_ref, sums_7_ref, dbias_ref,
    d2_ref, first_ref, x_ref, dconv_ref, gated_ref, halo_ref, part_ref, dqkv_ref, unit_q_ref, act_ref, unit_ref, inner_ref, w_out_ref, w_in_ref,
    mixed_ref, dout_2_ref, unit_2_ref, dglu_ref, act_c_ref, dout_3_ref,
    out_ref, out_part_ref, small_out_ref, table_out_ref, dx_ref,
    odd, even, core, first, second, whole, near, far,
    left, right, wo, wi, inner, dout, acc,
    small_0, small_y, small_x, small_c, small_z, table_got, d0, d1, some, dconv, gated, pad, taps,
    left_sem, right_sem, wo_sem, wi_sem, inner_sem, out_sem, part_sem, some_sem, taps_sem,
    core_send, core_recv, first_send, first_recv, second_send, second_recv,
    z_send, z_recv, small_send, small_recv, table_send, table_recv, dx_send, dx_recv, dx_sem, free_sem,
):
    r, d = out_ref.shape[1:]
    n_part = part_ref.shape[0]
    t = x_ref.shape[0]
    cut = r // 2
    me = lax.axis_index("fsdp")
    place = lax.axis_index("seq")
    two, four = jnp.int32(2), jnp.int32(4)
    chip = lax.div(me, two)
    bit_c, bit_x, bit_y = lax.rem(me, two), lax.rem(chip, two), lax.div(me, four)
    middle = lax.rem(lax.div(place + 1, two), two)
    to_c = {"fsdp": flipped_bit(me, 1)}
    to_x = {"fsdp": flipped_bit(me, 2)}
    to_y = {"fsdp": flipped_bit(me, 4)}
    to_1 = {"seq": flipped_bit(place, 1)}
    to_2 = {"seq": 3 - place}

    barrier = pltpu.get_barrier_semaphore()
    for device in (to_c, to_x, to_y, to_1, to_2, {"seq": flipped_bit(place, 2)}):
        pl.semaphore_signal(barrier, inc=1, device_id=device, device_id_type=MESH)
    pl.semaphore_wait(barrier, 6)

    def send(src, dst, send_sem, recv_sem, device):
        return pltpu.make_async_remote_copy(
            src_ref=src, dst_ref=dst, send_sem=send_sem, recv_sem=recv_sem, device_id=device, device_id_type=MESH
        )

    def at_2(c):
        return lax.rem(c, two)

    def at_3(c):
        return lax.rem(c, jnp.int32(3))

    def on(c, begin, end, work):
        pl.when((c >= begin) & (c < end))(lambda: work(c))

    def factor_copies(c, name, unit):
        cols = slice(unit * d, unit * d + d)
        lefts = {"q": unit_q_ref, "in": unit_ref, "m": (mixed_ref, unit_2_ref, unit_2_ref, act_c_ref)[unit % 4]}
        rights = {
            "q": lambda: dqkv_ref.at[:, cols],
            "m": lambda: (
                dout_2_ref if unit == 0 else dout_3_ref if unit == 3 else dglu_ref.at[:, (unit - 1) * d : unit * d]
            ),
        }
        src = act_ref.at[:, unit] if name == "out" else lefts[name]
        copies = [pltpu.make_async_copy(src, left.at[at_2(c)], left_sem.at[at_2(c)])]
        if name in rights:
            copies.append(pltpu.make_async_copy(rights[name](), right.at[at_3(c)], right_sem.at[at_3(c)]))
        return copies

    def fetch(c):
        for i, (name, unit) in enumerate(ORDER):

            @pl.when(c == i)
            def _(i=i, name=name, unit=unit):
                for copy in factor_copies(c, name, unit):
                    copy.start()

    def fetched(c):
        pltpu.make_async_copy(unit_ref, left.at[at_2(c)], left_sem.at[at_2(c)]).wait()
        has_right = functools.reduce(
            jnp.logical_or, [c == i for i, (name, _) in enumerate(ORDER) if name in ("q", "m")]
        )

        @pl.when(has_right)
        def _():
            pltpu.make_async_copy(dout_2_ref, right.at[at_3(c)], right_sem.at[at_3(c)]).wait()

    def is_in(c):
        return (c >= FIRST_IN) & (c <= LAST_IN) & (at_2(c) == FIRST_IN % 2)

    def wo_copy(j):
        return pltpu.make_async_copy(w_out_ref.at[pl.ds(2 * j, 2), pl.ds(0, 4)], wo, wo_sem)

    def wi_copy(j):
        return pltpu.make_async_copy(w_in_ref.at[:, j], wi, wi_sem)

    def wq_copy(i):
        return pltpu.make_async_copy(w_out_ref.at[:, 4 + i], wi, wi_sem)

    def inner_copy(j):
        return pltpu.make_async_copy(inner_ref.at[:, pl.ds(pl.multiple_of(j * d, d), d)], inner, inner_sem)

    def x_copy():
        return pltpu.make_async_copy(x_ref, inner, inner_sem)

    row = 53

    def hidden(c):
        j = lax.div(c - FIRST_IN, two)
        wo_copy(j).wait()
        inner_copy(j).wait()
        w = wo[...].reshape(d, d)
        dbias = jnp.zeros((1, d), F32)
        for rows in thin(t):
            da = dot(dout[rows, :], w, 1, 1)
            v = (da * silu_slope(inner[rows, :].astype(F32))).astype(BF)
            right[at_3(c), rows, :] = v
            dbias = dbias + total(v.astype(F32))
        for dev in range(2):
            for q in range(4):
                cols = pl.ds(pl.multiple_of((2 * j + dev) * r, r), r)
                small_0[row + 3 + q : row + 4 + q, cols] = dbias[:, dev * 4 * r + q * r : dev * 4 * r + (q + 1) * r]

        @pl.when(j < 3)
        def _():
            wo_copy(j + 1).start()
            inner_copy(j + 1).start()

        @pl.when(j == 3)
        def _():
            x_copy().start()

    def product(c):
        for i in range(4):
            value = dot(left[at_2(c), 2 * i : 2 * i + 2].reshape(2 * r, t), right[at_3(c)], 1, 0).astype(BF)
            low, high = value[:r], value[r:]
            p = i + bit_x - 2 * bit_x * (i % 2)
            p = p + 2 * bit_y - 4 * bit_y * lax.div(p, two)
            even[at_2(c), p] = jnp.where(bit_c == 0, low, high)
            odd[at_2(c), p] = jnp.where(bit_c == 0, high, low)

    def through(c, fresh):
        wi_copy(0).wait()
        w = wi[...].reshape(d, d)
        for rows in thin(t):
            p = dot(right[at_3(c), rows, :], w, 1, 1)
            acc[rows, :] = p + jnp.where(fresh, 0.0, acc[rows, :])

    def back(c):
        j = lax.div(c - FIRST_IN, two)
        through(c, j == 0)
        pl.when(j < 3)(lambda: wi_copy(j + 1).start())

    def back_q(c):
        through(c, c == 0)
        pl.when(c < 2)(lambda: wq_copy(c + 1).start())
        pl.when(c == 2)(lambda: wi_copy(0).start())
        column = total(right[at_3(c)].astype(F32))

        @pl.when(c == 0)
        def _():
            small_0[11:12, :] = column

        @pl.when(c == 2)
        def _():
            small_0[12:13, :] = column
            middle_gradient()

    def middle_gradient():
        pltpu.make_async_copy(d2_ref, d1, some_sem).wait()
        for rows in thin(t):
            copy = pltpu.make_async_copy(first_ref.at[rows], some, some_sem)
            copy.start()
            copy.wait()
            n, scale = normal(some[...])
            du = acc[rows, :]
            value = d1[rows, :] + normal_back(du, n, scale, gain_ref[1:2, :])
            d1[rows, :] = value
            small_0[0:1, :] += total(du * n)
            small_0[5:6, :] += total(du)
            v = (HALF * value).astype(BF)
            dout[rows, :] = v
            small_0[row + 2 : row + 3, :] += total(v.astype(F32))

    def taps_copies(b):
        cols = pl.ds(pl.multiple_of(b * COLS, COLS), COLS)
        return [
            pltpu.make_async_copy(dconv_ref.at[:, cols], dconv, taps_sem.at[0]),
            pltpu.make_async_copy(halo_ref.at[:, cols], gated.at[pl.ds(0, 32)], taps_sem.at[1]),
            pltpu.make_async_copy(gated_ref.at[:, cols], gated.at[pl.ds(32, t)], taps_sem.at[2]),
        ]

    def taps_columns(b):
        for copy in taps_copies(b):
            copy.wait()
        pad[...] = gated[...].astype(F32)
        taps[...] = jnp.zeros_like(taps)
        reach = taps.shape[0] // 8

        def body(i, _):
            base = pl.multiple_of(i * ROWS, ROWS)
            window = pad[pl.ds(base, ROWS + 32), :]
            here = dconv[pl.ds(base, ROWS), :]
            for q in range(8):
                sh = shifted(window, q)
                for a in range(0, 5):
                    m = 8 * a + q - 2
                    if 0 <= m < reach:
                        v = here * sh[8 * a : 8 * a + ROWS]
                        taps[8 * m : 8 * m + 8, :] += (v[0:8] + v[8:16]) + (v[16:24] + v[24:32])
            return 0

        lax.fori_loop(0, t // ROWS, body, 0)
        cols = pl.ds(pl.multiple_of(b * COLS, COLS), COLS)
        for m in range(reach):
            small_0[18 + m : 19 + m, cols] = total(taps[8 * m : 8 * m + 8, :])

        @pl.when(b < d // COLS - 1)
        def _():
            for copy in taps_copies(b + 1):
                copy.start()

    def held_at(c):
        return lax.rem(c, jnp.int32(HELD))

    def core_copy(c):
        return send(odd.at[at_2(c)], core.at[held_at(c)], core_send.at[c], core_recv.at[c], to_c)

    def make(c):
        fetch(c + 1)
        fetched(c)

        is_out = functools.reduce(jnp.logical_or, [c == i for i, (name, _) in enumerate(ORDER) if name == "out"])

        @pl.when(is_out)
        def _():
            right[at_3(c)] = dout[...]

        pl.when(is_in(c))(lambda: hidden(c))
        product(c)
        pl.when(c >= HELD)(lambda: pl.semaphore_wait(free_sem, 1))
        core_copy(c).start()

    def make_back(c):
        pl.when(is_in(c))(lambda: back(c))
        pl.when(c < 3)(lambda: back_q(c))

    def first_copies(c):
        top, rest = pl.ds(0, cut), pl.ds(cut, cut)
        o = held_at(c)
        return [
            send(core.at[o, 1, top], first.at[o, 0, 0], first_send.at[c, 0], first_recv.at[c, 0], to_x),
            send(core.at[o, 3, top], first.at[o, 0, 1], first_send.at[c, 1], first_recv.at[c, 1], to_x),
            send(core.at[o, 2, rest], first.at[o, 1, 0], first_send.at[c, 2], first_recv.at[c, 2], to_y),
            send(core.at[o, 3, rest], first.at[o, 1, 1], first_send.at[c, 3], first_recv.at[c, 3], to_y),
        ]

    def second_copies(c):
        o = held_at(c)
        return [
            send(first.at[o, 0, 1], second.at[o, 0], second_send.at[c, 0], second_recv.at[c, 0], to_y),
            send(first.at[o, 1, 1], second.at[o, 1], second_send.at[c, 1], second_recv.at[c, 1], to_x),
        ]

    def add_core(c):
        core_copy(c).wait()
        o = held_at(c)

        def rows(i, _):
            at = pl.ds(pl.multiple_of(i * 32, 32), 32)
            for b in range(4):
                core[o, b, at] = (core[o, b, at].astype(F32) + even[at_2(c), b, at].astype(F32)).astype(BF)
            return 0

        lax.fori_loop(0, r // 32, rows, 0)
        for copy in first_copies(c):
            copy.start()

    def add_first(c):
        for copy in first_copies(c):
            copy.wait()
        o = held_at(c)

        def rows(i, _):
            at = pl.ds(pl.multiple_of(i * 32, 32), 32)
            low_at = pl.ds(pl.multiple_of(cut + i * 32, 32), 32)
            for b in range(2):
                first[o, 0, b, at] = (first[o, 0, b, at].astype(F32) + core[o, 2 * b, at].astype(F32)).astype(BF)
                first[o, 1, b, at] = (first[o, 1, b, at].astype(F32) + core[o, b, low_at].astype(F32)).astype(BF)
            return 0

        lax.fori_loop(0, cut // 32, rows, 0)

        @pl.when(c < N_CHUNK - HELD)
        def _():
            pl.semaphore_signal(free_sem, inc=1, device_id=to_c, device_id_type=MESH)

        for copy in second_copies(c):
            copy.start()

    def add_second(c):
        for copy in second_copies(c):
            copy.wait()
        o = held_at(c)
        whole[c, 0:cut] = (first[o, 0, 0].astype(F32) + second[o, 0].astype(F32)).astype(BF)
        whole[c, cut:r] = (first[o, 1, 0].astype(F32) + second[o, 1].astype(F32)).astype(BF)
        z_begin(c)

    z_begin, z_step = z_line(middle, to_1, to_2, whole, near, far, z_send, z_recv)

    def result_do(i, act):
        for is_middle, src in ((1, far), (0, near)):
            chunk = pltpu.make_async_copy(src.at[i], out_ref.at[i], out_sem.at[i])
            part = pltpu.make_async_copy(src.at[i], out_part_ref.at[i - N_CHUNK], out_sem.at[i])
            pl.when((middle == is_middle) & (i < N_CHUNK))(lambda chunk=chunk: act(chunk))
            pl.when((middle == is_middle) & (i >= N_CHUNK))(lambda part=part: act(part))

    def z_stage(i, stage):
        z_step(i, stage)
        if stage == 2:
            result_do(i, lambda copy: copy.start())

    wide = [d // 2, d // 4, d // 8]
    bits = [bit_y, bit_x, bit_c]
    held = [small_0, small_y, small_x, small_c]
    partner = [to_y, to_x, to_c, to_1, to_2]

    def columns(step, bit):
        return pl.ds(pl.multiple_of(bit * wide[step], wide[step]), wide[step])

    def small_copy(step):
        sems = (small_send.at[step], small_recv.at[step])
        if step < 3:
            return send(held[step].at[:, columns(step, 1 - bits[step])], held[step + 1], *sems, partner[step])
        if step == 3:
            return send(small_c, small_z.at[0], *sems, partner[step])
        return send(small_z.at[0], small_z.at[1], *sems, partner[step])

    def small_step(step):
        small_copy(step).wait()
        if step < 3:
            held[step + 1][...] += held[step][:, columns(step, bits[step])]
        elif step == 3:
            small_z[0] = small_z[0] + small_c[...]
        else:
            small_out_ref[...] = small_z[0] + small_z[1]
        if step < 4:
            small_copy(step + 1).start()

    def table_copy(step):
        src = table_ref if step == 0 else table_got.at[step - 1]
        return send(src, table_got.at[step], table_send.at[step], table_recv.at[step], partner[step])

    def table_step(step):
        table_copy(step).wait()
        before = table_ref[...] if step == 0 else table_got[step - 1]
        table_got[step] = table_got[step] + before
        if step < 4:
            table_copy(step + 1).start()
        else:
            table_out_ref[...] = table_got[step]

    mine, seq = lax.rem(place, two), lax.div(place, two)

    def dx_copy(h):
        return send(d0.at[pl.ds(h * (t // 2), t // 2)], dx_ref.at[seq], dx_send.at[h], dx_recv.at[seq], {"seq": 2 * mine + h})

    def dx_keep(h):
        return pltpu.make_async_copy(d0.at[pl.ds(h * (t // 2), t // 2)], dx_ref.at[seq], dx_sem)

    def dx_arrived(s):
        return send(d0.at[pl.ds(0, t // 2)], dx_ref.at[s], dx_send.at[0], dx_recv.at[s], to_1)

    def input_gradient():
        x_copy().wait()
        for rows in thin(t):
            n, scale = normal(inner[rows, :].astype(F32))
            du = acc[rows, :]
            d0[rows, :] = (d1[rows, :] + normal_back(du, n, scale, gain_ref[0:1, :])).astype(BF)
            small_0[row : row + 1, :] += total(du * n)
            small_0[row + 1 : row + 2, :] += total(du)
        for h in range(2):
            away = 2 * mine + h != place
            pl.when(away)(lambda h=h: dx_copy(h).start())
            pl.when(jnp.logical_not(away))(lambda h=h: dx_keep(h).start())
        small_copy(0).start()

    def part_copy(i):
        return pltpu.make_async_copy(part_ref.at[i], whole.at[N_CHUNK + i], part_sem.at[i])

    fetch(jnp.int32(0))
    wq_copy(0).start()
    pltpu.make_async_copy(d2_ref, d1, some_sem).start()
    for copy in taps_copies(jnp.int32(0)):
        copy.start()
    for i in range(n_part):
        part_copy(i).start()
    table_copy(0).start()
    wo_copy(0).start()
    inner_copy(0).start()
    small_0[...] = jnp.zeros_like(small_0)
    here = {1: (sums_2_ref, 2), 2: (sums_3_ref, 1), 3: (sums_4_ref, 0), 4: (sums_5_ref, 0), 6: (sums_2_ref, 3)}
    here.update({7: (sums_3_ref, 2), 8: (sums_4_ref, 1), 9: (sums_5_ref, 1), 10: (sums_7_ref, 0), 13: (sums_2_ref, 4)})
    here.update({14: (sums_2_ref, 0), 15: (sums_2_ref, 1), 16: (sums_3_ref, 3), 17: (sums_3_ref, 0)})
    for at, (ref, i) in here.items():
        small_0[at : at + 1, :] = ref[i : i + 1, :]
    for j in range(4):
        for dev in range(2):
            for q in range(4):
                cols = slice((2 * j + dev) * r, (2 * j + dev + 1) * r)
                small_0[49 + q : 50 + q, cols] = dbias_ref[j, :, (4 * dev + q) * r : (4 * dev + q + 1) * r]
    for i in range(n_part):
        part_copy(i).wait()
    for c in range(AHEAD):
        make(jnp.int32(c))

    def slot(k, _):
        on(k, 0, N_CHUNK, add_core)
        on(k - 1, 0, N_CHUNK, add_first)
        on(k - 2, 0, N_CHUNK, add_second)
        for stage in range(3):
            on(k - 3 - stage, 0, N_CHUNK, lambda c, stage=stage: z_stage(c, stage))
        on(k, 0, n_part, lambda i: z_begin(N_CHUNK + i))
        for stage in range(3):
            on(k - 1 - stage, 0, n_part, lambda i, stage=stage: z_stage(N_CHUNK + i, stage))
        make_back(k)
        on(k + AHEAD, 0, N_CHUNK, make)
        pl.when(k == LAST_IN)(input_gradient)
        on(k - 1, 0, d // COLS, taps_columns)
        for step in range(5):
            pl.when(k == step)(lambda step=step: table_step(step))
            pl.when(k == LAST_IN + 1 + step)(lambda step=step: small_step(step))
        return 0

    lax.fori_loop(0, N_CHUNK + 5, slot, 0)
    for h in range(2):
        away = 2 * mine + h != place
        pl.when(away)(lambda h=h: dx_copy(h).wait_send())
        pl.when(jnp.logical_not(away))(lambda h=h: dx_keep(h).wait())
    for s in range(2):
        from_away = 2 * s + lax.div(place, two) != place
        pl.when(from_away)(lambda s=s: dx_arrived(s).wait_recv())

    def settle(i, _):
        result_do(i, lambda copy: copy.wait())
        return 0

    lax.fori_loop(0, N_CHUNK + n_part, settle, 0)


def last_reduced(
    gain, table, sums, dbias, d2, first, tokens, dconv, gated, halo, part, dqkv, unit_q, act_t, unit_t, inner, w_out, w_in, mixed_t, dout_2, unit_2, dglu, act_c, dout_3
):
    n, _, r, d = w_in.shape
    t = tokens.shape[0]
    rows = 64
    k = N_CHUNK
    m = part.shape[0]
    z = k + m
    dma = pltpu.SemaphoreType.DMA
    anywhere = pl.BlockSpec(memory_space=pl.ANY)
    vmem = pl.BlockSpec(memory_space=pltpu.VMEM)
    return pl.pallas_call(
        last_kernel,
        in_specs=[vmem] * 8 + [anywhere] * 20,
        out_specs=[anywhere, anywhere, vmem, vmem, anywhere],
        out_shape=[
            jax.ShapeDtypeStruct((k, r, d), BF),
            jax.ShapeDtypeStruct((m, r, d), BF),
            jax.ShapeDtypeStruct((rows, d // 8), F32),
            jax.ShapeDtypeStruct(table.shape, F32),
            jax.ShapeDtypeStruct((2, t // 2, d), BF),
        ],
        scratch_shapes=[
            scr((2, 4, r, d), BF),
            scr((2, 4, r, d), BF),
            scr((HELD, 4, r, d), BF),
            scr((HELD, 2, 2, r // 2, d), BF),
            scr((HELD, 2, r // 2, d), BF),
            scr((z, r, d), BF),
            scr((z, r, d), BF),
            scr((z, r, d), BF),
            scr((2, n, r, t), BF),
            scr((3, t, d), BF),
            scr((2, 4, r, d), BF),
            scr((n, r, d), BF),
            scr((t, d), BF),
            scr((t, d), BF),
            scr((t, d), F32),
            scr((rows, d), F32),
            scr((rows, d // 2), F32),
            scr((rows, d // 4), F32),
            scr((rows, d // 8), F32),
            scr((2, rows, d // 8), F32),
            scr((5,) + table.shape, F32),
            scr((t, d), BF),
            scr((t, d), F32),
            scr((128, d), F32),
            scr((t, COLS), F32),
            scr((t + 32, COLS), BF),
            scr((t + 32, COLS), F32),
            scr((8 * 31, COLS), F32),
            dma((2,)),
            dma((3,)),
            dma,
            dma,
            dma,
            dma((z,)),
            dma((m,)),
            dma,
            dma((3,)),
            dma((k,)),
            dma((k,)),
            dma((k, 4)),
            dma((k, 4)),
            dma((k, 2)),
            dma((k, 2)),
            dma((z, 3)),
            dma((z, 3)),
            dma((5,)),
            dma((5,)),
            dma((5,)),
            dma((5,)),
            dma((2,)),
            dma((2,)),
            dma,
            pltpu.SemaphoreType.REGULAR,
        ],
        compiler_params=pltpu.CompilerParams(vmem_limit_bytes=60 << 20, collective_id=0, has_side_effects=True),
        cost_estimate=pl.CostEstimate(flops=100_000_000_000, bytes_accessed=400_000_000, transcendentals=0),
        name="last",
    )(
        gain, table, *sums, dbias, d2, first, tokens, dconv, gated, halo, part, dqkv, unit_q.reshape(n, r, t), act_t.reshape(n, 4, r, t),
        unit_t.reshape(n, r, t), inner, w_out, w_in,
        mixed_t.reshape(n, r, t), dout_2, unit_2.reshape(n, r, t), dglu, act_c.reshape(n, r, t), dout_3,
    )


PLACE = {item: i for i, item in enumerate(ORDER)}


def finish_kernel(n_tap, main, in_b, out_b, small, table, g_in, g_out, g_qkv, g_attn, g_conv_in, g_conv_out, g_taps, g_gain, g_shift, g_bias, g_table):
    d = main.shape[-1]

    def of(name, unit):
        return main[PLACE[name, unit]].astype(F32)

    for u in range(4):
        cols = slice(u * d, (u + 1) * d)
        g_in[0, :, cols] = of("in", u)
        g_in[1, :, cols] = in_b[u].astype(F32)
        g_out[0, u] = of("out", u)
        g_out[1, u] = out_b[u].astype(F32)
    for u in range(3):
        g_qkv[u] = of("q", u)
    g_attn[...] = of("m", 0)
    g_conv_in[:, :d] = of("m", 1)
    g_conv_in[:, d:] = of("m", 2)
    g_conv_out[...] = of("m", 3)
    w = g_taps.shape[1]
    early, late = 0, 22 + n_tap
    g_taps[...] = small[18 : 18 + n_tap, :]
    g_gain[0:1, :] = small[late : late + 1, :]
    g_gain[1:6, :] = small[0:5, :]
    g_shift[0:1, :] = small[late + 1 : late + 2, :]
    g_shift[1:6, :] = small[5:10, :]
    g_shift[6:7, :] = small[late + 2 : late + 3, :]
    g_shift[7:15, :] = small[10:18, :]
    for u in range(4):
        g_bias[0:1, u * w : (u + 1) * w] = small[late + 3 + u : late + 4 + u, :]
        g_bias[1:2, u * w : (u + 1) * w] = small[18 + n_tap + u : 19 + n_tap + u, :]
    k, h = g_table.shape
    g_table[...] = table[0:k, 0:h] + table[0:k, h : 2 * h]


def finished(main, in_b, out_b, small, table, n_tap, table_shape):
    k, r, d = main.shape
    w = small.shape[1]
    step = min(r, 32)

    def rows(count):
        return pl.BlockSpec((count, step, d), lambda i: (0, i, 0))

    def whole(*shape):
        return pl.BlockSpec(shape, lambda i: (0,) * len(shape))

    outs = [
        ((2, r, 4 * d), pl.BlockSpec((2, step, 4 * d), lambda i: (0, i, 0))),
        ((2, 4, r, d), pl.BlockSpec((2, 4, step, d), lambda i: (0, 0, i, 0))),
        ((3, r, d), rows(3)),
        ((r, d), pl.BlockSpec((step, d), lambda i: (i, 0))),
        ((r, 2 * d), pl.BlockSpec((step, 2 * d), lambda i: (i, 0))),
        ((r, d), pl.BlockSpec((step, d), lambda i: (i, 0))),
        ((n_tap, w), whole(n_tap, w)),
        ((6, w), whole(6, w)),
        ((15, w), whole(15, w)),
        ((2, 4 * w), whole(2, 4 * w)),
        (table_shape, whole(*table_shape)),
    ]
    return pl.pallas_call(
        functools.partial(finish_kernel, n_tap),
        grid=(r // step,),
        in_specs=[rows(k), rows(4), rows(4), whole(*small.shape), whole(*table.shape)],
        out_specs=[b for _, b in outs],
        out_shape=[jax.ShapeDtypeStruct(s, F32) for s, _ in outs],
        compiler_params=pltpu.CompilerParams(vmem_limit_bytes=VMEM),
        cost_estimate=pl.CostEstimate(flops=0, bytes_accessed=18_000_000, transcendentals=0),
        name="finish",
    )(main, in_b, out_b, small, table)


def xor_route(axis, mask):
    return [(i, i ^ mask) for i in range(lax.axis_size(axis))]


def swapped(block, axis, mask):
    return lax.ppermute(block, axis, xor_route(axis, mask))


def after(value, *marks):
    return lax.optimization_barrier((value,) + marks)[0]


def over_seq(part):
    if lax.axis_size("seq") != 4 or part.shape[1] < 64:
        return lax.psum(part, "seq")
    place = lax.axis_index("seq")
    part = part.astype(F32)
    for mask in (1, 2):
        high = (place & mask) != 0
        half = part.shape[1] // 2
        first, second = part[:, :half], part[:, half:]
        sent = jnp.where(high, first, second).astype(BF)
        part = jnp.where(high, second, first) + swapped(sent, "seq", mask).astype(F32)
    part = part.astype(BF)
    for mask in (2, 1):
        high = (place & mask) != 0
        got = swapped(part, "seq", mask)
        part = jnp.where(high, jnp.concatenate([got, part], axis=1), jnp.concatenate([part, got], axis=1))
    return part


def reduced(g):
    return over_seq(lax.psum_scatter(g, "fsdp", scatter_dimension=0, tiled=False))


def small_reduced(rows):
    k, d = rows.shape
    n = lax.axis_size("fsdp")
    me = lax.axis_index("fsdp")
    rows = lax.psum(rows, ("seq", "fsdp"))
    return lax.dynamic_slice_in_dim(rows, me * (d // n), d // n, 1)


def to_pairs(array, place):
    one, two = array[0], array[1]
    got = lax.ppermute(jnp.where(place % 2 == 0, two, one), "seq", [(0, 2), (1, 0), (2, 3), (3, 1)])
    more = lax.ppermute(jnp.where(place == 1, two, one), "seq", [(1, 2), (2, 1)])
    first = jnp.where(place == 0, one, jnp.where(place == 1, more, got))
    second = jnp.where(place < 2, got, jnp.where(place == 2, more, two))
    return jnp.concatenate([first, second], axis=0)


def from_pairs(array, place):
    half = array.shape[0] // 2
    first, second = array[:half], array[half:]
    got = lax.ppermute(jnp.where(place < 2, second, first), "seq", [(2, 0), (0, 1), (3, 2), (1, 3)])
    more = lax.ppermute(jnp.where(place == 1, first, second), "seq", [(1, 2), (2, 1)])
    one = jnp.where(place == 0, first, jnp.where(place == 2, more, got))
    two = jnp.where(place == 3, second, jnp.where(place == 1, more, got))
    return jnp.stack([one, two])


def on_device(
    inputs,
    lengths,
    ffn_in,
    ffn_in_bias,
    ffn_out,
    qkv,
    attn_out,
    conv_in,
    conv_out,
    depthwise,
    gains,
    shifts,
    distance,
    grad_out,
):
    n = lax.axis_size("fsdp")
    me = lax.axis_index("fsdp")
    place = lax.axis_index("seq")
    odd = place % 2 == 1
    odd_word = (place % 2).astype(jnp.int32).reshape(1)
    me_word = me.astype(jnp.int32).reshape(1)
    width = inputs.shape[2]
    r = width // n
    inner_width = ffn_in.shape[2]
    n_gain, n_shift, n_tap = gains.shape[0], shifts.shape[0], depthwise.shape[0]
    cubed = n == 8 and lax.axis_size("seq") == 4

    def chunks(part):
        return [part[:, i : i + width] for i in range(0, part.shape[1], width)]

    shard_a = jnp.stack(chunks(ffn_in[0]))
    shard_b = jnp.concatenate([ffn_out[0].reshape(4, r, width), qkv], axis=0)
    shard_c = jnp.stack([attn_out] + chunks(conv_in) + [conv_out])
    shard_d = jnp.concatenate([jnp.stack(chunks(ffn_in[1])), ffn_out[1].reshape(4, r, width)], axis=0)
    small = jnp.concatenate([gains, shifts, depthwise, ffn_in_bias.reshape(-1, r)], axis=0)
    small = lax.all_gather(small, "fsdp", axis=0)
    w_a = lax.all_gather(shard_a, "fsdp", axis=0)

    small = small.astype(F32)
    rows = jnp.transpose(small, (1, 0, 2))
    n_plain = n_gain + n_shift + n_tap
    gain = rows[:n_gain].reshape(n_gain, width)
    shift = rows[n_gain : n_gain + n_shift].reshape(n_shift, width)
    taps = rows[n_gain + n_shift : n_plain].reshape(n_tap, width)
    bias = small[:, n_plain:].reshape(n, 2, -1).transpose(1, 0, 2).reshape(2, inner_width)

    tokens = to_pairs(inputs, place)
    cotangent = to_pairs(grad_out, place)
    length = jnp.where(place < 2, lengths[0], lengths[1]).reshape(1)
    wide, ends = tables(distance)
    pairs = [(0, 1), (2, 3)]

    w_b = lax.all_gather(after(shard_b, w_a, small, tokens), "fsdp", axis=0)
    inner_a, act_a, act_t_a, unit_t_a = ffn_in_forward(tokens, jnp.stack([gain[0], shift[0]]), bias[0], w_a, 0)
    w_c = lax.all_gather(after(shard_c, w_b, act_a), "fsdp", axis=0)
    first, unit_t_1, mine, other = out_qkv_forward(
        odd_word, tokens, act_a, w_b, jnp.stack([shift[6], gain[1], shift[1], shift[8], shift[9]])
    )
    w_d = lax.all_gather(after(shard_d, other), "fsdp", axis=0)
    probs, heads, mixed = attend(mine, other, length, wide, ends)
    second, mixed_t, unit_t_2, val, sig, gated = mid_forward(
        first, mixed, w_c, 0, 1, jnp.stack([shift[10], gain[2], shift[2], shift[11], shift[12]])
    )
    count = gated.shape[0]
    halo = lax.ppermute(gated[count - 32 :], "seq", pairs)
    conv, act_t_c, third = conv_forward(
        gated, halo, taps, jnp.stack([shift[13], gain[3], shift[3], shift[14]]), second, w_c, 3
    )
    inner_b, act_b, act_t_b, unit_t_b = ffn_in_forward(third, jnp.stack([gain[4], shift[4]]), bias[1], w_d, 0)
    outputs, d4, sums_5 = out_last(third, act_b, w_d, 1, cotangent, jnp.stack([shift[7], gain[5], shift[5]]))
    outputs = from_pairs(outputs, place)

    dinner, dout, dbias_b, sums_7 = ffn_hidden_back(d4, inner_b, w_d, 1)
    g_out_b = weight_grad(act_t_b, dout, n, 4, 0, True)
    g_in_b = weight_grad(unit_t_b, after(dinner, g_out_b), n, 4, 0, False)
    part_out_b = lax.psum_scatter(g_out_b, "fsdp", scatter_dimension=0, tiled=False)
    part_in_b = lax.psum_scatter(g_in_b, "fsdp", scatter_dimension=0, tiled=False)
    dinner = after(dinner, g_in_b)
    d3, sums_4 = norm_input_back(d4, dinner, third, w_d, 0, gain[4:5])
    d3, outputs = lax.optimization_barrier((d3, outputs))
    dconv, dout_3, sums_3 = conv_out_back(d3, conv, w_c, 3, jnp.stack([gain[3], shift[3]]))
    follow = lax.ppermute(dconv[:32], "seq", [(j, i) for i, j in pairs])
    d2, dout_2, dglu, mine, other, sums_2 = mid_back(
        odd_word, dconv, follow, taps, val, sig, second, d3, w_c, 0, 1, gain[2:3]
    )
    if cubed:
        dqkv, dtable, share_out_b = attend_back(heads, probs, wide, mine, other, part_out_b)
    else:
        dqkv, dtable = attend_back(heads, probs, wide, mine, other)
        share_out_b, share_in_b = over_seq(part_out_b), over_seq(part_in_b)

    def biases(part):
        return part.reshape(n, 4, r).transpose(1, 0, 2).reshape(4, width)

    if cubed:
        main, share_in_b, small, table, grad_tokens = last_reduced(
            gain[0:2], dtable, (sums_2, sums_3, sums_4, sums_5, sums_7), dbias_b, d2, first, tokens, dconv, gated, halo,
            part_in_b, dqkv, unit_t_1, act_t_a, unit_t_a, inner_a, w_b, w_a,
            mixed_t, dout_2, unit_t_2, dglu, act_t_c, dout_3,
        )
    else:
        d1, sums_1 = norm_input_back(d2, dqkv, first, w_b, 4, gain[1:2])
        bias_sums = jnp.sum(dqkv.astype(F32), axis=0)
        dtaps = taps_grad(dconv, gated, halo, n_tap)
        early = jnp.concatenate(
            [
                jnp.stack([sums_1[0], sums_2[2], sums_3[1], sums_4[0], sums_5[0]]),
                jnp.stack([sums_1[1], sums_2[3], sums_3[2], sums_4[1], sums_5[1]]),
                jnp.stack(
                    [
                        sums_7[0],
                        bias_sums[:width],
                        bias_sums[2 * width :],
                        sums_2[4],
                        sums_2[0],
                        sums_2[1],
                        sums_3[3],
                        sums_3[0],
                    ]
                ),
                dtaps,
                biases(dbias_b),
            ],
            axis=0,
        )
        dinner, dout, dbias_a, sums_6 = ffn_hidden_back(d1, inner_a, w_b, 0)
        g_m = weight_grad(unit_t_2, dglu, n, 4, 1, False)
        g_m = weight_grad(mixed_t, dout_2, n, 4, 0, False, into=g_m)
        g_m = weight_grad(act_t_c, dout_3, n, 4, 3, False, into=g_m)
        shares = {
            "m": reduced(g_m),
            "q": reduced(weight_grad(unit_t_1, dqkv, n, 3, 0, False)),
            "out": reduced(weight_grad(act_t_a, dout, n, 4, 0, True)),
            "in": reduced(weight_grad(unit_t_a, dinner, n, 4, 0, False)),
        }
        main = jnp.stack([shares[name][unit] for name, unit in ORDER])
        d0, sums_0 = norm_input_back(d1, dinner, tokens, w_a, 0, gain[0:1], BF)
        grad_tokens = from_pairs(d0, place)
        late = jnp.concatenate([jnp.stack([sums_0[0], sums_0[1], sums_6[0]]), biases(dbias_a)], axis=0)
        small = small_reduced(jnp.concatenate([early, late], axis=0))
        table = lax.psum(dtable, ("seq", "fsdp"))
    g_in, g_out, g_qkv, g_attn, g_conv_in, g_conv_out, g_taps, g_gain, g_shift, g_bias, total_table = finished(
        main, share_in_b, share_out_b, small, table, n_tap, distance.shape
    )
    return (
        outputs,
        grad_tokens,
        g_in,
        g_bias,
        g_out.reshape(2, 4 * r, width),
        g_qkv,
        g_attn,
        g_conv_in,
        g_conv_out,
        g_taps,
        g_gain,
        g_shift,
        total_table,
    )


def solution(mesh):
    return jax.shard_map(
        on_device,
        mesh=mesh,
        in_specs=(
            P("fsdp", "seq", None),
            P("fsdp"),
            P(None, "fsdp", None),
            P(None, "fsdp"),
            P(None, "fsdp", None),
            P(None, "fsdp", None),
            P("fsdp", None),
            P("fsdp", None),
            P("fsdp", None),
            P(None, "fsdp"),
            P(None, "fsdp"),
            P(None, "fsdp"),
            P(),
            P("fsdp", "seq", None),
        ),
        out_specs=(
            P("fsdp", "seq", None),
            P("fsdp", "seq", None),
            P(None, "fsdp", None),
            P(None, "fsdp"),
            P(None, "fsdp", None),
            P(None, "fsdp", None),
            P("fsdp", None),
            P("fsdp", None),
            P("fsdp", None),
            P(None, "fsdp"),
            P(None, "fsdp"),
            P(None, "fsdp"),
            P(),
        ),
        check_vma=False,
    )
```

time: 1610 us -> 725 us (0.45)
  waiting for transfers between devices: 559 us -> 124 us
  Pallas kernels: 95.8 us -> 497 us
  local copies, waits for them, and re-layouts: 363 us -> 23.9 us
  other arithmetic: 241 us -> 15.1 us
  matrix products: 154 us -> 0 us
  starting transfers between devices: 150 us -> 31.7 us
    ppermute x118 -> x2, waiting for transfers between devices: 432 us -> 7.35 us  [the longest x1 6.84 us: on_device(): follow = lax.ppermute(dconv[:32], 'seq', [(j, i) for i, j in pairs])]
    pallas_call x2 -> x16, Pallas kernels: 95.8 us -> 497 us  [the longest x1 195 us: last_reduced(): pl.pallas_call(last_kernel, in_specs=[vmem] * 8 + [anywhere] * 20, out_sp...]
    dot_general x34 -> x0, matrix products: 154 us -> none  [dot(): lax.dot_general(a, b, (((ca,), (cb,)), ((), ())), preferred_element_type=...]
    ppermute x118 -> x2, starting transfers between devices: 133 us -> 5.55 us  [the longest x1 4.26 us: on_device(): halo = lax.ppermute(gated[count - 32:], 'seq', pairs)]
    psum x1 -> x0, waiting for transfers between devices: 119 us -> none  [on_device(): flat = lax.psum(flat, ('seq', 'fsdp'))]
    slice x107 -> x10, local copies, waits for them, and re-layouts: 122 us -> 5.02 us  [the longest x1 1.88 us: on_device(): ffn_out[1].reshape(4, r, width)]
    unnamed x721 -> x44, local copies, waits for them, and re-layouts: 122 us -> 10.3 us
    all_gather x0 -> x4, waiting for transfers between devices: none -> 112 us  [the longest x1 66.4 us: on_device(): w_b = lax.all_gather(after(shard_b, w_a, small, tokens), 'fsdp', axis=0)]
  transfers between devices with their start and end apart: 127 -> 14, of which waited for: 46 -> 6; matrix products, arithmetic and copies ran while one was open for 30% -> 4% of each run, Pallas kernels for 6% -> 35%
where the time goes in v2:
time: 725 us; the launch traced here: 717 us
  Pallas kernels  497 us (69%)
  waiting for transfers between devices  124 us (17%)
  starting transfers between devices  31.7 us (4%)
  local copies, waits for them, and re-layouts  23.9 us (3%)
  between operations  16.2 us (2%)
  other arithmetic  15.1 us (2%)
  blocking collectives  9.46 us (1%)
    pallas_call x1, Pallas kernels, last_reduced(): pl.pallas_call(last_kernel, in_specs=[vmem] * 8 + [anywhere] * 20, out_sp...  195 us
    pallas_call x12, Pallas kernels, call(): pl.pallas_call(kernel, grid=grid, in_specs=[spec(a.shape, b, w) for a, b,...  147 us
    pallas_call x1, Pallas kernels, attend_back(): pl.pallas_call(functools.partial(bwd_kernel, with_part), grid=(pairs, STE...  82.8 us
    all_gather x1, waiting for transfers between devices, on_device(): w_b = lax.all_gather(after(shard_b, w_a, small, tokens), 'fsdp', axis=0)  66.4 us
    pallas_call x1, Pallas kernels, attend(): pl.pallas_call(fwd_kernel, grid=(pairs, STEPS), in_specs=[pl.BlockSpec(me...  64.1 us
    all_gather x1, waiting for transfers between devices, on_device(): w_a = lax.all_gather(shard_a, 'fsdp', axis=0)  34.6 us
  transfers between devices with their start and end apart: 14, of which 6 were waited for; matrix products, arithmetic and copies ran while one was open for 4% of the time, Pallas kernels for 35%

profile of v2, /device:TPU:0, one launch (start us, length us, event | category | flops | bytes accessed | tf_op | source)
XLA Modules:
  0.0 716.9 jit_solution(5408786696816928458)
XLA Ops:
  13.1 5.0 collective-permute-start.1
  20.1 9.5 %all-gather.5 = bf16[8,60,128]{2,1,0:T(8,128)(2,1)S(1)} all-gather(bf16[1,60,128]{2,1,0:T(8,128)(2,1)S(1)} %maximum_bitcast_fusion), channel_id=2, replica_groups=mesh['seq'=4,'fsdp'=8] {'fsdp'}, dimensions={0}, use_global_device_ids=true | all-gather | bytes 138240 | tf_op jit(solution)/shard_map/all_gather | solution.py:1702
  33.4 34.6 %all-gather.11.cloned.1.call-done = bf16[32,128,1024]{2,1,0:T(8,128)(2,1)} async-done(((bf16[4,128,1024]{2,1,0:T(8,128)(2,1)}), bf16[32,128,1024]{2,1,0:T(8,128)(2,1)}) %all-gather.11.cloned.1.call-update) | async-done | bytes 8388624 | tf_op jit(solution)/shard_map/all_gather | solution.py:1703
  71.9 12.6 %ffn_in.2 = (bf16[512,4096]{1,0:T(8,128)(2,1)}, bf16[512,4096]{1,0:T(8,128)(2,1)}, bf16[4096,512]{1,0:T(8,128)(2,1)}, bf16[1024,512]{1,0:T(8,128)(2,1)}) custom-call(bf16[512,1024]{1,0:T(8,128)(2,1)} %pad_maximum_fusion.1.x_ref, f32[2,1024]{1,0:T(2,128)} %pad_maximum_fusion.9.vec_ref, f32[4,1,1024]{2,1,0:T(1,128)} %reshape_squeeze.12.bias_ref, ...), custom_call_target="tpu_custom_call" | custom-call | flops 4294967296 | bytes 20971520 | tf_op jit(solution)/shard_map/ffn_in/pallas_call | solution.py:390
  84.6 66.4 %all-gather.13.cloned.1.call-done = bf16[56,128,1024]{2,1,0:T(8,128)(2,1)} async-done(((bf16[7,128,1024]{2,1,0:T(8,128)(2,1)}), bf16[56,128,1024]{2,1,0:T(8,128)(2,1)}) %all-gather.13.cloned.1.call-update) | async-done | bytes 14680080 | tf_op jit(solution)/shard_map/all_gather | solution.py:1719
  155.7 16.9 %out_qkv.1 = (f32[512,1024]{1,0:T(8,128)}, bf16[1024,512]{1,0:T(8,128)(2,1)}, bf16[4,3,512,128]{3,2,1,0:T(8,128)(2,1)}, bf16[4,3,512,128]{3,2,1,0:T(8,128)(2,1)}) custom-call(s32[1]{0:T(128)} %bitcast.odd_ref, bf16[512,1024]{1,0:T(8,128)(2,1)} %pad_maximum_fusion.1.x_ref, bf16[512,4096]{1,0:T(8,128)(2,1)} %get-tuple-element.81.act_ref, ...), custom_call_target="tpu_custom_call" | custom-call | flops 7516192768 | bytes 25165824 | tf_op jit(solution)/shard_map/out_qkv/pallas_call | solution.py:390
  186.7 4.5 collective-permute-done.4
  192.4 64.1 %attend_fwd.1 = (bf16[8,1024,1024]{2,1,0:T(8,128)(2,1)}, bf16[4,3,1024,128]{3,2,1,0:T(8,128)(2,1)}, bf16[512,1024]{1,0:T(8,128)(2,1)}) custom-call(s32[1]{0:T(128)} %bitcast.23.len_ref, bf16[128,512]{1,0:T(8,128)(2,1)} %maximum_maximum_fusion.wide_ref, bf16[128,128]{1,0:T(8,128)(2,1)} %pad_maximum_fusion.6.ends_ref, ...), custom_call_target="tpu_custom_call" | custom-call | flops 40000000000 | bytes 120000000 | tf_op jit(solution)/shard_map/attend_fwd/pallas_call | solution.py:312
  256.5 11.0 %mid.1 = (f32[512,1024]{1,0:T(8,128)}, bf16[1024,512]{1,0:T(8,128)(2,1)}, bf16[1024,512]{1,0:T(8,128)(2,1)}, bf16[512,1024]{1,0:T(8,128)(2,1)}, bf16[512,1024]{1,0:T(8,128)(2,1)}, /*index=5*/bf16[512,1024]{1,0:T(8,128)(2,1)}) custom-call(f32[512,1024]{1,0:T(8,128)} %get-tuple-element.83.first_ref, bf16[512,1024]{1,0:T(8,128)(2,1)} %get-tuple-element.86.mixed_ref, ...), custom_call_target="tpu_custom_call" | custom-call | flops 3221225472 | bytes 16777216 | tf_op jit(solution)/shard_map/mid/pallas_call | solution.py:390
  274.8 13.9 %conv.1 = (f32[512,1024]{1,0:T(8,128)}, bf16[1024,512]{1,0:T(8,128)(2,1)}, f32[512,1024]{1,0:T(8,128)}) custom-call(bf16[512,1024]{1,0:T(8,128)(2,1)} %get-tuple-element.88.gated_ref, bf16[32,1024]{1,0:T(8,128)(2,1)} %copy-done.10, f32[31,1024]{1,0:T(8,128)} %bitcast.147, f32[4,1024]{1,0:T(4,128)} %pad_maximum_fusion.7.vec_ref, ...), custom_call_target="tpu_custom_call" | custom-call | flops 1073741824 | bytes 10485760 | tf_op jit(solution)/shard_map/conv/pallas_call | solution.py:390
  288.7 10.7 %all-gather.17.cloned.1.call-done = bf16[64,128,1024]{2,1,0:T(8,128)(2,1)} async-done(((bf16[8,128,1024]{2,1,0:T(8,128)(2,1)}), bf16[64,128,1024]{2,1,0:T(8,128)(2,1)}) %all-gather.17.cloned.1.call-update) | async-done | bytes 16777232 | tf_op jit(solution)/shard_map/all_gather | solution.py:1725
  299.5 12.5 %ffn_in.3 = (bf16[512,4096]{1,0:T(8,128)(2,1)}, bf16[512,4096]{1,0:T(8,128)(2,1)}, bf16[4096,512]{1,0:T(8,128)(2,1)}, bf16[1024,512]{1,0:T(8,128)(2,1)}) custom-call(f32[512,1024]{1,0:T(8,128)} %get-tuple-element.90.x_ref, f32[2,1024]{1,0:T(2,128)} %pad_maximum_fusion.10.vec_ref, f32[4,1,1024]{2,1,0:T(1,128)} %reshape_squeeze.14.bias_ref, ...), custom_call_target="tpu_custom_call" | custom-call | flops 4294967296 | bytes 20971520 | tf_op jit(solution)/shard_map/ffn_in/pallas_call | solution.py:390
  312.0 12.3 %out_last.1 = (bf16[512,1024]{1,0:T(8,128)(2,1)}, f32[512,1024]{1,0:T(8,128)}, f32[8,1024]{1,0:T(8,128)}) custom-call(f32[512,1024]{1,0:T(8,128)} %get-tuple-element.90.x_ref, bf16[512,4096]{1,0:T(8,128)(2,1)} %get-tuple-element.92.act_ref, bf16[8,8,128,1024]{3,2,1,0:T(8,128)(2,1)} %bitcast.139, bf16[512,1024]{1,0:T(8,128)(2,1)} %pad_maximum_fusion.4.cot_ref, ...), custom_call_target="tpu_custom_call" | custom-call | flops 4294967296 | bytes 18874368 | tf_op jit(solution)/shard_map/out_last/pallas_call | solution.py:390
  324.2 11.4 %ffn_hidden_back.1 = (bf16[512,4096]{1,0:T(8,128)(2,1)}, bf16[512,1024]{1,0:T(8,128)(2,1)}, f32[4,1,1024]{2,1,0:T(1,128)}, f32[8,1024]{1,0:T(8,128)}) custom-call(f32[512,1024]{1,0:T(8,128)} %get-tuple-element.93.d_ref.dy_ref, bf16[512,4096]{1,0:T(8,128)(2,1)} %get-tuple-element.94.inner_ref, bf16[8,8,128,1024]{3,2,1,0:T(8,128)(2,1)} %bitcast.140), custom_call_target="tpu_custom_call" | custom-call | flops 4294967296 | bytes 16777216 | tf_op jit(solution)/shard_map/ffn_hidden_back/pallas_call | solution.py:390
  335.6 8.7 %weight_grad.2 = bf16[8,4,128,1024]{3,2,1,0:T(8,128)(2,1)} custom-call(bf16[4096,512]{1,0:T(8,128)(2,1)} %get-tuple-element.97.left_ref, bf16[512,1024]{1,0:T(8,128)(2,1)} %get-tuple-element.98.right_ref), custom_call_target="tpu_custom_call" | custom-call | flops 4294967296 | bytes 13631488 | tf_op jit(solution)/shard_map/weight_grad/pallas_call | solution.py:390
  344.4 8.8 %weight_grad.3 = bf16[8,4,128,1024]{3,2,1,0:T(8,128)(2,1)} custom-call(bf16[1024,512]{1,0:T(8,128)(2,1)} %get-tuple-element.96.left_ref, bf16[512,4096]{1,0:T(8,128)(2,1)} %get-tuple-element.100.right_ref.g_ref), custom_call_target="tpu_custom_call" | custom-call | flops 4294967296 | bytes 13631488 | tf_op jit(solution)/shard_map/weight_grad/pallas_call | solution.py:390
  356.3 12.9 %collective-permute-start.5 = (bf16[256,1024]{1,0:T(8,128)(2,1)S(1)}, bf16[256,1024]{1,0:T(8,128)(2,1)S(1)}, u32[]{:S(2)}, u32[]{:S(2)}) collective-permute-start(bf16[256,1024]{1,0:T(8,128)(2,1)S(1)} %get-tuple-element.201), channel_id=1, source_target_pairs={{8,16},{16,8},{9,17},{17,9},{10,18},{18,10},{11,19},{19,11},{12,20... | collective-permute-start | bytes 1572872 | tf_op jit(solution)/shard_map/ppermute | solution.py:1660
  371.1 12.0 %norm_input_back.1 = (f32[512,1024]{1,0:T(8,128)}, f32[8,1024]{1,0:T(8,128)}) custom-call(f32[512,1024]{1,0:T(8,128)} %get-tuple-element.93.d_ref.dy_ref, bf16[512,4096]{1,0:T(8,128)(2,1)} %get-tuple-element.100.right_ref.g_ref, f32[512,1024]{1,0:T(8,128)} %get-tuple-element.90.x_ref, bf16[8,8,128,1024]{3,2,1,0:T(8,128)(2,1)} %bitcast.141, f32[1,1024]{1,0:T(1,128)} %copy-done.12), custom_call_target="tpu_custom_call" | custom-call | flops 4294967296 | bytes 18874368 | tf_op jit(solution)/shard_map/norm_input_back/pallas_call | solution.py:390
  384.4 6.9 conv_out_back.1
  394.1 6.8 collective-permute-done.7.follow_ref
  401.6 20.0 %mid_back.1 = (f32[512,1024]{1,0:T(8,128)}, bf16[512,1024]{1,0:T(8,128)(2,1)}, bf16[512,2048]{1,0:T(8,128)(2,1)}, bf16[4,512,128]{2,1,0:T(8,128)(2,1)}, bf16[4,512,128]{2,1,0:T(8,128)(2,1)}, /*index=5*/f32[8,1024]{1,0:T(8,128)}) custom-call(s32[1]{0:T(128)} %bitcast.odd_ref, f32[512,1024]{1,0:T(8,128)} %get-tuple-element.108.dconv_ref, ...), custom_call_target="tpu_custom_call" | custom-call | flops 3221225472 | bytes 18874368 | tf_op jit(solution)/shard_map/mid_back/pallas_call | solution.py:390
  421.6 82.8 %attend_bwd.1 = (bf16[512,3072]{1,0:T(8,128)(2,1)}, f32[128,128]{1,0:T(8,128)}, bf16[4,128,1024]{2,1,0:T(8,128)(2,1)}) custom-call(bf16[4,3,1024,128]{3,2,1,0:T(8,128)(2,1)} %get-tuple-element.104.heads_ref, bf16[8,1024,1024]{2,1,0:T(8,128)(2,1)} %get-tuple-element.105.p_ref, bf16[128,128]{1,0:T(8,128)(2,1)} %slice.370.wide_ref, ...), custom_call_target="tpu_custom_call" | custom-call | flops 49999998976 | bytes 150000000 | tf_op jit(solution)/shard_map/attend_bwd/pallas_call | solution.py:331
  504.5 194.9 %last.1 = (bf16[15,128,1024]{2,1,0:T(8,128)(2,1)}, bf16[4,128,1024]{2,1,0:T(8,128)(2,1)}, f32[64,128]{1,0:T(8,128)}, f32[128,128]{1,0:T(8,128)}, bf16[2,256,1024]{2,1,0:T(8,128)(2,1)}) custom-call(f32[2,1024]{1,0:T(2,128)} %slice_bitcast_fusion.12.gain_ref, f32[128,128]{1,0:T(8,128)} %get-tuple-element.113.table_ref, ...), custom_call_target="tpu_custom_call" | custom-call | flops 99999997952 | bytes 400000000 | tf_op jit(solution)/shard_map/last/pallas_call | solution.py:1455
  699.5 7.7 %finish.1 = (f32[2,128,4096]{2,1,0:T(8,128)}, f32[2,4,128,1024]{3,2,1,0:T(8,128)}, f32[3,128,1024]{2,1,0:T(8,128)}, f32[128,1024]{1,0:T(8,128)}, f32[128,2048]{1...) custom-call(bf16[15,128,1024]{2,1,0:T(8,128)(2,1)} %get-tuple-elemen, ...), custom_call_target="tpu_custom_call" | custom-call | bytes 18000000 | tf_op jit(solution)/shard_map/finish/pallas_call | solution.py:1592
  (120 shorter events, 53.5 us)
Async XLA Ops:
  7.2 60.8 %all-gather.11.cloned.1.call-start = ((), (), s32[]{:S(2)}) async-start(), calls=%async_computation.4 | async-start | bytes 9437184 | tf_op jit(solution)/shard_map/all_gather | solution.py:1703
  10.1 8.0 %copy-start.16 = (bf16[2,512]{1,0:T(2,128)(2,1)S(1)}, bf16[2,512]{1,0:T(2,128)(2,1)}, u32[]{:S(2)}) copy-start(bf16[2,512]{1,0:T(2,128)(2,1)} %param.17) | copy-start | bytes 6148
  10.1 140.8 %all-gather.13.cloned.1.call-start = ((), (), s32[]{:S(2)}) async-start(), calls=%async_computation.5 | async-start | bytes 16515072 | tf_op jit(solution)/shard_map/all_gather | solution.py:1719
  11.6 19.4 %collective-permute-start = (bf16[256,1024]{1,0:T(8,128)(2,1)}, bf16[256,1024]{1,0:T(8,128)(2,1)}, u32[]{:S(2)}, u32[]{:S(2)}) collective-permute-start(bf16[256,1024]{1,0:T(8,128)(2,1)} %get-tuple-element.208), channel_id=1, source_target_pairs={{8,16},{16,8},{9,17},{17,9},{10,18},{18,10},{11,19},{19,11},{12,20... | collective-permute-start | bytes 1572872 | tf_op jit(solution)/shard_map/ppermute | solution.py:1650
  13.1 17.9 %collective-permute-start.1 = (bf16[256,1024]{1,0:T(8,128)(2,1)}, bf16[256,1024]{1,0:T(8,128)(2,1)}, u32[]{:S(2)}, u32[]{:S(2)}) collective-permute-start(bf16[256,1024]{1,0:T(8,128)(2,1)} %get-tuple-element.209), channel_id=1, source_target_pairs={{0,16},{8,0},{16,24},{24,8},{1,17},{9,1},{17,25},{25,9},{2,18},{10... | collective-permute-start | bytes 1572872 | tf_op jit(solution)/shard_map/ppermute | solution.py:1649
  18.1 11.4 %copy-start.4 = (bf16[3,128,1024]{2,1,0:T(8,128)(2,1)S(1)}, bf16[3,128,1024]{2,1,0:T(8,128)(2,1)}, u32[]{:S(2)}) copy-start(bf16[3,128,1024]{2,1,0:T(8,128)(2,1)} %param.19) | copy-start | bytes 2359300
  32.3 38.4 %copy-start.5 = (bf16[128,2048]{1,0:T(8,128)(2,1)S(1)}, bf16[128,2048]{1,0:T(8,128)(2,1)}, u32[]{:S(2)}) copy-start(bf16[128,2048]{1,0:T(8,128)(2,1)} %param.21) | copy-start | bytes 1572868
  33.4 37.4 %copy-start.6 = (bf16[128,1024]{1,0:T(8,128)(2,1)S(1)}, bf16[128,1024]{1,0:T(8,128)(2,1)}, u32[]{:S(2)}) copy-start(bf16[128,1024]{1,0:T(8,128)(2,1)} %param.22) | copy-start | bytes 786436
  33.4 37.4 %copy-start.7 = (bf16[128,1024]{1,0:T(8,128)(2,1)S(1)}, bf16[128,1024]{1,0:T(8,128)(2,1)}, u32[]{:S(2)}) copy-start(bf16[128,1024]{1,0:T(8,128)(2,1)} %param.20) | copy-start | bytes 786436
  68.0 188.4 %all-gather.15.cloned.1.call-start = ((), (), s32[]{:S(2)}) async-start(), calls=%async_computation.6 | async-start | bytes 9437184 | tf_op jit(solution)/shard_map/all_gather | solution.py:1721
  151.0 148.5 %all-gather.17.cloned.1.call-start = ((), (), s32[]{:S(2)}) async-start(), calls=%async_computation.7 | async-start | bytes 18874368 | tf_op jit(solution)/shard_map/all_gather | solution.py:1725
  151.1 31.6 %copy-start.11 = (f32[1,1024]{1,0:T(1,128)}, f32[1,1024]{1,0:T(1,128)S(1)}, u32[]{:S(2)}) copy-start(f32[1,1024]{1,0:T(1,128)S(1)} %get-tuple-element.224.vec_ref) | copy-start | bytes 12292
  151.1 32.3 %copy-start.12 = (f32[1,1024]{1,0:T(1,128)}, f32[1,1024]{1,0:T(1,128)S(1)}, u32[]{:S(2)}) copy-start(f32[1,1024]{1,0:T(1,128)S(1)} %get-tuple-element.216.vec_ref) | copy-start | bytes 12292
  172.6 7.8 %copy-start.17 = (s32[2]{0:T(128)S(1)}, s32[2]{0:T(128)}, u32[]{:S(2)}) copy-start(s32[2]{0:T(128)} %param.15) | copy-start | bytes 28
  172.7 9.7 %copy-start.8 = (bf16[73,64]{0,1:T(8,128)(2,1)S(1)}, bf16[73,64]{0,1:T(8,128)(2,1)}, u32[]{:S(2)}) copy-start(bf16[73,64]{0,1:T(8,128)(2,1)} %param.26) | copy-start | bytes 28036
  172.7 248.9 %reduce-scatter.3.cloned.1.call-start = ((), (), s32[]{:S(2)}) async-start(), calls=%async_computation.2 | async-start | bytes 9437184 | tf_op jit(solution)/shard_map/reduce_scatter | solution.py:1742
  173.9 12.8 %collective-permute-start.3 = (bf16[256,1024]{1,0:T(8,128)(2,1)S(1)}, bf16[256,1024]{1,0:T(8,128)(2,1)S(1)}, u32[]{:S(2)}, u32[]{:S(2)}) collective-permute-start(bf16[256,1024]{1,0:T(8,128)(2,1)S(1)} %get-tuple-element.202), channel_id=1, source_target_pairs={{8,16},{16,8},{9,17},{17,9},{10,18},{18,10},{11,19},{19,11},{12,20... | collective-permute-start | bytes 1572872 | tf_op jit(solution)/shard_map/ppermute | solution.py:1650
  174.6 16.6 %collective-permute-start.4 = (bf16[256,1024]{1,0:T(8,128)(2,1)S(1)}, bf16[256,1024]{1,0:T(8,128)(2,1)}, u32[]{:S(2)}, u32[]{:S(2)}) collective-permute-start(bf16[256,1024]{1,0:T(8,128)(2,1)S(1)} %get-tuple-element.203), channel_id=1, source_target_pairs={{0,16},{8,0},{16,24},{24,8},{1,17},{9,1},{17,25},{25,9},{2,18},{10... | collective-permute-start | bytes 1572872 | tf_op jit(solution)/shard_map/ppermute | solution.py:1649
  268.3 5.8 collective-permute-start.2
  344.4 160.1 %reduce-scatter.5.cloned.1.call-start = ((), (), s32[]{:S(2)}) async-start(), calls=%async_computation.3 | async-start | bytes 9437184 | tf_op jit(solution)/shard_map/reduce_scatter | solution.py:1743
  354.8 28.4 %collective-permute-start.6 = (bf16[256,1024]{1,0:T(8,128)(2,1)S(1)}, bf16[256,1024]{1,0:T(8,128)(2,1)S(1)}, u32[]{:S(2)}, u32[]{:S(2)}) collective-permute-start(bf16[256,1024]{1,0:T(8,128)(2,1)S(1)} %get-tuple-element.200), channel_id=1, source_target_pairs={{16,0},{0,8},{24,16},{8,24},{17,1},{1,9},{25,17},{9,25},{18,2},{2,... | collective-permute-start | bytes 1572872 | tf_op jit(solution)/shard_map/ppermute | solution.py:1659
  356.3 26.9 %collective-permute-start.5 = (bf16[256,1024]{1,0:T(8,128)(2,1)S(1)}, bf16[256,1024]{1,0:T(8,128)(2,1)S(1)}, u32[]{:S(2)}, u32[]{:S(2)}) collective-permute-start(bf16[256,1024]{1,0:T(8,128)(2,1)S(1)} %get-tuple-element.201), channel_id=1, source_target_pairs={{8,16},{16,8},{9,17},{17,9},{10,18},{18,10},{11,19},{19,11},{12,20... | collective-permute-start | bytes 1572872 | tf_op jit(solution)/shard_map/ppermute | solution.py:1660
  392.2 8.7 %collective-permute-start.7 = (f32[32,1024]{1,0:T(8,128)S(1)}, f32[32,1024]{1,0:T(8,128)S(1)}, u32[]{:S(2)}, u32[]{:S(2)}) collective-permute-start(f32[32,1024]{1,0:T(8,128)S(1)} %slice.333), channel_id=1, source_target_pairs={{8,0},{24,16},{9,1},{25,17},{10,2},{26,18},{11,3},{27,19},{12,4},{... | collective-permute-start | bytes 393224 | tf_op jit(solution)/shard_map/ppermute | solution.py:1748
  699.5 9.2 %copy-start.3 = (bf16[2,256,1024]{2,1,0:T(8,128)(2,1)S(1)}, bf16[2,256,1024]{2,1,0:T(8,128)(2,1)}, u32[]{:S(2)}) copy-start(bf16[2,256,1024]{2,1,0:T(8,128)(2,1)} %get-tuple-element.257) | copy-start | bytes 3145732
  (8 other events, 11.3 us)
Sparse Core Ops, SparseCore 0:
  10.5 57.5 all-gather.10
  69.9 80.9 all-gather.12
  153.4 54.3 all-gather.14
  209.6 89.8 all-gather.16
  344.5 71.2 reduce-scatter.2
  419.5 71.2 reduce-scatter.4

commit v3 on v2

--- a/solution.py
+++ b/solution.py
@@ -978,6 +978,240 @@
     )[0]
 
 
+def flipped_bit(index, mask):
+    return index + mask - 2 * mask * lax.rem(lax.div(index, jnp.int32(mask)), jnp.int32(2))
+
+
+def first_kernel(
+    x_ref, w_ref, gains_ref, shifts_ref, taps_ref, bias_ref,
+    inner_ref, act_ref, act_t_ref, unit_t_ref, tokens_ref, small_out_ref, w_out_ref,
+    w, small, small_ref, tokens, unit, vec,
+    own_send, own_recv, far_send, far_recv, core_send, core_recv, x_send, x_recv, x_load, w_leave,
+):
+    j = pl.program_id(0)
+    n, k, r, d = w.shape
+    t = tokens.shape[0]
+    cut, thin_cut = r // 2, small.shape[1] // 2
+    me, place = lax.axis_index("fsdp"), lax.axis_index("seq")
+    two = jnp.int32(2)
+    other_x, other_y, other_c = flipped_bit(me, 2), flipped_bit(me, 4), flipped_bit(me, 1)
+    other_xy = flipped_bit(other_x, 4)
+    to_x, to_y, to_c = {"fsdp": other_x}, {"fsdp": other_y}, {"fsdp": other_c}
+
+    def send(src, dst, send_sem, recv_sem, device):
+        return pltpu.make_async_remote_copy(
+            src_ref=src, dst_ref=dst, send_sem=send_sem, recv_sem=recv_sem, device_id=device, device_id_type=MESH
+        )
+
+    def held(dev, u, rows=None):
+        if u == k:
+            return small.at[dev] if rows is None else small.at[dev, rows]
+        return w.at[dev, u] if rows is None else w.at[dev, u, rows]
+
+    def own(u):
+        return small_ref if u == k else w_ref.at[u]
+
+    def own_copies(u):
+        return [
+            send(own(u), held(me, u), own_send.at[i, u], own_recv.at[i, u], device)
+            for i, device in enumerate((to_x, to_y, to_c))
+        ]
+
+    def keep_copy(u):
+        return pltpu.make_async_copy(own(u), held(me, u), x_load.at[2 + u])
+
+    def far_copies(u):
+        half = thin_cut if u == k else cut
+        top, low = pl.ds(0, half), pl.ds(half, half)
+        return [
+            send(held(other_x, u, top), held(other_x, u, top), far_send.at[0, u], far_recv.at[0, u], to_y),
+            send(held(other_y, u, low), held(other_y, u, low), far_send.at[1, u], far_recv.at[1, u], to_x),
+        ]
+
+    def core_copy(i, u):
+        dev = (other_x, other_y, other_xy)[i]
+        return send(held(dev, u), held(dev, u), core_send.at[i, u], core_recv.at[i, u], to_c)
+
+    def gather_begin(u):
+        keep_copy(u).start()
+        for copy in own_copies(u):
+            copy.start()
+
+    def gather_forward(u):
+        across = own_copies(u)
+        far = far_copies(u)
+        across[0].wait_recv()
+        far[0].start()
+        core_copy(0, u).start()
+        across[1].wait_recv()
+        far[1].start()
+        core_copy(1, u).start()
+
+    def gather_far(u):
+        for copy in far_copies(u):
+            copy.wait_recv()
+        core_copy(2, u).start()
+
+    def gather_end(u):
+        keep_copy(u).wait()
+        own_copies(u)[2].wait_recv()
+        for i in range(3):
+            core_copy(i, u).wait_recv()
+
+    def gather_sent(u):
+        for copy in own_copies(u) + far_copies(u) + [core_copy(i, u) for i in range(3)]:
+            copy.wait_send()
+
+    side, half_of = lax.div(place, two), lax.rem(place, two)
+
+    def token_rows(h):
+        return pl.ds(pl.multiple_of(h * (t // 2), t // 2), t // 2)
+
+    def token_copy(s):
+        return send(x_ref.at[s], tokens.at[token_rows(half_of)], x_send.at[s], x_recv.at[half_of], {"seq": 2 * s + side})
+
+    def token_keep(s):
+        return pltpu.make_async_copy(x_ref.at[s], tokens.at[token_rows(half_of)], x_load.at[s])
+
+    def token_arrived(h):
+        return send(x_ref.at[0], tokens.at[token_rows(h)], x_send.at[0], x_recv.at[h], {"seq": flipped_bit(place, 1)})
+
+    @pl.when(j == 0)
+    def _():
+        small_ref[...] = jnp.zeros_like(small_ref)
+        at = 0
+        for ref in (gains_ref, shifts_ref, taps_ref):
+            small_ref[at : at + ref.shape[0], :] = ref[...]
+            at += ref.shape[0]
+        for layer in range(2):
+            for q in range(4):
+                row = at + 4 * layer + q
+                small_ref[row : row + 1, :] = bias_ref[layer : layer + 1, q * r : (q + 1) * r]
+        barrier = pltpu.get_barrier_semaphore()
+        devices = [to_x, to_y, to_c, {"seq": flipped_bit(place, 1)}, {"seq": flipped_bit(place, 2)}, {"seq": 3 - place}]
+        for device in devices:
+            pl.semaphore_signal(barrier, inc=1, device_id=device, device_id_type=MESH)
+        pl.semaphore_wait(barrier, 6)
+        gather_begin(k)
+        for s in range(2):
+            away = 2 * s + side != place
+            pl.when(away)(lambda s=s: token_copy(s).start())
+            pl.when(jnp.logical_not(away))(lambda s=s: token_keep(s).start())
+        for u in range(k):
+            gather_begin(u)
+        gather_forward(k)
+        gather_far(k)
+        gather_end(k)
+        for dev in range(n):
+            cols = slice(dev * r, (dev + 1) * r)
+            vec[0:1, cols] = small[dev, 0:1, :].astype(F32)
+            vec[1:2, cols] = small[dev, 6:7, :].astype(F32)
+            for q in range(4):
+                at = 4 * (dev % 2) + q
+                vec[2 + dev // 2 : 3 + dev // 2, at * r : (at + 1) * r] = small[dev, 52 + q : 53 + q, :].astype(F32)
+        gather_forward(0)
+        gather_forward(1)
+        for s in range(2):
+            away = 2 * s + side != place
+            pl.when(away)(lambda s=s: token_copy(s).wait_send())
+            pl.when(jnp.logical_not(away))(lambda s=s: token_keep(s).wait())
+        for h in range(2):
+            pl.when(2 * half_of + h != place)(lambda h=h: token_arrived(h).wait_recv())
+        gather_forward(2)
+        gather_forward(3)
+        for rows in cuts(t):
+            c, _ = normal(tokens[rows, :].astype(F32))
+            v = (c * vec[0:1, :] + vec[1:2, :]).astype(BF)
+            unit[rows, :] = v
+            unit_t_ref[:, rows] = v.T
+        tokens_ref[...] = tokens[...]
+        small_out_ref[...] = small[...]
+        for u in range(k):
+            gather_far(u)
+
+    def leave(u):
+        return pltpu.make_async_copy(w.at[:, u], w_out_ref.at[:, u], w_leave.at[u])
+
+    for u in range(k):
+
+        @pl.when(j == u)
+        def _(u=u):
+            gather_end(u)
+            leave(u).start()
+
+    weights = w[:, j].reshape(d, d)
+    for rows in cuts(t):
+        s = dot(unit[rows, :], weights, 1, 0) + vec[pl.ds(2 + j, 1), :]
+        inner_ref[rows, :] = s.astype(BF)
+        a = (s * jax.nn.sigmoid(s)).astype(BF)
+        act_ref[rows, :] = a
+        act_t_ref[:, rows] = a.T
+
+    @pl.when(j == k - 1)
+    def _():
+        for u in range(k + 1):
+            gather_sent(u)
+        for u in range(k):
+            leave(u).wait()
+
+
+def first_forward(x, w, gains, shifts, taps, bias):
+    _, half, d = x.shape
+    k, r, _ = w.shape
+    n, t = 8, 2 * half
+    rows = 64
+    dma = pltpu.SemaphoreType.DMA
+    anywhere = pl.BlockSpec(memory_space=pl.ANY)
+
+    def whole(*shape):
+        return pl.BlockSpec(shape, lambda j: (0,) * len(shape))
+
+    return pl.pallas_call(
+        first_kernel,
+        grid=(k,),
+        in_specs=[anywhere] * 2 + [whole(*a.shape) for a in (gains, shifts, taps, bias)],
+        out_specs=[
+            pl.BlockSpec((t, d), lambda j: (0, j)),
+            pl.BlockSpec((t, d), lambda j: (0, j)),
+            pl.BlockSpec((d, t), lambda j: (j, 0)),
+            whole(d, t),
+            whole(t, d),
+            whole(n, rows, r),
+            anywhere,
+        ],
+        out_shape=[
+            jax.ShapeDtypeStruct((t, k * d), BF),
+            jax.ShapeDtypeStruct((t, k * d), BF),
+            jax.ShapeDtypeStruct((k * d, t), BF),
+            jax.ShapeDtypeStruct((d, t), BF),
+            jax.ShapeDtypeStruct((t, d), BF),
+            jax.ShapeDtypeStruct((n, rows, r), BF),
+            jax.ShapeDtypeStruct((n, k, r, d), BF),
+        ],
+        scratch_shapes=[
+            scr((n, k, r, d), BF),
+            scr((n, rows, r), BF),
+            scr((rows, r), BF),
+            scr((t, d), BF),
+            scr((t, d), BF),
+            scr((8, d), F32),
+            dma((3, k + 1)),
+            dma((3, k + 1)),
+            dma((2, k + 1)),
+            dma((2, k + 1)),
+            dma((3, k + 1)),
+            dma((3, k + 1)),
+            dma((2,)),
+            dma((2,)),
+            dma((2 + k + 1,)),
+            dma((k,)),
+        ],
+        compiler_params=pltpu.CompilerParams(vmem_limit_bytes=VMEM, collective_id=3, has_side_effects=True),
+        cost_estimate=pl.CostEstimate(flops=30_000_000_000, bytes_accessed=100_000_000, transcendentals=0),
+        name="first",
+    )(x, w, gains, shifts, taps, bias)
+
+
 ORDER = [
     ("q", 0), ("q", 1), ("q", 2), ("m", 0), ("m", 1), ("in", 0), ("m", 2), ("in", 1), ("m", 3),
     ("in", 2), ("out", 0), ("in", 3), ("out", 1), ("out", 2), ("out", 3),
@@ -987,10 +1221,6 @@
 LAST_IN = 11
 AHEAD = 2
 HELD = 6
-
-
-def flipped_bit(index, mask):
-    return index + mask - 2 * mask * lax.rem(lax.div(index, jnp.int32(mask)), jnp.int32(2))
 
 
 def thin(count):
@@ -1696,11 +1926,20 @@
 
     shard_a = jnp.stack(chunks(ffn_in[0]))
     shard_b = jnp.concatenate([ffn_out[0].reshape(4, r, width), qkv], axis=0)
-    shard_c = jnp.stack([attn_out] + chunks(conv_in) + [conv_out])
-    shard_d = jnp.concatenate([jnp.stack(chunks(ffn_in[1])), ffn_out[1].reshape(4, r, width)], axis=0)
-    small = jnp.concatenate([gains, shifts, depthwise, ffn_in_bias.reshape(-1, r)], axis=0)
-    small = lax.all_gather(small, "fsdp", axis=0)
-    w_a = lax.all_gather(shard_a, "fsdp", axis=0)
+    shard_c = jnp.stack(chunks(ffn_in[1]) + [attn_out] + chunks(conv_in) + [conv_out])
+    shard_d = ffn_out[1].reshape(4, r, width)
+    if cubed:
+        w_b = lax.all_gather(shard_b, "fsdp", axis=0)
+        inner_a, act_a, act_t_a, unit_t_a, tokens, small, w_a = first_forward(
+            inputs, after(shard_a, shard_b), gains, shifts, depthwise, ffn_in_bias
+        )
+        cotangent = to_pairs(after(grad_out, act_a), place)
+    else:
+        small = jnp.concatenate([gains, shifts, depthwise, ffn_in_bias.reshape(-1, r)], axis=0)
+        small = lax.all_gather(small, "fsdp", axis=0)
+        w_a = lax.all_gather(shard_a, "fsdp", axis=0)
+        w_b = lax.all_gather(shard_b, "fsdp", axis=0)
+        tokens, cotangent = to_pairs(inputs, place), to_pairs(grad_out, place)
 
     small = small.astype(F32)
     rows = jnp.transpose(small, (1, 0, 2))
@@ -1708,46 +1947,44 @@
     gain = rows[:n_gain].reshape(n_gain, width)
     shift = rows[n_gain : n_gain + n_shift].reshape(n_shift, width)
     taps = rows[n_gain + n_shift : n_plain].reshape(n_tap, width)
-    bias = small[:, n_plain:].reshape(n, 2, -1).transpose(1, 0, 2).reshape(2, inner_width)
-
-    tokens = to_pairs(inputs, place)
-    cotangent = to_pairs(grad_out, place)
+    bias = small[:, n_plain : n_plain + 8].reshape(n, 2, -1).transpose(1, 0, 2).reshape(2, inner_width)
+
     length = jnp.where(place < 2, lengths[0], lengths[1]).reshape(1)
     wide, ends = tables(distance)
     pairs = [(0, 1), (2, 3)]
 
-    w_b = lax.all_gather(after(shard_b, w_a, small, tokens), "fsdp", axis=0)
-    inner_a, act_a, act_t_a, unit_t_a = ffn_in_forward(tokens, jnp.stack([gain[0], shift[0]]), bias[0], w_a, 0)
-    w_c = lax.all_gather(after(shard_c, w_b, act_a), "fsdp", axis=0)
+    if not cubed:
+        inner_a, act_a, act_t_a, unit_t_a = ffn_in_forward(tokens, jnp.stack([gain[0], shift[0]]), bias[0], w_a, 0)
+    w_c = lax.all_gather(after(shard_c, w_b, cotangent, act_a), "fsdp", axis=0)
     first, unit_t_1, mine, other = out_qkv_forward(
         odd_word, tokens, act_a, w_b, jnp.stack([shift[6], gain[1], shift[1], shift[8], shift[9]])
     )
-    w_d = lax.all_gather(after(shard_d, other), "fsdp", axis=0)
     probs, heads, mixed = attend(mine, other, length, wide, ends)
+    w_d = lax.all_gather(after(shard_d, w_c, mixed), "fsdp", axis=0)
     second, mixed_t, unit_t_2, val, sig, gated = mid_forward(
-        first, mixed, w_c, 0, 1, jnp.stack([shift[10], gain[2], shift[2], shift[11], shift[12]])
+        first, mixed, w_c, 4, 5, jnp.stack([shift[10], gain[2], shift[2], shift[11], shift[12]])
     )
     count = gated.shape[0]
     halo = lax.ppermute(gated[count - 32 :], "seq", pairs)
     conv, act_t_c, third = conv_forward(
-        gated, halo, taps, jnp.stack([shift[13], gain[3], shift[3], shift[14]]), second, w_c, 3
+        gated, halo, taps, jnp.stack([shift[13], gain[3], shift[3], shift[14]]), second, w_c, 7
     )
-    inner_b, act_b, act_t_b, unit_t_b = ffn_in_forward(third, jnp.stack([gain[4], shift[4]]), bias[1], w_d, 0)
-    outputs, d4, sums_5 = out_last(third, act_b, w_d, 1, cotangent, jnp.stack([shift[7], gain[5], shift[5]]))
+    inner_b, act_b, act_t_b, unit_t_b = ffn_in_forward(third, jnp.stack([gain[4], shift[4]]), bias[1], w_c, 0)
+    outputs, d4, sums_5 = out_last(third, act_b, w_d, 0, cotangent, jnp.stack([shift[7], gain[5], shift[5]]))
     outputs = from_pairs(outputs, place)
 
-    dinner, dout, dbias_b, sums_7 = ffn_hidden_back(d4, inner_b, w_d, 1)
+    dinner, dout, dbias_b, sums_7 = ffn_hidden_back(d4, inner_b, w_d, 0)
     g_out_b = weight_grad(act_t_b, dout, n, 4, 0, True)
     g_in_b = weight_grad(unit_t_b, after(dinner, g_out_b), n, 4, 0, False)
     part_out_b = lax.psum_scatter(g_out_b, "fsdp", scatter_dimension=0, tiled=False)
     part_in_b = lax.psum_scatter(g_in_b, "fsdp", scatter_dimension=0, tiled=False)
     dinner = after(dinner, g_in_b)
-    d3, sums_4 = norm_input_back(d4, dinner, third, w_d, 0, gain[4:5])
+    d3, sums_4 = norm_input_back(d4, dinner, third, w_c, 0, gain[4:5])
     d3, outputs = lax.optimization_barrier((d3, outputs))
-    dconv, dout_3, sums_3 = conv_out_back(d3, conv, w_c, 3, jnp.stack([gain[3], shift[3]]))
+    dconv, dout_3, sums_3 = conv_out_back(d3, conv, w_c, 7, jnp.stack([gain[3], shift[3]]))
     follow = lax.ppermute(dconv[:32], "seq", [(j, i) for i, j in pairs])
     d2, dout_2, dglu, mine, other, sums_2 = mid_back(
-        odd_word, dconv, follow, taps, val, sig, second, d3, w_c, 0, 1, gain[2:3]
+        odd_word, dconv, follow, taps, val, sig, second, d3, w_c, 4, 5, gain[2:3]
     )
     if cubed:
         dqkv, dtable, share_out_b = attend_back(heads, probs, wide, mine, other, part_out_b)

time: 725 us -> 682 us (0.941)
  waiting for transfers between devices: 124 us -> 46.2 us
  Pallas kernels: 497 us -> 562 us
  starting transfers between devices: 31.7 us -> 20.9 us
  blocking collectives: 9.46 us -> 0 us
    all_gather x4 -> x3, waiting for transfers between devices: 112 us -> 24.9 us  [the longest x1 11.8 us: on_device(): w_c = lax.all_gather(after(shard_c, w_b, cotangent, act_a), 'fsdp', axis=0)]
    pallas_call x0 -> x1, Pallas kernels: none -> 82.7 us  [first_forward(): pl.pallas_call(first_kernel, grid=(k,), in_specs=[anywhere] * 2 + [whole(...]
    pallas_call x12 -> x11, Pallas kernels: 147 us -> 135 us  [call(): pl.pallas_call(kernel, grid=grid, in_specs=[spec(a.shape, b, w) for a, b,...]
    all_gather x1 -> x0, blocking collectives: 9.46 us -> none  [on_device(): small = lax.all_gather(small, 'fsdp', axis=0)]
    ppermute x2 -> x1, starting transfers between devices: 9.38 us -> 0.01 us  [to_pairs(): lax.ppermute(jnp.where(place % 2 == 0, two, one), 'seq', [(0, 2), (1, 0),...]
    ppermute x2 -> x1, waiting for transfers between devices: 4.49 us -> 13.5 us  [to_pairs(): lax.ppermute(jnp.where(place % 2 == 0, two, one), 'seq', [(0, 2), (1, 0),...]
  transfers between devices with their start and end apart: 14 -> 11, of which waited for: 6 -> 6; matrix products, arithmetic and copies ran while one was open for 4% -> 3% of each run, Pallas kernels for 35% -> 49%
where the time goes in v3:
time: 682 us; the launch traced here: 674 us
  Pallas kernels  562 us (82%)
  waiting for transfers between devices  46.2 us (7%)
  starting transfers between devices  20.9 us (3%)
  local copies, waits for them, and re-layouts  17.7 us (3%)
  between operations  15.9 us (2%)
  other arithmetic  10.5 us (2%)
    pallas_call x1, Pallas kernels, last_reduced(): pl.pallas_call(last_kernel, in_specs=[vmem] * 8 + [anywhere] * 20, out_sp...  195 us
    pallas_call x11, Pallas kernels, call(): pl.pallas_call(kernel, grid=grid, in_specs=[spec(a.shape, b, w) for a, b,...  135 us
    pallas_call x1, Pallas kernels, attend_back(): pl.pallas_call(functools.partial(bwd_kernel, with_part), grid=(pairs, STE...  82.8 us
    pallas_call x1, Pallas kernels, first_forward(): pl.pallas_call(first_kernel, grid=(k,), in_specs=[anywhere] * 2 + [whole(...  82.7 us
    pallas_call x1, Pallas kernels, attend(): pl.pallas_call(fwd_kernel, grid=(pairs, STEPS), in_specs=[pl.BlockSpec(me...  58.6 us
  transfers between devices with their start and end apart: 11, of which 6 were waited for; matrix products, arithmetic and copies ran while one was open for 3% of the time, Pallas kernels for 49%

profile of v3, /device:TPU:0, one launch (start us, length us, event | category | flops | bytes accessed | tf_op | source)
XLA Modules:
  0.0 673.6 jit_solution(12021341849089365647)
XLA Ops:
  7.2 2.7 fusion.5
  13.6 82.7 %first.1 = (bf16[512,4096]{1,0:T(8,128)(2,1)}, bf16[512,4096]{1,0:T(8,128)(2,1)}, bf16[4096,512]{1,0:T(8,128)(2,1)}, bf16[1024,512]{1,0:T(8,128)(2,1)}, bf16[512...) custom-call(bf16[2,256,1024]{2,1,0:T(8,128)(2,1)} %x_ref.1, ...), custom_call_target="tpu_custom_call" | custom-call | flops 30000001024 | bytes 100000000 | tf_op jit(solution)/shard_map/first/pallas_call | solution.py:1169
  100.1 13.5 %collective-permute-done.1 = bf16[256,1024]{1,0:T(8,128)(2,1)} collective-permute-done((bf16[256,1024]{1,0:T(8,128)(2,1)}, bf16[256,1024]{1,0:T(8,128)(2,1)}, u32[]{:S(2)}, u32[]{:S(2)}) %collective-permute-start.1) | collective-permute-done | bytes 524320 | tf_op jit(solution)/shard_map/ppermute | solution.py:1879
  116.0 4.2 all-gather.7.cloned.1.call-done
  124.8 17.2 %out_qkv.1 = (f32[512,1024]{1,0:T(8,128)}, bf16[1024,512]{1,0:T(8,128)(2,1)}, bf16[4,3,512,128]{3,2,1,0:T(8,128)(2,1)}, bf16[4,3,512,128]{3,2,1,0:T(8,128)(2,1)}) custom-call(s32[1]{0:T(128)} %bitcast.odd_ref, bf16[512,1024]{1,0:T(8,128)(2,1)} %get-tuple-element.86.x_ref, bf16[512,4096]{1,0:T(8,128)(2,1)} %get-tuple-element.87.act_ref, ...), custom_call_target="tpu_custom_call" | custom-call | flops 7516192768 | bytes 25165824 | tf_op jit(solution)/shard_map/out_qkv/pallas_call | solution.py:390
  142.0 58.6 %attend_fwd.1 = (bf16[8,1024,1024]{2,1,0:T(8,128)(2,1)}, bf16[4,3,1024,128]{3,2,1,0:T(8,128)(2,1)}, bf16[512,1024]{1,0:T(8,128)(2,1)}) custom-call(s32[1]{0:T(128)} %bitcast.16.len_ref, bf16[128,512]{1,0:T(8,128)(2,1)} %maximum_maximum_fusion.wide_ref, bf16[128,128]{1,0:T(8,128)(2,1)} %pad_maximum_fusion.4.ends_ref, ...), custom_call_target="tpu_custom_call" | custom-call | flops 40000000000 | bytes 120000000 | tf_op jit(solution)/shard_map/attend_fwd/pallas_call | solution.py:312
  200.6 11.8 %all-gather.9.cloned.1.call-done = bf16[64,128,1024]{2,1,0:T(8,128)(2,1)} async-done(((bf16[8,128,1024]{2,1,0:T(8,128)(2,1)}), bf16[64,128,1024]{2,1,0:T(8,128)(2,1)}) %all-gather.9.cloned.1.call-update) | async-done | bytes 16777232 | tf_op jit(solution)/shard_map/all_gather | solution.py:1958
  216.1 11.1 %mid.1 = (f32[512,1024]{1,0:T(8,128)}, bf16[1024,512]{1,0:T(8,128)(2,1)}, bf16[1024,512]{1,0:T(8,128)(2,1)}, bf16[512,1024]{1,0:T(8,128)(2,1)}, bf16[512,1024]{1,0:T(8,128)(2,1)}, /*index=5*/bf16[512,1024]{1,0:T(8,128)(2,1)}) custom-call(f32[512,1024]{1,0:T(8,128)} %get-tuple-element.89.first_ref, bf16[512,1024]{1,0:T(8,128)(2,1)} %get-tuple-element.92.mixed_ref, ...), custom_call_target="tpu_custom_call" | custom-call | flops 3221225472 | bytes 16777216 | tf_op jit(solution)/shard_map/mid/pallas_call | solution.py:390
  228.1 3.4 collective-permute-start.2
  234.0 13.6 %conv.1 = (f32[512,1024]{1,0:T(8,128)}, bf16[1024,512]{1,0:T(8,128)(2,1)}, f32[512,1024]{1,0:T(8,128)}) custom-call(bf16[512,1024]{1,0:T(8,128)(2,1)} %get-tuple-element.95.gated_ref, bf16[32,1024]{1,0:T(8,128)(2,1)} %copy-done.12, f32[31,1024]{1,0:T(8,128)} %bitcast.130, f32[4,1024]{1,0:T(4,128)} %pad_maximum_fusion.5.vec_ref, ...), custom_call_target="tpu_custom_call" | custom-call | flops 1073741824 | bytes 10485760 | tf_op jit(solution)/shard_map/conv/pallas_call | solution.py:390
  247.6 12.6 %ffn_in.1 = (bf16[512,4096]{1,0:T(8,128)(2,1)}, bf16[512,4096]{1,0:T(8,128)(2,1)}, bf16[4096,512]{1,0:T(8,128)(2,1)}, bf16[1024,512]{1,0:T(8,128)(2,1)}) custom-call(f32[512,1024]{1,0:T(8,128)} %get-tuple-element.97.x_ref, f32[2,1024]{1,0:T(2,128)} %get-tuple-element.237.vec_ref, f32[4,1,1024]{2,1,0:T(1,128)} %reshape_squeeze.10.bias_ref, ...), custom_call_target="tpu_custom_call" | custom-call | flops 4294967296 | bytes 20971520 | tf_op jit(solution)/shard_map/ffn_in/pallas_call | solution.py:390
  260.3 9.0 %all-gather.11.cloned.1.call-done = bf16[32,128,1024]{2,1,0:T(8,128)(2,1)} async-done(((bf16[4,128,1024]{2,1,0:T(8,128)(2,1)}), bf16[32,128,1024]{2,1,0:T(8,128)(2,1)}) %all-gather.11.cloned.1.call-update) | async-done | bytes 8388624 | tf_op jit(solution)/shard_map/all_gather | solution.py:1963
  269.3 12.3 %out_last.1 = (bf16[512,1024]{1,0:T(8,128)(2,1)}, f32[512,1024]{1,0:T(8,128)}, f32[8,1024]{1,0:T(8,128)}) custom-call(f32[512,1024]{1,0:T(8,128)} %get-tuple-element.97.x_ref, bf16[512,4096]{1,0:T(8,128)(2,1)} %get-tuple-element.98.act_ref, bf16[8,4,128,1024]{3,2,1,0:T(8,128)(2,1)} %bitcast.136, bf16[512,1024]{1,0:T(8,128)(2,1)} %pad_maximum_fusion.2.cot_ref, ...), custom_call_target="tpu_custom_call" | custom-call | flops 4294967296 | bytes 18874368 | tf_op jit(solution)/shard_map/out_last/pallas_call | solution.py:390
  281.5 11.3 %ffn_hidden_back.1 = (bf16[512,4096]{1,0:T(8,128)(2,1)}, bf16[512,1024]{1,0:T(8,128)(2,1)}, f32[4,1,1024]{2,1,0:T(1,128)}, f32[8,1024]{1,0:T(8,128)}) custom-call(f32[512,1024]{1,0:T(8,128)} %get-tuple-element.100.d_ref.dy_ref, bf16[512,4096]{1,0:T(8,128)(2,1)} %get-tuple-element.101.inner_ref, bf16[8,4,128,1024]{3,2,1,0:T(8,128)(2,1)} %bitcast.137), custom_call_target="tpu_custom_call" | custom-call | flops 4294967296 | bytes 16777216 | tf_op jit(solution)/shard_map/ffn_hidden_back/pallas_call | solution.py:390
  292.8 8.8 %weight_grad.2 = bf16[8,4,128,1024]{3,2,1,0:T(8,128)(2,1)} custom-call(bf16[4096,512]{1,0:T(8,128)(2,1)} %get-tuple-element.104.left_ref, bf16[512,1024]{1,0:T(8,128)(2,1)} %get-tuple-element.105.right_ref), custom_call_target="tpu_custom_call" | custom-call | flops 4294967296 | bytes 13631488 | tf_op jit(solution)/shard_map/weight_grad/pallas_call | solution.py:390
  301.7 8.9 %weight_grad.3 = bf16[8,4,128,1024]{3,2,1,0:T(8,128)(2,1)} custom-call(bf16[1024,512]{1,0:T(8,128)(2,1)} %get-tuple-element.103.left_ref, bf16[512,4096]{1,0:T(8,128)(2,1)} %get-tuple-element.107.right_ref.g_ref), custom_call_target="tpu_custom_call" | custom-call | flops 4294967296 | bytes 13631488 | tf_op jit(solution)/shard_map/weight_grad/pallas_call | solution.py:390
  313.5 12.8 %collective-permute-start.3 = (bf16[256,1024]{1,0:T(8,128)(2,1)S(1)}, bf16[256,1024]{1,0:T(8,128)(2,1)S(1)}, u32[]{:S(2)}, u32[]{:S(2)}) collective-permute-start(bf16[256,1024]{1,0:T(8,128)(2,1)S(1)} %get-tuple-element.207), channel_id=1, source_target_pairs={{8,16},{16,8},{9,17},{17,9},{10,18},{18,10},{11,19},{19,11},{12,20... | collective-permute-start | bytes 1572872 | tf_op jit(solution)/shard_map/ppermute | solution.py:1890
  327.7 12.1 %norm_input_back.1 = (f32[512,1024]{1,0:T(8,128)}, f32[8,1024]{1,0:T(8,128)}) custom-call(f32[512,1024]{1,0:T(8,128)} %get-tuple-element.100.d_ref.dy_ref, bf16[512,4096]{1,0:T(8,128)(2,1)} %get-tuple-element.107.right_ref.g_ref, f32[512,1024]{1,0:T(8,128)} %get-tuple-element.97.x_ref, bf16[8,8,128,1024]{3,2,1,0:T(8,128)(2,1)} %bitcast.121, f32[1,1024]{1,0:T(1,128)} %copy-done.14), custom_call_target="tpu_custom_call" | custom-call | flops 4294967296 | bytes 18874368 | tf_op jit(solution)/shard_map/norm_input_back/pallas_call | solution.py:390
  341.1 7.0 %conv_out_back.1 = (f32[512,1024]{1,0:T(8,128)}, bf16[512,1024]{1,0:T(8,128)(2,1)}, f32[8,1024]{1,0:T(8,128)}) custom-call(f32[512,1024]{1,0:T(8,128)} %get-tuple-element.113.d_ref.d3_ref, f32[512,1024]{1,0:T(8,128)} %get-tuple-element.114.conv_ref, bf16[8,8,128,1024]{3,2,1,0:T(8,128)(2,1)} %bitcast.122, f32[2,1024]{1,0:T(2,128)} %get-tuple-element.238.vec_ref), custom_call_target="tpu_custom_call" | custom-call | flops 1073741824 | bytes 10485760 | tf_op jit(solution)/shard_map/conv_out_back/pallas_call | solution.py:390
  350.9 6.5 collective-permute-done.5.follow_ref
  358.1 20.2 %mid_back.1 = (f32[512,1024]{1,0:T(8,128)}, bf16[512,1024]{1,0:T(8,128)(2,1)}, bf16[512,2048]{1,0:T(8,128)(2,1)}, bf16[4,512,128]{2,1,0:T(8,128)(2,1)}, bf16[4,512,128]{2,1,0:T(8,128)(2,1)}, /*index=5*/f32[8,1024]{1,0:T(8,128)}) custom-call(s32[1]{0:T(128)} %bitcast.odd_ref, f32[512,1024]{1,0:T(8,128)} %get-tuple-element.115.dconv_ref, ...), custom_call_target="tpu_custom_call" | custom-call | flops 3221225472 | bytes 18874368 | tf_op jit(solution)/shard_map/mid_back/pallas_call | solution.py:390
  378.3 82.8 %attend_bwd.1 = (bf16[512,3072]{1,0:T(8,128)(2,1)}, f32[128,128]{1,0:T(8,128)}, bf16[4,128,1024]{2,1,0:T(8,128)(2,1)}) custom-call(bf16[4,3,1024,128]{3,2,1,0:T(8,128)(2,1)} %get-tuple-element.111.heads_ref, bf16[8,1024,1024]{2,1,0:T(8,128)(2,1)} %get-tuple-element.112.p_ref, bf16[128,128]{1,0:T(8,128)(2,1)} %slice.336.wide_ref, ...), custom_call_target="tpu_custom_call" | custom-call | flops 49999998976 | bytes 150000000 | tf_op jit(solution)/shard_map/attend_bwd/pallas_call | solution.py:331
  461.2 195.4 %last.1 = (bf16[15,128,1024]{2,1,0:T(8,128)(2,1)}, bf16[4,128,1024]{2,1,0:T(8,128)(2,1)}, f32[64,128]{1,0:T(8,128)}, f32[128,128]{1,0:T(8,128)}, bf16[2,256,1024]{2,1,0:T(8,128)(2,1)}) custom-call(f32[2,1024]{1,0:T(2,128)} %slice_bitcast_fusion.10.gain_ref, f32[128,128]{1,0:T(8,128)} %get-tuple-element.120.table_ref, ...), custom_call_target="tpu_custom_call" | custom-call | flops 99999997952 | bytes 400000000 | tf_op jit(solution)/shard_map/last/pallas_call | solution.py:1685
  656.6 7.7 %finish.1 = (f32[2,128,4096]{2,1,0:T(8,128)}, f32[2,4,128,1024]{3,2,1,0:T(8,128)}, f32[3,128,1024]{2,1,0:T(8,128)}, f32[128,1024]{1,0:T(8,128)}, f32[128,2048]{1...) custom-call(bf16[15,128,1024]{2,1,0:T(8,128)(2,1)} %get-tuple-elemen, ...), custom_call_target="tpu_custom_call" | custom-call | bytes 18000000 | tf_op jit(solution)/shard_map/finish/pallas_call | solution.py:1822
  (100 shorter events, 31.5 us)
Async XLA Ops:
  7.2 2.8 copy-start.5
  7.2 113.0 %all-gather.7.cloned.1.call-start = ((), (), s32[]{:S(2)}) async-start(), calls=%async_computation.4 | async-start | bytes 16515072 | tf_op jit(solution)/shard_map/all_gather | solution.py:1932
  10.0 2.3 copy-start.3
  11.4 201.0 %all-gather.9.cloned.1.call-start = ((), (), s32[]{:S(2)}) async-start(), calls=%async_computation.5 | async-start | bytes 18874368 | tf_op jit(solution)/shard_map/all_gather | solution.py:1958
  13.6 82.7 %copy-start = (bf16[2,256,1024]{2,1,0:T(8,128)(2,1)S(1)}, bf16[2,256,1024]{2,1,0:T(8,128)(2,1)}, u32[]{:S(2)}) copy-start(bf16[2,256,1024]{2,1,0:T(8,128)(2,1)} %param.27) | copy-start | bytes 3145732
  96.3 2.7 copy-start.7
  96.3 2.8 copy-start.6
  97.3 2.7 copy-start.8
  97.3 2.8 collective-permute-start
  98.9 14.7 %collective-permute-start.1 = (bf16[256,1024]{1,0:T(8,128)(2,1)}, bf16[256,1024]{1,0:T(8,128)(2,1)}, u32[]{:S(2)}, u32[]{:S(2)}) collective-permute-start(bf16[256,1024]{1,0:T(8,128)(2,1)} %get-tuple-element.209), channel_id=1, source_target_pairs={{0,16},{8,0},{16,24},{24,8},{1,17},{9,1},{17,25},{25,9},{2,18},{10... | collective-permute-start | bytes 1572872 | tf_op jit(solution)/shard_map/ppermute | solution.py:1879
  100.1 15.9 %copy-start.2 = (bf16[8,128,1024]{2,1,0:T(8,128)(2,1)}, bf16[8,128,1024]{2,1,0:T(8,128)(2,1)S(1)}, u32[]{:S(2)}) copy-start(bf16[8,128,1024]{2,1,0:T(8,128)(2,1)S(1)} %bitcast_dynamic-update-slice_fusion) | copy-start | bytes 6291460
  114.9 5.4 copy-start.15
  114.9 7.2 %copy-start.10 = (bf16[73,64]{0,1:T(8,128)(2,1)S(1)}, bf16[73,64]{0,1:T(8,128)(2,1)}, u32[]{:S(2)}) copy-start(bf16[73,64]{0,1:T(8,128)(2,1)} %param.26) | copy-start | bytes 28036
  114.9 7.5 %copy-start.9 = (bf16[8,64,128]{2,1,0:T(8,128)(2,1)S(1)}, bf16[8,64,128]{2,1,0:T(8,128)(2,1)}, u32[]{:S(2)}) copy-start(bf16[8,64,128]{2,1,0:T(8,128)(2,1)} %get-tuple-element.88) | copy-start | bytes 393220
  120.2 149.1 %all-gather.11.cloned.1.call-start = ((), (), s32[]{:S(2)}) async-start(), calls=%async_computation.6 | async-start | bytes 9437184 | tf_op jit(solution)/shard_map/all_gather | solution.py:1963
  122.6 91.6 %copy-start.13 = (f32[1,1024]{1,0:T(1,128)}, f32[1,1024]{1,0:T(1,128)S(1)}, u32[]{:S(2)}) copy-start(f32[1,1024]{1,0:T(1,128)S(1)} %get-tuple-element.226.vec_ref) | copy-start | bytes 12292
  122.6 92.9 %copy-start.14 = (f32[1,1024]{1,0:T(1,128)}, f32[1,1024]{1,0:T(1,128)S(1)}, u32[]{:S(2)}) copy-start(f32[1,1024]{1,0:T(1,128)S(1)} %get-tuple-element.218.vec_ref) | copy-start | bytes 12292
  212.4 165.9 %reduce-scatter.3.cloned.1.call-start = ((), (), s32[]{:S(2)}) async-start(), calls=%async_computation.2 | async-start | bytes 9437184 | tf_op jit(solution)/shard_map/reduce_scatter | solution.py:1979
  228.1 5.2 collective-permute-start.2
  301.6 159.5 %reduce-scatter.5.cloned.1.call-start = ((), (), s32[]{:S(2)}) async-start(), calls=%async_computation.3 | async-start | bytes 9437184 | tf_op jit(solution)/shard_map/reduce_scatter | solution.py:1980
  312.1 27.8 %collective-permute-start.4 = (bf16[256,1024]{1,0:T(8,128)(2,1)S(1)}, bf16[256,1024]{1,0:T(8,128)(2,1)S(1)}, u32[]{:S(2)}, u32[]{:S(2)}) collective-permute-start(bf16[256,1024]{1,0:T(8,128)(2,1)S(1)} %get-tuple-element.206), channel_id=1, source_target_pairs={{16,0},{0,8},{24,16},{8,24},{17,1},{1,9},{25,17},{9,25},{18,2},{2,... | collective-permute-start | bytes 1572872 | tf_op jit(solution)/shard_map/ppermute | solution.py:1889
  313.5 26.3 %collective-permute-start.3 = (bf16[256,1024]{1,0:T(8,128)(2,1)S(1)}, bf16[256,1024]{1,0:T(8,128)(2,1)S(1)}, u32[]{:S(2)}, u32[]{:S(2)}) collective-permute-start(bf16[256,1024]{1,0:T(8,128)(2,1)S(1)} %get-tuple-element.207), channel_id=1, source_target_pairs={{8,16},{16,8},{9,17},{17,9},{10,18},{18,10},{11,19},{19,11},{12,20... | collective-permute-start | bytes 1572872 | tf_op jit(solution)/shard_map/ppermute | solution.py:1890
  349.0 8.4 %collective-permute-start.5 = (f32[32,1024]{1,0:T(8,128)S(1)}, f32[32,1024]{1,0:T(8,128)S(1)}, u32[]{:S(2)}, u32[]{:S(2)}) collective-permute-start(f32[32,1024]{1,0:T(8,128)S(1)} %slice.302), channel_id=1, source_target_pairs={{8,0},{24,16},{9,1},{25,17},{10,2},{26,18},{11,3},{27,19},{12,4},{... | collective-permute-start | bytes 393224 | tf_op jit(solution)/shard_map/ppermute | solution.py:1985
  656.5 9.2 %copy-start.4 = (bf16[2,256,1024]{2,1,0:T(8,128)(2,1)S(1)}, bf16[2,256,1024]{2,1,0:T(8,128)(2,1)}, u32[]{:S(2)}) copy-start(bf16[2,256,1024]{2,1,0:T(8,128)(2,1)} %get-tuple-element.253) | copy-start | bytes 3145732
  (3 other events, 2.7 us)
Sparse Core Ops, SparseCore 0:
  11.5 108.6 all-gather.6
  122.7 89.6 all-gather.8
  214.9 54.3 all-gather.10
  301.8 71.2 reduce-scatter.2
  376.8 71.2 reduce-scatter.4

commit v4 on v3

--- a/solution.py
+++ b/solution.py
@@ -208,7 +208,7 @@
     @pl.when(step==0)
     def _():
         load(pair).wait()
-        arrive(pair).wait()
+        pl.when(pair>0)(lambda: arrive(pair).wait())
         kx_ref[:,0:128]=heads_ref[0,1]
         dka[...]=jnp.zeros_like(dka); dva[...]=jnp.zeros_like(dva)
     if with_part:
@@ -223,7 +223,11 @@
                     z_step(i,stage)
                     if stage==2:
                         result_do(i,lambda copy: copy.start())
-    i0=pl.multiple_of(block_at(step,half)*RB,RB)
+    @pl.when((pair==0)&(step==2))
+    def _():
+        arrive(pair).wait()
+    turned=lax.rem(step+2*jnp.where(pair==0,1,0),jnp.int32(STEPS))
+    i0=pl.multiple_of(block_at(turned,half)*RB,RB)
     q2=heads_ref[0,0,pl.ds(i0,RB)]
     v2=heads_ref[0,2]
     do2=buf[pair,pl.ds(i0,RB)]
@@ -264,13 +268,13 @@
         dqs.append(dq)
         dea[...]+=dot(drel,qh,0,0)
     dq=(jnp.where(lane<64,dqs[0],dqs[1])*HEAD_DIM**-0.5).astype(BF)
-    @pl.when(step<2)
-    def _():
-        stage_q[pair,step]=dq
-        leave_q(pair,step,half).start()
-    @pl.when(step>=2)
-    def _():
-        dqkv[pl.ds(pl.multiple_of((step-2)*RB,RB),RB),columns(0,half,pair)]=dq
+    @pl.when(turned<2)
+    def _():
+        stage_q[pair,turned]=dq
+        leave_q(pair,turned,half).start()
+    @pl.when(turned>=2)
+    def _():
+        dqkv[pl.ds(pl.multiple_of((turned-2)*RB,RB),RB),columns(0,half,pair)]=dq
     @pl.when(step==STEPS-1)
     def _():
         for i,acc in enumerate((dka,dva)):
@@ -330,7 +334,7 @@
     extra=[pltpu.VMEM(part.shape,BF)]*3+[dma((part.shape[0],))]*2+[dma((part.shape[0],3))]*2 if with_part else []
     return pl.pallas_call(functools.partial(bwd_kernel,with_part),
         grid=(pairs,STEPS),
-        in_specs=[pl.BlockSpec((1,3,n,128),lambda a,b:(a,0,0,0)),pl.BlockSpec((2,RB,n),lambda a,b:(a,b,0)),whole(128,128),anywhere,anywhere]+[anywhere]*with_part,
+        in_specs=[pl.BlockSpec((1,3,n,128),lambda a,b:(a,0,0,0)),pl.BlockSpec((2,RB,n),lambda a,b:(a,jnp.where(a==0,lax.rem(b+2,STEPS),b),0)),whole(128,128),anywhere,anywhere]+[anywhere]*with_part,
         out_specs=[whole(own,6*own),whole(128,128)]+[anywhere]*with_part,
         out_shape=[jax.ShapeDtypeStruct((own,6*own),BF),jax.ShapeDtypeStruct((128,128),F32)]+([jax.ShapeDtypeStruct(part.shape,BF)] if with_part else []),
         scratch_shapes=[pltpu.VMEM((RB,PADL+n+256),F32),pltpu.VMEM((n,256),BF),pltpu.VMEM((128,n),F32),pltpu.VMEM((128,n),F32),pltpu.VMEM((128,128),F32),
@@ -643,7 +647,7 @@
     )
 
 
-def out_last_kernel(x_ref, act_ref, w_ref, cot_ref, vec_ref, out_ref, d_ref, sums_ref, acc):
+def out_last_kernel(x_ref, act_ref, w_ref, cot_ref, vec_ref, out_ref, d_ref, dout_ref, sums_ref, acc):
     s = pl.program_id(0)
     t = x_ref.shape[0]
     w = flat(w_ref)
@@ -659,7 +663,9 @@
             n, r = normal(fourth)
             out_ref[rows, :] = (n * vec_ref[1:2, :] + vec_ref[2:3, :]).astype(BF)
             dy = cot_ref[rows, :].astype(F32)
-            d_ref[rows, :] = normal_back(dy, n, r, vec_ref[1:2, :])
+            d = normal_back(dy, n, r, vec_ref[1:2, :])
+            d_ref[rows, :] = d
+            dout_ref[rows, :] = (HALF * d).astype(BF)
             sums_ref[0:1, :] += total(dy * n)
             sums_ref[1:2, :] += total(dy)
 
@@ -677,7 +683,7 @@
             (cot, None, None),
             (vec, None, None),
         ],
-        [((t, d), BF, None, None), ((t, d), F32, None, None), ((8, d), F32, None, None)],
+        [((t, d), BF, None, None), ((t, d), F32, None, None), ((t, d), BF, None, None), ((8, d), F32, None, None)],
         [scr((t, d), F32)],
         name="out_last",
         flops=8 * t * d * d,
@@ -692,7 +698,7 @@
     def _():
         sums_ref[...] = jnp.zeros_like(sums_ref)
         for rows in cuts(t):
-            v = (HALF * d_ref[rows, :]).astype(BF)
+            v = d_ref[rows, :] if d_ref.dtype == BF else (HALF * d_ref[rows, :]).astype(BF)
             dout_ref[rows, :] = v
             sums_ref[0:1, :] += total(v.astype(F32))
 
@@ -1212,6 +1218,206 @@
     )(x, w, gains, shifts, taps, bias)
 
 
+def middle_kernel(
+    g_ref, w_ref, w_attn_ref, taps_ref, vec_ref, dy_in, third_in, conv_in, val_in, sig_in, second_in, result_ref,
+    d2_ref, dout_2_ref, mine_ref, other_ref, sums_4_ref, sums_3_ref, sums_2_ref, dconv_out, dout_3_out, dglu_out, outputs_ref,
+    dy_ref, third_ref, conv_ref, val_ref, sig_ref, second_ref, dout_3_ref, dglu_ref,
+    acc, d3, pad, load_sem, leave_sem, halo_send, halo_recv, out_send, out_recv, out_keep,
+):
+    s = pl.program_id(0)
+    t, d = third_ref.shape
+
+    def load(i):
+        src = (dy_in, third_in, conv_in, val_in, sig_in, second_in)[i]
+        dst = (dy_ref, third_ref, conv_ref, val_ref, sig_ref, second_ref)[i]
+        return pltpu.make_async_copy(src, dst, load_sem.at[i])
+
+    def leave(i):
+        src = (pad.at[pl.ds(0, t)], dout_3_ref, dglu_ref)[i]
+        return pltpu.make_async_copy(src, (dconv_out, dout_3_out, dglu_out)[i], leave_sem.at[i])
+
+    place = lax.axis_index("seq")
+    two = jnp.int32(2)
+    odd, seq = lax.rem(place, two), lax.div(place, two)
+    partner = {"seq": flipped_bit(place, 1)}
+    half = d // 2
+
+    def halo_copy():
+        return pltpu.make_async_remote_copy(
+            src_ref=pad.at[pl.ds(0, 32)],
+            dst_ref=pad.at[pl.ds(t, 32)],
+            send_sem=halo_send,
+            recv_sem=halo_recv,
+            device_id=partner,
+            device_id_type=MESH,
+        )
+
+    def out_copy(h, to, s):
+        return pltpu.make_async_remote_copy(
+            src_ref=result_ref.at[pl.ds(h * (t // 2), t // 2)],
+            dst_ref=outputs_ref.at[s],
+            send_sem=out_send.at[h],
+            recv_sem=out_recv.at[s],
+            device_id={"seq": to},
+            device_id_type=MESH,
+        )
+
+    def out_stay(h):
+        return pltpu.make_async_copy(result_ref.at[pl.ds(h * (t // 2), t // 2)], outputs_ref.at[seq], out_keep)
+
+    @pl.when(s == 0)
+    def _():
+        for i in range(6):
+            load(i).start()
+        barrier = pltpu.get_barrier_semaphore()
+        for device in (partner, {"seq": flipped_bit(place, 2)}, {"seq": 3 - place}):
+            pl.semaphore_signal(barrier, inc=1, device_id=device, device_id_type=MESH)
+        pl.semaphore_wait(barrier, 3)
+        for h in range(2):
+            away = 2 * odd + h != place
+            pl.when(away)(lambda h=h: out_copy(h, 2 * odd + h, seq).start())
+            pl.when(jnp.logical_not(away))(lambda h=h: out_stay(h).start())
+        for ref in (sums_4_ref, sums_3_ref, sums_2_ref):
+            ref[...] = jnp.zeros_like(ref)
+
+    w = flat(w_ref)
+
+    @pl.when(s < 4)
+    def _():
+        for rows in cuts(t):
+            p = dot(g_ref[rows, :], w, 1, 1)
+            acc[rows, :] = p + jnp.where(s == 0, 0.0, acc[rows, :])
+
+    @pl.when(s == 3)
+    def _():
+        load(0).wait()
+        load(1).wait()
+        for rows in cuts(t):
+            n, r = normal(third_ref[rows, :])
+            du = acc[rows, :]
+            value = dy_ref[rows, :] + normal_back(du, n, r, vec_ref[0:1, :])
+            d3[rows, :] = value
+            dout = value.astype(BF)
+            dout_3_ref[rows, :] = dout
+            sums_4_ref[0:1, :] += total(du * n)
+            sums_4_ref[1:2, :] += total(du)
+            sums_3_ref[0:1, :] += total(dout.astype(F32))
+        leave(1).start()
+
+    @pl.when(s == 4)
+    def _():
+        load(2).wait()
+        for i, rows in enumerate(cuts(t)):
+            da = dot(dout_3_ref[rows, :], w, 1, 1)
+            n, r = normal(conv_ref[rows, :])
+            du = da * silu_slope(n * vec_ref[1:2, :] + vec_ref[2:3, :])
+            dconv = normal_back(du, n, r, vec_ref[1:2, :])
+            pad[rows, :] = dconv
+            sums_3_ref[1:2, :] += total(du * n)
+            sums_3_ref[2:3, :] += total(du)
+            sums_3_ref[3:4, :] += total(dconv)
+            if i == 0:
+
+                @pl.when(odd == 1)
+                def _():
+                    halo_copy().start()
+                    pad[t : t + 32, :] = jnp.zeros((32, d), F32)
+
+        leave(0).start()
+
+    @pl.when(s == 5)
+    def _():
+        load(3).wait()
+        load(4).wait()
+        pl.when(odd == 1)(lambda: halo_copy().wait_send())
+        pl.when(odd == 0)(lambda: halo_copy().wait_recv())
+
+        def write(rows, cols, dgated):
+            sig = sig_ref[rows, cols].astype(F32)
+            dval = dgated * sig
+            dglu_ref[rows, cols] = dval.astype(BF)
+            dgate = dval * val_ref[rows, cols].astype(F32) * (1.0 - sig)
+            dglu_ref[rows, cols.start + d : cols.stop + d] = dgate.astype(BF)
+
+        fir(pad, taps_ref, 0, t, d, lambda cols: jnp.zeros((ROWS, COLS), F32), write, turned=True)
+        for rows in cuts(t):
+            sums_2_ref[0:1, :] += total(dglu_ref[rows, :d].astype(F32))
+            sums_2_ref[1:2, :] += total(dglu_ref[rows, d:].astype(F32))
+            acc[rows, :] = dot(dglu_ref[rows, :d], w, 1, 1)
+        leave(2).start()
+
+    @pl.when(s == 6)
+    def _():
+        load(5).wait()
+        w_attn = flat(w_attn_ref)
+        for rows in cuts(t):
+            du = acc[rows, :] + dot(dglu_ref[rows, d:], w, 1, 1)
+            n, r = normal(second_ref[rows, :])
+            d2 = d3[rows, :] + normal_back(du, n, r, vec_ref[3:4, :])
+            sums_2_ref[2:3, :] += total(du * n)
+            sums_2_ref[3:4, :] += total(du)
+            d2_ref[rows, :] = d2
+            dout = d2.astype(BF)
+            dout_2_ref[rows, :] = dout
+            sums_2_ref[4:5, :] += total(dout.astype(F32))
+            dm = dot(dout, w_attn, 1, 1)
+            low, high = dm[:, :half], dm[:, half:]
+            mine = jnp.where(odd == 1, high, low).astype(BF)
+            other = jnp.where(odd == 1, low, high).astype(BF)
+            for part in range(half // 128):
+                cols = slice(part * 128, part * 128 + 128)
+                mine_ref[part, rows, :] = mine[:, cols]
+                other_ref[part, rows, :] = other[:, cols]
+        for i in range(3):
+            leave(i).wait()
+        for h in range(2):
+            away = 2 * odd + h != place
+            pl.when(away)(lambda h=h: out_copy(h, 2 * odd + h, seq).wait_send())
+            pl.when(jnp.logical_not(away))(lambda h=h: out_stay(h).wait())
+        for q in range(2):
+            pl.when(2 * q + seq != place)(lambda q=q: out_copy(0, flipped_bit(place, 1), q).wait_recv())
+
+
+def middle_back(dy, g, third, conv, val, sig, second, w, taps, vec, result):
+    t, d = dy.shape
+    n, _, r, _ = w.shape
+    dma = pltpu.SemaphoreType.DMA
+
+    def whole(*shape):
+        return pl.BlockSpec(shape, lambda s: (0,) * len(shape))
+
+    anywhere = pl.BlockSpec(memory_space=pl.ANY)
+    outs = [
+        ((t, d), F32), ((t, d), BF), ((d // 256, t, 128), BF), ((d // 256, t, 128), BF),
+        ((8, d), F32), ((8, d), F32), ((8, d), F32),
+    ]
+    far = [((t, d), F32), ((t, d), BF), ((t, 2 * d), BF), ((2, t // 2, d), BF)]
+    d2, dout_2, mine, other, sums_4, sums_3, sums_2, dconv, dout_3, dglu, result = pl.pallas_call(
+        middle_kernel,
+        grid=(7,),
+        in_specs=[
+            pl.BlockSpec((t, d), lambda s: (0, jnp.minimum(s, 3))),
+            pl.BlockSpec((n, 1, r, d), lambda s: (0, jnp.where(s == 4, 7, s), 0, 0)),
+            pl.BlockSpec((n, 1, r, d), lambda s: (0, 4, 0, 0)),
+            whole(*taps.shape),
+            whole(*vec.shape),
+        ]
+        + [anywhere] * 7,
+        out_specs=[whole(*shape) for shape, _ in outs] + [anywhere] * 4,
+        out_shape=[jax.ShapeDtypeStruct(shape, kind) for shape, kind in outs + far],
+        scratch_shapes=[
+            scr((t, d), F32), scr((t, d), F32), scr((t, d), F32), scr((t, d), BF), scr((t, d), BF), scr((t, d), F32),
+            scr((t, d), BF), scr((t, 2 * d), BF),
+            scr((t, d), F32), scr((t, d), F32), scr((t + 32, d), F32),
+            dma((6,)), dma((3,)), dma, dma, dma((2,)), dma((2,)), dma,
+        ],
+        compiler_params=pltpu.CompilerParams(vmem_limit_bytes=58 << 20, collective_id=4, has_side_effects=True),
+        cost_estimate=pl.CostEstimate(flops=40_000_000_000, bytes_accessed=120_000_000, transcendentals=0),
+        name="middle_back",
+    )(g, w, w, taps, vec, dy, third, conv, val, sig, second, result)
+    return dconv, dout_3, d2, dout_2, dglu, mine, other, sums_4, sums_3, sums_2, result
+
+
 ORDER = [
     ("q", 0), ("q", 1), ("q", 2), ("m", 0), ("m", 1), ("in", 0), ("m", 2), ("in", 1), ("m", 3),
     ("in", 2), ("out", 0), ("in", 3), ("out", 1), ("out", 2), ("out", 3),
@@ -1235,7 +1441,7 @@
     odd, even, core, first, second, whole, near, far,
     left, right, wo, wi, inner, dout, acc,
     small_0, small_y, small_x, small_c, small_z, table_got, d0, d1, some, dconv, gated, pad, taps,
-    left_sem, right_sem, wo_sem, wi_sem, inner_sem, out_sem, part_sem, some_sem, taps_sem,
+    left_sem, right_sem, wo_sem, wi_sem, inner_sem, out_sem, part_sem, d1_sem, some_sem, taps_sem,
     core_send, core_recv, first_send, first_recv, second_send, second_recv,
     z_send, z_recv, small_send, small_recv, table_send, table_recv, dx_send, dx_recv, dx_sem, free_sem,
 ):
@@ -1258,7 +1464,6 @@
     barrier = pltpu.get_barrier_semaphore()
     for device in (to_c, to_x, to_y, to_1, to_2, {"seq": flipped_bit(place, 2)}):
         pl.semaphore_signal(barrier, inc=1, device_id=device, device_id_type=MESH)
-    pl.semaphore_wait(barrier, 6)
 
     def send(src, dst, send_sem, recv_sem, device):
         return pltpu.make_async_remote_copy(
@@ -1389,12 +1594,13 @@
             middle_gradient()
 
     def middle_gradient():
-        pltpu.make_async_copy(d2_ref, d1, some_sem).wait()
-        for rows in thin(t):
-            copy = pltpu.make_async_copy(first_ref.at[rows], some, some_sem)
-            copy.start()
-            copy.wait()
-            n, scale = normal(some[...])
+        pltpu.make_async_copy(d2_ref, d1, d1_sem).wait()
+        copies = [
+            pltpu.make_async_copy(first_ref.at[rows], some.at[i % 2], some_sem.at[i % 2]) for i, rows in enumerate(thin(t))
+        ]
+        for i, rows in enumerate(thin(t)):
+            copies[i].wait()
+            n, scale = normal(some[i % 2])
             du = acc[rows, :]
             value = d1[rows, :] + normal_back(du, n, scale, gain_ref[1:2, :])
             d1[rows, :] = value
@@ -1403,6 +1609,11 @@
             v = (HALF * value).astype(BF)
             dout[rows, :] = v
             small_0[row + 2 : row + 3, :] += total(v.astype(F32))
+            if i + 2 < len(copies):
+                copies[i + 2].start()
+
+    def first_rows(i):
+        return pltpu.make_async_copy(first_ref.at[pl.ds(128 * i, 128)], some.at[i], some_sem.at[i])
 
     def taps_copies(b):
         cols = pl.ds(pl.multiple_of(b * COLS, COLS), COLS)
@@ -1610,14 +1821,19 @@
     def part_copy(i):
         return pltpu.make_async_copy(part_ref.at[i], whole.at[N_CHUNK + i], part_sem.at[i])
 
+    def part_begin(i):
+        part_copy(i).wait()
+        z_begin(N_CHUNK + i)
+
     fetch(jnp.int32(0))
     wq_copy(0).start()
-    pltpu.make_async_copy(d2_ref, d1, some_sem).start()
+    pltpu.make_async_copy(d2_ref, d1, d1_sem).start()
+    for i in range(2):
+        first_rows(i).start()
     for copy in taps_copies(jnp.int32(0)):
         copy.start()
     for i in range(n_part):
         part_copy(i).start()
-    table_copy(0).start()
     wo_copy(0).start()
     inner_copy(0).start()
     small_0[...] = jnp.zeros_like(small_0)
@@ -1631,8 +1847,8 @@
             for q in range(4):
                 cols = slice((2 * j + dev) * r, (2 * j + dev + 1) * r)
                 small_0[49 + q : 50 + q, cols] = dbias_ref[j, :, (4 * dev + q) * r : (4 * dev + q + 1) * r]
-    for i in range(n_part):
-        part_copy(i).wait()
+    pl.semaphore_wait(barrier, 6)
+    table_copy(0).start()
     for c in range(AHEAD):
         make(jnp.int32(c))
 
@@ -1642,13 +1858,14 @@
         on(k - 2, 0, N_CHUNK, add_second)
         for stage in range(3):
             on(k - 3 - stage, 0, N_CHUNK, lambda c, stage=stage: z_stage(c, stage))
-        on(k, 0, n_part, lambda i: z_begin(N_CHUNK + i))
+        on(k, 0, n_part, part_begin)
         for stage in range(3):
             on(k - 1 - stage, 0, n_part, lambda i, stage=stage: z_stage(N_CHUNK + i, stage))
         make_back(k)
         on(k + AHEAD, 0, N_CHUNK, make)
         pl.when(k == LAST_IN)(input_gradient)
-        on(k - 1, 0, d // COLS, taps_columns)
+        for b in range(d // COLS):
+            pl.when(k == 4 + 2 * b)(lambda b=b: taps_columns(jnp.int32(b)))
         for step in range(5):
             pl.when(k == step)(lambda step=step: table_step(step))
             pl.when(k == LAST_IN + 1 + step)(lambda step=step: small_step(step))
@@ -1717,7 +1934,7 @@
             scr((5,) + table.shape, F32),
             scr((t, d), BF),
             scr((t, d), F32),
-            scr((128, d), F32),
+            scr((2, 128, d), F32),
             scr((t, COLS), F32),
             scr((t + 32, COLS), BF),
             scr((t + 32, COLS), F32),
@@ -1730,6 +1947,7 @@
             dma((z,)),
             dma((m,)),
             dma,
+            dma((2,)),
             dma((3,)),
             dma((k,)),
             dma((k,)),
@@ -1970,22 +2188,27 @@
         gated, halo, taps, jnp.stack([shift[13], gain[3], shift[3], shift[14]]), second, w_c, 7
     )
     inner_b, act_b, act_t_b, unit_t_b = ffn_in_forward(third, jnp.stack([gain[4], shift[4]]), bias[1], w_c, 0)
-    outputs, d4, sums_5 = out_last(third, act_b, w_d, 0, cotangent, jnp.stack([shift[7], gain[5], shift[5]]))
-    outputs = from_pairs(outputs, place)
-
-    dinner, dout, dbias_b, sums_7 = ffn_hidden_back(d4, inner_b, w_d, 0)
+    outputs, d4, dout, sums_5 = out_last(third, act_b, w_d, 0, cotangent, jnp.stack([shift[7], gain[5], shift[5]]))
+
     g_out_b = weight_grad(act_t_b, dout, n, 4, 0, True)
-    g_in_b = weight_grad(unit_t_b, after(dinner, g_out_b), n, 4, 0, False)
     part_out_b = lax.psum_scatter(g_out_b, "fsdp", scatter_dimension=0, tiled=False)
+    dinner, dout, dbias_b, sums_7 = ffn_hidden_back(after(dout, g_out_b), inner_b, w_d, 0)
+    g_in_b = weight_grad(unit_t_b, dinner, n, 4, 0, False)
     part_in_b = lax.psum_scatter(g_in_b, "fsdp", scatter_dimension=0, tiled=False)
     dinner = after(dinner, g_in_b)
-    d3, sums_4 = norm_input_back(d4, dinner, third, w_c, 0, gain[4:5])
-    d3, outputs = lax.optimization_barrier((d3, outputs))
-    dconv, dout_3, sums_3 = conv_out_back(d3, conv, w_c, 7, jnp.stack([gain[3], shift[3]]))
-    follow = lax.ppermute(dconv[:32], "seq", [(j, i) for i, j in pairs])
-    d2, dout_2, dglu, mine, other, sums_2 = mid_back(
-        odd_word, dconv, follow, taps, val, sig, second, d3, w_c, 4, 5, gain[2:3]
-    )
+    if cubed:
+        vec = jnp.stack([gain[4], gain[3], shift[3], gain[2]])
+        dconv, dout_3, d2, dout_2, dglu, mine, other, sums_4, sums_3, sums_2, outputs = middle_back(
+            d4, dinner, third, conv, val, sig, second, w_c, taps, vec, outputs
+        )
+    else:
+        outputs = from_pairs(outputs, place)
+        d3, sums_4 = norm_input_back(d4, dinner, third, w_c, 0, gain[4:5])
+        dconv, dout_3, sums_3 = conv_out_back(d3, conv, w_c, 7, jnp.stack([gain[3], shift[3]]))
+        follow = lax.ppermute(dconv[:32], "seq", [(j, i) for i, j in pairs])
+        d2, dout_2, dglu, mine, other, sums_2 = mid_back(
+            odd_word, dconv, follow, taps, val, sig, second, d3, w_c, 4, 5, gain[2:3]
+        )
     if cubed:
         dqkv, dtable, share_out_b = attend_back(heads, probs, wide, mine, other, part_out_b)
     else:

time: 682 us -> 658 us (0.965)
  starting transfers between devices: 20.9 us -> 5.43 us
    pallas_call x0 -> x1, Pallas kernels: none -> 48 us  [middle_back(): pl.pallas_call(middle_kernel, grid=(7,), in_specs=[pl.BlockSpec((t, d), l...]
    pallas_call x11 -> x8, Pallas kernels: 135 us -> 97.1 us  [call(): pl.pallas_call(kernel, grid=grid, in_specs=[spec(a.shape, b, w) for a, b,...]
    ppermute x3 -> x0, starting transfers between devices: 15.6 us -> none  [the longest x1 12.8 us: from_pairs(): lax.ppermute(jnp.where(place == 1, first, second), 'seq', [(1, 2), (2, 1)])]
    pallas_call x1, Pallas kernels: 195 us -> 188 us  [last_reduced(): pl.pallas_call(last_kernel, in_specs=[vmem] * 8 + [anywhere] * 20, out_sp...]
  transfers between devices with their start and end apart: 11 -> 8, of which waited for: 6 -> 6; matrix products, arithmetic and copies ran while one was open for 3% -> 2% of each run, Pallas kernels for 49% -> 53%
where the time goes in v4:
time: 658 us; the launch traced here: 649 us
  Pallas kernels  563 us (86%)
  waiting for transfers between devices  40.2 us (6%)
  between operations  15.9 us (2%)
  local copies, waits for them, and re-layouts  15.7 us (2%)
  other arithmetic  9.16 us (1%)
    pallas_call x1, Pallas kernels, last_reduced(): pl.pallas_call(last_kernel, in_specs=[vmem] * 8 + [anywhere] * 20, out_sp...  188 us
    pallas_call x8, Pallas kernels, call(): pl.pallas_call(kernel, grid=grid, in_specs=[spec(a.shape, b, w) for a, b,...  97.1 us
    pallas_call x1, Pallas kernels, first_forward(): pl.pallas_call(first_kernel, grid=(k,), in_specs=[anywhere] * 2 + [whole(...  82.6 us
    pallas_call x1, Pallas kernels, attend_back(): pl.pallas_call(functools.partial(bwd_kernel, with_part), grid=(pairs, STE...  81.3 us
    pallas_call x1, Pallas kernels, attend(): pl.pallas_call(fwd_kernel, grid=(pairs, STEPS), in_specs=[pl.BlockSpec(me...  58.6 us
    pallas_call x1, Pallas kernels, middle_back(): pl.pallas_call(middle_kernel, grid=(7,), in_specs=[pl.BlockSpec((t, d), l...  48 us
    ppermute x1, waiting for transfers between devices, to_pairs(): lax.ppermute(jnp.where(place % 2 == 0, two, one), 'seq', [(0, 2), (1, 0),...  13.5 us
  transfers between devices with their start and end apart: 8, of which 6 were waited for; matrix products, arithmetic and copies ran while one was open for 2% of the time, Pallas kernels for 53%

profile of v4, /device:TPU:0, one launch (start us, length us, event | category | flops | bytes accessed | tf_op | source)
XLA Modules:
  0.0 649.4 jit_solution(11842525646591659874)
XLA Ops:
  7.2 2.7 fusion.7
  10.0 1.4 pad_maximum_fusion
  13.6 82.6 %first.1 = (bf16[512,4096]{1,0:T(8,128)(2,1)}, bf16[512,4096]{1,0:T(8,128)(2,1)}, bf16[4096,512]{1,0:T(8,128)(2,1)}, bf16[1024,512]{1,0:T(8,128)(2,1)}, bf16[512...) custom-call(bf16[2,256,1024]{2,1,0:T(8,128)(2,1)} %x_ref.1, ...), custom_call_target="tpu_custom_call" | custom-call | flops 30000001024 | bytes 100000000 | tf_op jit(solution)/shard_map/first/pallas_call | solution.py:1175
  97.2 1.6 collective-permute-start
  100.1 13.5 %collective-permute-done.1 = bf16[256,1024]{1,0:T(8,128)(2,1)} collective-permute-done((bf16[256,1024]{1,0:T(8,128)(2,1)}, bf16[256,1024]{1,0:T(8,128)(2,1)}, u32[]{:S(2)}, u32[]{:S(2)}) %collective-permute-start.1) | collective-permute-done | bytes 524320 | tf_op jit(solution)/shard_map/ppermute | solution.py:2097
  115.9 4.3 all-gather.7.cloned.1.call-done
  124.8 17.2 %out_qkv.1 = (f32[512,1024]{1,0:T(8,128)}, bf16[1024,512]{1,0:T(8,128)(2,1)}, bf16[4,3,512,128]{3,2,1,0:T(8,128)(2,1)}, bf16[4,3,512,128]{3,2,1,0:T(8,128)(2,1)}) custom-call(s32[1]{0:T(128)} %bitcast.odd_ref, bf16[512,1024]{1,0:T(8,128)(2,1)} %get-tuple-element.84.x_ref, bf16[512,4096]{1,0:T(8,128)(2,1)} %get-tuple-element.85.act_ref, ...), custom_call_target="tpu_custom_call" | custom-call | flops 7516192768 | bytes 25165824 | tf_op jit(solution)/shard_map/out_qkv/pallas_call | solution.py:394
  142.0 58.6 %attend_fwd.1 = (bf16[8,1024,1024]{2,1,0:T(8,128)(2,1)}, bf16[4,3,1024,128]{3,2,1,0:T(8,128)(2,1)}, bf16[512,1024]{1,0:T(8,128)(2,1)}) custom-call(s32[1]{0:T(128)} %bitcast.16.len_ref, bf16[128,512]{1,0:T(8,128)(2,1)} %maximum_maximum_fusion.wide_ref, bf16[128,128]{1,0:T(8,128)(2,1)} %pad_maximum_fusion.3.ends_ref, ...), custom_call_target="tpu_custom_call" | custom-call | flops 40000000000 | bytes 120000000 | tf_op jit(solution)/shard_map/attend_fwd/pallas_call | solution.py:316
  200.6 11.7 %all-gather.9.cloned.1.call-done = bf16[64,128,1024]{2,1,0:T(8,128)(2,1)} async-done(((bf16[8,128,1024]{2,1,0:T(8,128)(2,1)}), bf16[64,128,1024]{2,1,0:T(8,128)(2,1)}) %all-gather.9.cloned.1.call-update) | async-done | bytes 16777232 | tf_op jit(solution)/shard_map/all_gather | solution.py:2176
  216.0 11.1 %mid.1 = (f32[512,1024]{1,0:T(8,128)}, bf16[1024,512]{1,0:T(8,128)(2,1)}, bf16[1024,512]{1,0:T(8,128)(2,1)}, bf16[512,1024]{1,0:T(8,128)(2,1)}, bf16[512,1024]{1,0:T(8,128)(2,1)}, /*index=5*/bf16[512,1024]{1,0:T(8,128)(2,1)}) custom-call(f32[512,1024]{1,0:T(8,128)} %get-tuple-element.87.first_ref, bf16[512,1024]{1,0:T(8,128)(2,1)} %get-tuple-element.90.mixed_ref, ...), custom_call_target="tpu_custom_call" | custom-call | flops 3221225472 | bytes 16777216 | tf_op jit(solution)/shard_map/mid/pallas_call | solution.py:394
  227.9 3.3 collective-permute-start.2
  233.8 13.7 %conv.1 = (f32[512,1024]{1,0:T(8,128)}, bf16[1024,512]{1,0:T(8,128)(2,1)}, f32[512,1024]{1,0:T(8,128)}) custom-call(bf16[512,1024]{1,0:T(8,128)(2,1)} %get-tuple-element.93.gated_ref, bf16[32,1024]{1,0:T(8,128)(2,1)} %copy-done.11, f32[31,1024]{1,0:T(8,128)} %bitcast.124, f32[4,1024]{1,0:T(4,128)} %get-tuple-element.228.vec_ref, ...), custom_call_target="tpu_custom_call" | custom-call | flops 1073741824 | bytes 10485760 | tf_op jit(solution)/shard_map/conv/pallas_call | solution.py:394
  247.5 12.6 %ffn_in.1 = (bf16[512,4096]{1,0:T(8,128)(2,1)}, bf16[512,4096]{1,0:T(8,128)(2,1)}, bf16[4096,512]{1,0:T(8,128)(2,1)}, bf16[1024,512]{1,0:T(8,128)(2,1)}) custom-call(f32[512,1024]{1,0:T(8,128)} %get-tuple-element.95.x_ref.third_in, f32[2,1024]{1,0:T(2,128)} %pad_maximum_fusion.9.vec_ref, f32[4,1,1024]{2,1,0:T(1,128)} %reshape_squeeze.10.bias_ref, ...), custom_call_target="tpu_custom_call" | custom-call | flops 4294967296 | bytes 20971520 | tf_op jit(solution)/shard_map/ffn_in/pallas_call | solution.py:394
  260.2 9.0 %all-gather.11.cloned.1.call-done = bf16[32,128,1024]{2,1,0:T(8,128)(2,1)} async-done(((bf16[4,128,1024]{2,1,0:T(8,128)(2,1)}), bf16[32,128,1024]{2,1,0:T(8,128)(2,1)}) %all-gather.11.cloned.1.call-update) | async-done | bytes 8388624 | tf_op jit(solution)/shard_map/all_gather | solution.py:2181
  269.1 12.7 %out_last.1 = (bf16[512,1024]{1,0:T(8,128)(2,1)}, f32[512,1024]{1,0:T(8,128)}, bf16[512,1024]{1,0:T(8,128)(2,1)}, f32[8,1024]{1,0:T(8,128)}) custom-call(f32[512,1024]{1,0:T(8,128)} %get-tuple-element.95.x_ref.third_in, bf16[512,4096]{1,0:T(8,128)(2,1)} %get-tuple-element.96.act_ref, bf16[8,4,128,1024]{3,2,1,0:T(8,128)(2,1)} %bitcast.130, ...), custom_call_target="tpu_custom_call" | custom-call | flops 4294967296 | bytes 18874368 | tf_op jit(solution)/shard_map/out_last/pallas_call | solution.py:394
  281.9 8.8 %weight_grad.2 = bf16[8,4,128,1024]{3,2,1,0:T(8,128)(2,1)} custom-call(bf16[4096,512]{1,0:T(8,128)(2,1)} %get-tuple-element.99.left_ref, bf16[512,1024]{1,0:T(8,128)(2,1)} %get-tuple-element.100.right_ref.d_ref), custom_call_target="tpu_custom_call" | custom-call | flops 4294967296 | bytes 13631488 | tf_op jit(solution)/shard_map/weight_grad/pallas_call | solution.py:394
  290.7 11.7 %ffn_hidden_back.1 = (bf16[512,4096]{1,0:T(8,128)(2,1)}, bf16[512,1024]{1,0:T(8,128)(2,1)}, f32[4,1,1024]{2,1,0:T(1,128)}, f32[8,1024]{1,0:T(8,128)}) custom-call(bf16[512,1024]{1,0:T(8,128)(2,1)} %get-tuple-element.100.right_ref.d_ref, bf16[512,4096]{1,0:T(8,128)(2,1)} %get-tuple-element.101.inner_ref, bf16[8,4,128,1024]{3,2,1,0:T(8,128)(2,1)} %bitcast.131), custom_call_target="tpu_custom_call" | custom-call | flops 4294967296 | bytes 16777216 | tf_op jit(solution)/shard_map/ffn_hidden_back/pallas_call | solution.py:394
  302.4 9.2 %weight_grad.3 = bf16[8,4,128,1024]{3,2,1,0:T(8,128)(2,1)} custom-call(bf16[1024,512]{1,0:T(8,128)(2,1)} %get-tuple-element.103.left_ref, bf16[512,4096]{1,0:T(8,128)(2,1)} %get-tuple-element.104.right_ref.g_ref), custom_call_target="tpu_custom_call" | custom-call | flops 4294967296 | bytes 13631488 | tf_op jit(solution)/shard_map/weight_grad/pallas_call | solution.py:394
  311.7 1.4 slice.324.wide_ref
  313.7 48.0 %middle_back.1 = (f32[512,1024]{1,0:T(8,128)}, bf16[512,1024]{1,0:T(8,128)(2,1)}, bf16[4,512,128]{2,1,0:T(8,128)(2,1)}, bf16[4,512,128]{2,1,0:T(8,128)(2,1)}, f3...) custom-call(bf16[512,4096]{1,0:T(8,128)(2,1)} %get-tuple-element.104, ...), custom_call_target="tpu_custom_call" | custom-call | flops 40000000000 | bytes 120000000 | tf_op jit(solution)/shard_map/middle_back/pallas_call | solution.py:1395
  362.1 81.3 %attend_bwd.1 = (bf16[512,3072]{1,0:T(8,128)(2,1)}, f32[128,128]{1,0:T(8,128)}, bf16[4,128,1024]{2,1,0:T(8,128)(2,1)}) custom-call(bf16[4,3,1024,128]{3,2,1,0:T(8,128)(2,1)} %get-tuple-element.111.heads_ref, bf16[8,1024,1024]{2,1,0:T(8,128)(2,1)} %get-tuple-element.112.p_ref, bf16[128,128]{1,0:T(8,128)(2,1)} %slice.324.wide_ref, ...), custom_call_target="tpu_custom_call" | custom-call | flops 49999998976 | bytes 150000000 | tf_op jit(solution)/shard_map/attend_bwd/pallas_call | solution.py:335
  443.4 187.9 %last.1 = (bf16[15,128,1024]{2,1,0:T(8,128)(2,1)}, bf16[4,128,1024]{2,1,0:T(8,128)(2,1)}, f32[64,128]{1,0:T(8,128)}, f32[128,128]{1,0:T(8,128)}, bf16[2,256,1024]{2,1,0:T(8,128)(2,1)}) custom-call(f32[2,1024]{1,0:T(2,128)} %slice_bitcast_fusion.10.gain_ref, f32[128,128]{1,0:T(8,128)} %get-tuple-element.115.table_ref, ...), custom_call_target="tpu_custom_call" | custom-call | flops 99999997952 | bytes 400000000 | tf_op jit(solution)/shard_map/last/pallas_call | solution.py:1902
  631.3 7.7 %finish.1 = (f32[2,128,4096]{2,1,0:T(8,128)}, f32[2,4,128,1024]{3,2,1,0:T(8,128)}, f32[3,128,1024]{2,1,0:T(8,128)}, f32[128,1024]{1,0:T(8,128)}, f32[128,2048]{1...) custom-call(bf16[15,128,1024]{2,1,0:T(8,128)(2,1)} %get-tuple-elemen, ...), custom_call_target="tpu_custom_call" | custom-call | bytes 18000000 | tf_op jit(solution)/shard_map/finish/pallas_call | solution.py:2040
  639.0 1.6 copy.35
  (83 shorter events, 20.1 us)
Async XLA Ops:
  7.2 2.8 copy-start.5
  7.2 113.0 %all-gather.7.cloned.1.call-start = ((), (), s32[]{:S(2)}) async-start(), calls=%async_computation.4 | async-start | bytes 16515072 | tf_op jit(solution)/shard_map/all_gather | solution.py:2150
  10.0 2.3 copy-start.2
  11.4 200.8 %all-gather.9.cloned.1.call-start = ((), (), s32[]{:S(2)}) async-start(), calls=%async_computation.5 | async-start | bytes 18874368 | tf_op jit(solution)/shard_map/all_gather | solution.py:2176
  13.6 82.6 %copy-start = (bf16[2,256,1024]{2,1,0:T(8,128)(2,1)S(1)}, bf16[2,256,1024]{2,1,0:T(8,128)(2,1)}, u32[]{:S(2)}) copy-start(bf16[2,256,1024]{2,1,0:T(8,128)(2,1)} %param.27) | copy-start | bytes 3145732
  96.2 2.8 copy-start.7
  96.2 2.8 copy-start.6
  97.2 2.8 copy-start.8
  97.2 2.8 collective-permute-start
  98.8 14.7 %collective-permute-start.1 = (bf16[256,1024]{1,0:T(8,128)(2,1)}, bf16[256,1024]{1,0:T(8,128)(2,1)}, u32[]{:S(2)}, u32[]{:S(2)}) collective-permute-start(bf16[256,1024]{1,0:T(8,128)(2,1)} %get-tuple-element.201), channel_id=1, source_target_pairs={{0,16},{8,0},{16,24},{24,8},{1,17},{9,1},{17,25},{25,9},{2,18},{10... | collective-permute-start | bytes 1572872 | tf_op jit(solution)/shard_map/ppermute | solution.py:2097
  100.0 15.9 %copy-start.1 = (bf16[8,128,1024]{2,1,0:T(8,128)(2,1)}, bf16[8,128,1024]{2,1,0:T(8,128)(2,1)S(1)}, u32[]{:S(2)}) copy-start(bf16[8,128,1024]{2,1,0:T(8,128)(2,1)S(1)} %bitcast_dynamic-update-slice_fusion) | copy-start | bytes 6291460
  114.9 5.4 copy-start.12
  114.9 7.3 %copy-start.10 = (bf16[73,64]{0,1:T(8,128)(2,1)S(1)}, bf16[73,64]{0,1:T(8,128)(2,1)}, u32[]{:S(2)}) copy-start(bf16[73,64]{0,1:T(8,128)(2,1)} %param.26) | copy-start | bytes 28036
  114.9 7.6 %copy-start.9 = (bf16[8,64,128]{2,1,0:T(8,128)(2,1)S(1)}, bf16[8,64,128]{2,1,0:T(8,128)(2,1)}, u32[]{:S(2)}) copy-start(bf16[8,64,128]{2,1,0:T(8,128)(2,1)} %get-tuple-element.86) | copy-start | bytes 393220
  120.2 148.9 %all-gather.11.cloned.1.call-start = ((), (), s32[]{:S(2)}) async-start(), calls=%async_computation.6 | async-start | bytes 9437184 | tf_op jit(solution)/shard_map/all_gather | solution.py:2181
  212.3 149.8 %reduce-scatter.3.cloned.1.call-start = ((), (), s32[]{:S(2)}) async-start(), calls=%async_computation.2 | async-start | bytes 9437184 | tf_op jit(solution)/shard_map/reduce_scatter | solution.py:2194
  227.9 5.2 collective-permute-start.2
  233.2 0.6 copy-start.11
  290.7 152.7 %reduce-scatter.5.cloned.1.call-start = ((), (), s32[]{:S(2)}) async-start(), calls=%async_computation.3 | async-start | bytes 9437184 | tf_op jit(solution)/shard_map/reduce_scatter | solution.py:2197
  631.3 9.3 %copy-start.3 = (bf16[2,256,1024]{2,1,0:T(8,128)(2,1)S(1)}, bf16[2,256,1024]{2,1,0:T(8,128)(2,1)}, u32[]{:S(2)}) copy-start(bf16[2,256,1024]{2,1,0:T(8,128)(2,1)} %get-tuple-element.244) | copy-start | bytes 3145732
  639.0 2.6 copy-start.4
Sparse Core Ops, SparseCore 0:
  11.5 108.6 all-gather.6
  122.7 89.5 all-gather.8
  214.7 54.3 all-gather.10
  290.8 71.2 reduce-scatter.2
  365.8 71.2 reduce-scatter.4

commit v5 on v4

--- a/solution.py
+++ b/solution.py
@@ -80,27 +80,30 @@
     masked=jnp.where(t>=len_ref[0],-1e30,0.0)
     ext=jnp.where(c<2,left,jnp.where(c<4,right,jnp.where(c==4,masked,0.0)))
     kx_ref[:,128:256]=ext.astype(BF)
-    outs=[]
+    qhs,qxs=[],[]
     for h in range(2):
         head=(lane<64) if h==0 else (lane>=64)
         qh=jnp.where(head,q2,jnp.zeros_like(q2))
         ends=dot(qh,ends_ref[...],1,0)
         hi=ends.astype(BF).astype(F32)
         qx=jnp.where((lane==0)|(lane==2),hi,jnp.where((lane==1)|(lane==3),ends-hi,jnp.where(lane==4,1.0,0.0))).astype(BF)
-        s_ref[:,PADL:PADL+n]=dot(jnp.concatenate([qh,qx],axis=1),kx_ref[...],1,1)
-        wide=dot(qh,wide_ref[...],1,0)
+        qhs.append(qh); qxs.append(jnp.concatenate([qh,qx],axis=1))
+    for h in range(2):
+        s_ref[h,:,PADL:PADL+n]=dot(qxs[h],kx_ref[...],1,1)
+    j=band_offset()
+    w=pl.ds(i0,WIN)
+    for h in range(2):
+        wide=dot(qhs[h],wide_ref[...],1,0)
         band=pltpu.roll(wide,LEFT,1,stride=1,stride_axis=0)
-        j=band_offset()
         band=jnp.where(j>=LEFT+RIGHT,wide[:,LEFT+RIGHT:LEFT+RIGHT+1],band)
-        w=pl.ds(i0,WIN)
-        s_ref[:,w]=s_ref[:,w]+band
-        s=s_ref[:,PADL:PADL+n]
+        s_ref[h,:,w]=s_ref[h,:,w]+band
+    for h in range(2):
+        s=s_ref[h,:,PADL:PADL+n]
         m=jnp.max(s,axis=1,keepdims=True)
         e=jnp.exp(s-m)
         z=jnp.sum(e,axis=1,keepdims=True)
-        p=(e*(1.0/z)).astype(BF)
-        p_ref[h]=p
-        outs.append(dot(p,v2,1,0))
+        p_ref[h]=(e*(1.0/z)).astype(BF)
+    outs=[dot(p_ref[h],v2,1,0) for h in range(2)]
     out=jnp.where(lane<64,outs[0],outs[1]).astype(BF)
     @pl.when(step<2)
     def _():
@@ -203,8 +206,9 @@
             for i in range(n_part):
                 part_copy(i).start()
         dea[...]=jnp.zeros_like(dea)
-        ds_ref[:,0:PADL]=jnp.zeros((RB,PADL),F32)
-        ds_ref[:,PADL+n:]=jnp.zeros((RB,ds_ref.shape[1]-PADL-n),F32)
+        for h in range(2):
+            ds_ref[h,:,0:PADL]=jnp.zeros((RB,PADL),F32)
+            ds_ref[h,:,PADL+n:]=jnp.zeros((RB,ds_ref.shape[2]-PADL-n),F32)
     @pl.when(step==0)
     def _():
         load(pair).wait()
@@ -237,24 +241,26 @@
     c=lanes((n,128))
     left=(t<i0-128).astype(F32)
     kx_ref[:,128:256]=jnp.where(c==0,left,jnp.where(c==1,1.0,0.0)).astype(BF)
-    dqs=[]
+    heads=[]
     for h in range(2):
         head=(lane<64) if h==0 else (lane>=64)
-        doh=jnp.where(head,do2,jnp.zeros_like(do2))
-        qh=jnp.where(head,q2,jnp.zeros_like(q2))
-        p=p_ref[h]
-        dp=dot(doh,v2,1,1)
-        pf=p.astype(F32)
-        d=jnp.sum(pf*dp,axis=1,keepdims=True)
-        dsf=pf*(dp-d)
-        ds=dsf.astype(BF)
-        ds_ref[:,PADL:PADL+n]=ds.astype(F32)
-        dva[...]+=dot(doh,p,0,0)
-        dka[...]+=dot(qh,ds,0,0)
-        dqx=dot(ds,kx_ref[...],1,0)
-        dq,sums=dqx[:,0:128],dqx[:,128:256]
-        win=ds_ref[:,pl.ds(i0,WIN)]
-        j=band_offset()
+        heads.append((jnp.where(head,do2,jnp.zeros_like(do2)),jnp.where(head,q2,jnp.zeros_like(q2))))
+    dps=[dot(doh,v2,1,1) for doh,_ in heads]
+    dss=[]
+    for h in range(2):
+        pf=p_ref[h].astype(F32)
+        d=jnp.sum(pf*dps[h],axis=1,keepdims=True)
+        dsf=pf*(dps[h]-d)
+        ds_ref[h,:,PADL:PADL+n]=dsf
+        dss.append(dsf.astype(BF))
+    dva[...]+=dot(heads[0][0],p_ref[0],0,0)+dot(heads[1][0],p_ref[1],0,0)
+    dka[...]+=dot(heads[0][1],dss[0],0,0)+dot(heads[1][1],dss[1],0,0)
+    dqxs=[dot(ds,kx_ref[...],1,0) for ds in dss]
+    j=band_offset()
+    drels=[]
+    for h in range(2):
+        sums=dqxs[h][:,128:256]
+        win=ds_ref[h,:,pl.ds(i0,WIN)]
         inleft=jnp.sum(jnp.where(j<=0,win,0.0),axis=1,keepdims=True)
         drel=jnp.concatenate([win[8*g:8*g+8,LEFT+8*g:LEFT+8*g+128] for g in range(RB//8)],axis=0)
         for bit in (1,2,4):
@@ -263,10 +269,9 @@
         bandsum=jnp.sum(drel,axis=1,keepdims=True)
         l=sums[:,0:1]+inleft
         r=sums[:,1:2]-l-bandsum
-        drel=jnp.where(lane==0,l,jnp.where(lane==LEFT+RIGHT,r,drel)).astype(BF)
-        dq=dq+dot(drel,wide_ref[...],1,1)
-        dqs.append(dq)
-        dea[...]+=dot(drel,qh,0,0)
+        drels.append(jnp.where(lane==0,l,jnp.where(lane==LEFT+RIGHT,r,drel)).astype(BF))
+    dqs=[dqxs[h][:,0:128]+dot(drels[h],wide_ref[...],1,1) for h in range(2)]
+    dea[...]+=dot(drels[0],heads[0][1],0,0)+dot(drels[1],heads[1][1],0,0)
     dq=(jnp.where(lane<64,dqs[0],dqs[1])*HEAD_DIM**-0.5).astype(BF)
     @pl.when(turned<2)
     def _():
@@ -318,7 +323,7 @@
         in_specs=[pl.BlockSpec(memory_space=pltpu.SMEM),whole(128,WIN),whole(128,128),anywhere,anywhere],
         out_specs=[pl.BlockSpec((2,RB,n),lambda a,b:(a,b,0)),pl.BlockSpec((1,3,n,128),lambda a,b:(a,0,0,0)),whole(own,2*own)],
         out_shape=[jax.ShapeDtypeStruct((2*pairs,n,n),BF),jax.ShapeDtypeStruct((pairs,3,n,128),BF),jax.ShapeDtypeStruct((own,2*own),BF)],
-        scratch_shapes=[pltpu.VMEM((RB,PADL+n+256),F32),pltpu.VMEM((n,256),BF),pltpu.VMEM((pairs,3,n,128),BF),pltpu.VMEM((own,2*own),BF),pltpu.VMEM((pairs,2,RB,128),BF),
+        scratch_shapes=[pltpu.VMEM((2,RB,PADL+n+256),F32),pltpu.VMEM((n,256),BF),pltpu.VMEM((pairs,3,n,128),BF),pltpu.VMEM((own,2*own),BF),pltpu.VMEM((pairs,2,RB,128),BF),
             dma((pairs,)),dma((pairs,)),dma((pairs,)),dma((pairs,2)),dma((pairs,2))],
         compiler_params=pltpu.CompilerParams(vmem_limit_bytes=58<<20,collective_id=1,has_side_effects=True),
         cost_estimate=pl.CostEstimate(flops=40_000_000_000,bytes_accessed=120_000_000,transcendentals=0),
@@ -337,7 +342,7 @@
         in_specs=[pl.BlockSpec((1,3,n,128),lambda a,b:(a,0,0,0)),pl.BlockSpec((2,RB,n),lambda a,b:(a,jnp.where(a==0,lax.rem(b+2,STEPS),b),0)),whole(128,128),anywhere,anywhere]+[anywhere]*with_part,
         out_specs=[whole(own,6*own),whole(128,128)]+[anywhere]*with_part,
         out_shape=[jax.ShapeDtypeStruct((own,6*own),BF),jax.ShapeDtypeStruct((128,128),F32)]+([jax.ShapeDtypeStruct(part.shape,BF)] if with_part else []),
-        scratch_shapes=[pltpu.VMEM((RB,PADL+n+256),F32),pltpu.VMEM((n,256),BF),pltpu.VMEM((128,n),F32),pltpu.VMEM((128,n),F32),pltpu.VMEM((128,128),F32),
+        scratch_shapes=[pltpu.VMEM((2,RB,PADL+n+256),F32),pltpu.VMEM((n,256),BF),pltpu.VMEM((128,n),F32),pltpu.VMEM((128,n),F32),pltpu.VMEM((128,128),F32),
             pltpu.VMEM((pairs,n,128),BF),pltpu.VMEM((own,6*own),BF),pltpu.VMEM((pairs,2,RB,128),BF),pltpu.VMEM((pairs,2,own,128),BF),
             dma((pairs,)),dma((pairs,)),dma((pairs,)),dma((pairs,2)),dma((pairs,2)),dma((pairs,2)),dma((pairs,2))]+extra,
         compiler_params=pltpu.CompilerParams(vmem_limit_bytes=58<<20,collective_id=2,has_side_effects=True),
@@ -578,6 +583,8 @@
 
 ROWS = 32
 COLS = 256
+FIR_ROWS = 64
+FIR_COLS = 128
 
 
 def shifted(window, b):
@@ -586,12 +593,12 @@
 
 def fir(pad, taps, offset, count, width, start, write, turned=False):
     reach = taps.shape[0]
-    for c in range(0, width, COLS):
-        cols = slice(c, c + COLS)
+    for c in range(0, width, FIR_COLS):
+        cols = slice(c, c + FIR_COLS)
 
         def body(i, _):
-            base = pl.multiple_of(i * ROWS, ROWS)
-            window = pad[pl.ds(base, ROWS + 32), cols]
+            base = pl.multiple_of(i * FIR_ROWS, FIR_ROWS)
+            window = pad[pl.ds(base, FIR_ROWS + 32), cols]
             acc = start(cols)
             for b in range(8):
                 sh = shifted(window, b)
@@ -599,11 +606,11 @@
                     m = 8 * a + b - offset
                     if 0 <= m < reach:
                         tap = reach - 1 - m if turned else m
-                        acc = acc + taps[tap : tap + 1, cols] * sh[8 * a : 8 * a + ROWS]
-            write(pl.ds(base, ROWS), cols, acc)
+                        acc = acc + taps[tap : tap + 1, cols] * sh[8 * a : 8 * a + FIR_ROWS]
+            write(pl.ds(base, FIR_ROWS), cols, acc)
             return 0
 
-        lax.fori_loop(0, count // ROWS, body, 0)
+        lax.fori_loop(0, count // FIR_ROWS, body, 0)
 
 
 def conv_kernel(gated_ref, halo_ref, taps_ref, vec_ref, second_ref, w_ref, conv_ref, act_t_ref, third_ref, pad):
@@ -615,7 +622,7 @@
     def write(rows, cols, acc):
         conv_ref[rows, cols] = acc
 
-    fir(pad, taps_ref, 2, t, d, lambda cols: jnp.broadcast_to(vec_ref[0:1, cols], (ROWS, COLS)), write)
+    fir(pad, taps_ref, 2, t, d, lambda cols: jnp.broadcast_to(vec_ref[0:1, cols], (FIR_ROWS, FIR_COLS)), write)
     w = flat(w_ref)
     for rows in cuts(t):
         n, _ = normal(conv_ref[rows, :])
@@ -872,7 +879,7 @@
             dgate = dval * val_ref[rows, cols].astype(F32) * (1.0 - sig)
             dglu_ref[rows, cols.start + d : cols.stop + d] = dgate.astype(BF)
 
-        fir(pad, taps_ref, 0, t, d, lambda cols: jnp.zeros((ROWS, COLS), F32), write, turned=True)
+        fir(pad, taps_ref, 0, t, d, lambda cols: jnp.zeros((FIR_ROWS, FIR_COLS), F32), write, turned=True)
         sums_ref[...] = jnp.zeros_like(sums_ref)
         for rows in cuts(t):
             sums_ref[0:1, :] += total(dglu_ref[rows, :d].astype(F32))
@@ -1339,7 +1346,7 @@
             dgate = dval * val_ref[rows, cols].astype(F32) * (1.0 - sig)
             dglu_ref[rows, cols.start + d : cols.stop + d] = dgate.astype(BF)
 
-        fir(pad, taps_ref, 0, t, d, lambda cols: jnp.zeros((ROWS, COLS), F32), write, turned=True)
+        fir(pad, taps_ref, 0, t, d, lambda cols: jnp.zeros((FIR_ROWS, FIR_COLS), F32), write, turned=True)
         for rows in cuts(t):
             sums_2_ref[0:1, :] += total(dglu_ref[rows, :d].astype(F32))
             sums_2_ref[1:2, :] += total(dglu_ref[rows, d:].astype(F32))
@@ -1858,9 +1865,10 @@
         on(k - 2, 0, N_CHUNK, add_second)
         for stage in range(3):
             on(k - 3 - stage, 0, N_CHUNK, lambda c, stage=stage: z_stage(c, stage))
-        on(k, 0, n_part, part_begin)
-        for stage in range(3):
-            on(k - 1 - stage, 0, n_part, lambda i, stage=stage: z_stage(N_CHUNK + i, stage))
+        for h in range(2):
+            on(2 * k + h, 0, n_part, part_begin)
+            for stage in range(3):
+                on(2 * (k - 1 - stage) + h, 0, n_part, lambda i, stage=stage: z_stage(N_CHUNK + i, stage))
         make_back(k)
         on(k + AHEAD, 0, N_CHUNK, make)
         pl.when(k == LAST_IN)(input_gradient)
@@ -1979,7 +1987,9 @@
 PLACE = {item: i for i, item in enumerate(ORDER)}
 
 
-def finish_kernel(n_tap, main, in_b, out_b, small, table, g_in, g_out, g_qkv, g_attn, g_conv_in, g_conv_out, g_taps, g_gain, g_shift, g_bias, g_table):
+def finish_kernel(n_tap, main, in_b, out_b, small, table, result, dx, g_in, g_out, g_qkv, g_attn, g_conv_in, g_conv_out, g_taps, g_gain, g_shift, g_bias, g_table, g_result, g_dx):
+    g_result[...] = result[...]
+    g_dx[...] = dx[...]
     d = main.shape[-1]
 
     def of(name, unit):
@@ -2013,7 +2023,7 @@
     g_table[...] = table[0:k, 0:h] + table[0:k, h : 2 * h]
 
 
-def finished(main, in_b, out_b, small, table, n_tap, table_shape):
+def finished(main, in_b, out_b, small, table, result, dx, n_tap, table_shape):
     k, r, d = main.shape
     w = small.shape[1]
     step = min(r, 32)
@@ -2037,16 +2047,18 @@
         ((2, 4 * w), whole(2, 4 * w)),
         (table_shape, whole(*table_shape)),
     ]
+    count = result.shape[1] // (r // step)
+    tokens = pl.BlockSpec((result.shape[0], count, d), lambda i: (0, i, 0))
     return pl.pallas_call(
         functools.partial(finish_kernel, n_tap),
         grid=(r // step,),
-        in_specs=[rows(k), rows(4), rows(4), whole(*small.shape), whole(*table.shape)],
-        out_specs=[b for _, b in outs],
-        out_shape=[jax.ShapeDtypeStruct(s, F32) for s, _ in outs],
+        in_specs=[rows(k), rows(4), rows(4), whole(*small.shape), whole(*table.shape), tokens, tokens],
+        out_specs=[b for _, b in outs] + [tokens, tokens],
+        out_shape=[jax.ShapeDtypeStruct(s, F32) for s, _ in outs] + [jax.ShapeDtypeStruct(result.shape, BF)] * 2,
         compiler_params=pltpu.CompilerParams(vmem_limit_bytes=VMEM),
         cost_estimate=pl.CostEstimate(flops=0, bytes_accessed=18_000_000, transcendentals=0),
         name="finish",
-    )(main, in_b, out_b, small, table)
+    )(main, in_b, out_b, small, table, result, dx)
 
 
 def xor_route(axis, mask):
@@ -2265,9 +2277,9 @@
         late = jnp.concatenate([jnp.stack([sums_0[0], sums_0[1], sums_6[0]]), biases(dbias_a)], axis=0)
         small = small_reduced(jnp.concatenate([early, late], axis=0))
         table = lax.psum(dtable, ("seq", "fsdp"))
-    g_in, g_out, g_qkv, g_attn, g_conv_in, g_conv_out, g_taps, g_gain, g_shift, g_bias, total_table = finished(
-        main, share_in_b, share_out_b, small, table, n_tap, distance.shape
-    )
+    (
+        g_in, g_out, g_qkv, g_attn, g_conv_in, g_conv_out, g_taps, g_gain, g_shift, g_bias, total_table, outputs, grad_tokens
+    ) = finished(main, share_in_b, share_out_b, small, table, outputs, grad_tokens, n_tap, distance.shape)
     return (
         outputs,
         grad_tokens,

time: 658 us -> 656 us (level)
  no operation moved by 1% of the time
where the time goes in v5:
time: 656 us; the launch traced here: 647 us
  Pallas kernels  559 us (85%)
  waiting for transfers between devices  43.7 us (7%)
  between operations  15.8 us (2%)
  local copies, waits for them, and re-layouts  13.6 us (2%)
  other arithmetic  9.15 us (1%)
    pallas_call x1, Pallas kernels, last_reduced(): pl.pallas_call(last_kernel, in_specs=[vmem] * 8 + [anywhere] * 20, out_sp...  187 us
    pallas_call x8, Pallas kernels, call(): pl.pallas_call(kernel, grid=grid, in_specs=[spec(a.shape, b, w) for a, b,...  96.7 us
    pallas_call x1, Pallas kernels, first_forward(): pl.pallas_call(first_kernel, grid=(k,), in_specs=[anywhere] * 2 + [whole(...  82.6 us
    pallas_call x1, Pallas kernels, attend_back(): pl.pallas_call(functools.partial(bwd_kernel, with_part), grid=(pairs, STE...  80.9 us
    pallas_call x1, Pallas kernels, attend(): pl.pallas_call(fwd_kernel, grid=(pairs, STEPS), in_specs=[pl.BlockSpec(me...  55.1 us
    pallas_call x1, Pallas kernels, middle_back(): pl.pallas_call(middle_kernel, grid=(7,), in_specs=[pl.BlockSpec((t, d), l...  48.4 us
    all_gather x1, waiting for transfers between devices, on_device(): w_c = lax.all_gather(after(shard_c, w_b, cotangent, act_a), 'fsdp', axis=0)  15 us
    ppermute x1, waiting for transfers between devices, to_pairs(): lax.ppermute(jnp.where(place % 2 == 0, two, one), 'seq', [(0, 2), (1, 0),...  13.5 us
  transfers between devices with their start and end apart: 8, of which 6 were waited for; matrix products, arithmetic and copies ran while one was open for 2% of the time, Pallas kernels for 53%

profile of v5, /device:TPU:0, one launch (start us, length us, event | category | flops | bytes accessed | tf_op | source)
XLA Modules:
  0.0 647.1 jit_solution(7485368067146959980)
XLA Ops:
  7.2 2.7 fusion.7
  10.0 1.4 pad_maximum_fusion
  13.6 82.6 %first.1 = (bf16[512,4096]{1,0:T(8,128)(2,1)}, bf16[512,4096]{1,0:T(8,128)(2,1)}, bf16[4096,512]{1,0:T(8,128)(2,1)}, bf16[1024,512]{1,0:T(8,128)(2,1)}, bf16[512...) custom-call(bf16[2,256,1024]{2,1,0:T(8,128)(2,1)} %x_ref.1, ...), custom_call_target="tpu_custom_call" | custom-call | flops 30000001024 | bytes 100000000 | tf_op jit(solution)/shard_map/first/pallas_call | solution.py:1182
  97.2 1.6 collective-permute-start
  100.1 13.5 %collective-permute-done.1 = bf16[256,1024]{1,0:T(8,128)(2,1)} collective-permute-done((bf16[256,1024]{1,0:T(8,128)(2,1)}, bf16[256,1024]{1,0:T(8,128)(2,1)}, u32[]{:S(2)}, u32[]{:S(2)}) %collective-permute-start.1) | collective-permute-done | bytes 524320 | tf_op jit(solution)/shard_map/ppermute | solution.py:2109
  116.0 4.2 all-gather.7.cloned.1.call-done
  124.8 17.2 %out_qkv.1 = (f32[512,1024]{1,0:T(8,128)}, bf16[1024,512]{1,0:T(8,128)(2,1)}, bf16[4,3,512,128]{3,2,1,0:T(8,128)(2,1)}, bf16[4,3,512,128]{3,2,1,0:T(8,128)(2,1)}) custom-call(s32[1]{0:T(128)} %bitcast.12.odd_ref, bf16[512,1024]{1,0:T(8,128)(2,1)} %get-tuple-element.87.x_ref, bf16[512,4096]{1,0:T(8,128)(2,1)} %get-tuple-element.88.act_ref, ...), custom_call_target="tpu_custom_call" | custom-call | flops 7516192768 | bytes 25165824 | tf_op jit(solution)/shard_map/out_qkv/pallas_call | solution.py:399
  142.0 55.1 %attend_fwd.1 = (bf16[8,1024,1024]{2,1,0:T(8,128)(2,1)}, bf16[4,3,1024,128]{3,2,1,0:T(8,128)(2,1)}, bf16[512,1024]{1,0:T(8,128)(2,1)}) custom-call(s32[1]{0:T(128)} %bitcast.10.len_ref, bf16[128,512]{1,0:T(8,128)(2,1)} %maximum_maximum_fusion.wide_ref, bf16[128,128]{1,0:T(8,128)(2,1)} %pad_maximum_fusion.3.ends_ref, ...), custom_call_target="tpu_custom_call" | custom-call | flops 40000000000 | bytes 120000000 | tf_op jit(solution)/shard_map/attend_fwd/pallas_call | solution.py:321
  197.1 15.0 %all-gather.9.cloned.1.call-done = bf16[64,128,1024]{2,1,0:T(8,128)(2,1)} async-done(((bf16[8,128,1024]{2,1,0:T(8,128)(2,1)}), bf16[64,128,1024]{2,1,0:T(8,128)(2,1)}) %all-gather.9.cloned.1.call-update) | async-done | bytes 16777232 | tf_op jit(solution)/shard_map/all_gather | solution.py:2188
  215.8 11.1 %mid.1 = (f32[512,1024]{1,0:T(8,128)}, bf16[1024,512]{1,0:T(8,128)(2,1)}, bf16[1024,512]{1,0:T(8,128)(2,1)}, bf16[512,1024]{1,0:T(8,128)(2,1)}, bf16[512,1024]{1,0:T(8,128)(2,1)}, /*index=5*/bf16[512,1024]{1,0:T(8,128)(2,1)}) custom-call(f32[512,1024]{1,0:T(8,128)} %get-tuple-element.93.first_ref, bf16[512,1024]{1,0:T(8,128)(2,1)} %get-tuple-element.94.mixed_ref, ...), custom_call_target="tpu_custom_call" | custom-call | flops 3221225472 | bytes 16777216 | tf_op jit(solution)/shard_map/mid/pallas_call | solution.py:399
  227.8 3.4 collective-permute-start.2
  233.7 13.3 %conv.1 = (f32[512,1024]{1,0:T(8,128)}, bf16[1024,512]{1,0:T(8,128)(2,1)}, f32[512,1024]{1,0:T(8,128)}) custom-call(bf16[512,1024]{1,0:T(8,128)(2,1)} %get-tuple-element.97.gated_ref, bf16[32,1024]{1,0:T(8,128)(2,1)} %copy-done.9, f32[31,1024]{1,0:T(8,128)} %bitcast.124, f32[4,1024]{1,0:T(4,128)} %get-tuple-element.232.vec_ref, ...), custom_call_target="tpu_custom_call" | custom-call | flops 1073741824 | bytes 10485760 | tf_op jit(solution)/shard_map/conv/pallas_call | solution.py:399
  247.0 12.6 %ffn_in.1 = (bf16[512,4096]{1,0:T(8,128)(2,1)}, bf16[512,4096]{1,0:T(8,128)(2,1)}, bf16[4096,512]{1,0:T(8,128)(2,1)}, bf16[1024,512]{1,0:T(8,128)(2,1)}) custom-call(f32[512,1024]{1,0:T(8,128)} %get-tuple-element.99.x_ref.third_in, f32[2,1024]{1,0:T(2,128)} %pad_maximum_fusion.9.vec_ref, f32[4,1,1024]{2,1,0:T(1,128)} %reshape_squeeze.10.bias_ref, ...), custom_call_target="tpu_custom_call" | custom-call | flops 4294967296 | bytes 20971520 | tf_op jit(solution)/shard_map/ffn_in/pallas_call | solution.py:399
  259.6 9.4 %all-gather.11.cloned.1.call-done = bf16[32,128,1024]{2,1,0:T(8,128)(2,1)} async-done(((bf16[4,128,1024]{2,1,0:T(8,128)(2,1)}), bf16[32,128,1024]{2,1,0:T(8,128)(2,1)}) %all-gather.11.cloned.1.call-update) | async-done | bytes 8388624 | tf_op jit(solution)/shard_map/all_gather | solution.py:2193
  269.0 12.8 %out_last.1 = (bf16[512,1024]{1,0:T(8,128)(2,1)}, f32[512,1024]{1,0:T(8,128)}, bf16[512,1024]{1,0:T(8,128)(2,1)}, f32[8,1024]{1,0:T(8,128)}) custom-call(f32[512,1024]{1,0:T(8,128)} %get-tuple-element.99.x_ref.third_in, bf16[512,4096]{1,0:T(8,128)(2,1)} %get-tuple-element.100.act_ref, bf16[8,4,128,1024]{3,2,1,0:T(8,128)(2,1)} %bitcast.130, ...), custom_call_target="tpu_custom_call" | custom-call | flops 4294967296 | bytes 18874368 | tf_op jit(solution)/shard_map/out_last/pallas_call | solution.py:399
  281.8 8.8 %weight_grad.2 = bf16[8,4,128,1024]{3,2,1,0:T(8,128)(2,1)} custom-call(bf16[4096,512]{1,0:T(8,128)(2,1)} %get-tuple-element.103.left_ref, bf16[512,1024]{1,0:T(8,128)(2,1)} %get-tuple-element.104.right_ref.d_ref), custom_call_target="tpu_custom_call" | custom-call | flops 4294967296 | bytes 13631488 | tf_op jit(solution)/shard_map/weight_grad/pallas_call | solution.py:399
  290.6 11.7 %ffn_hidden_back.1 = (bf16[512,4096]{1,0:T(8,128)(2,1)}, bf16[512,1024]{1,0:T(8,128)(2,1)}, f32[4,1,1024]{2,1,0:T(1,128)}, f32[8,1024]{1,0:T(8,128)}) custom-call(bf16[512,1024]{1,0:T(8,128)(2,1)} %get-tuple-element.104.right_ref.d_ref, bf16[512,4096]{1,0:T(8,128)(2,1)} %get-tuple-element.105.inner_ref, bf16[8,4,128,1024]{3,2,1,0:T(8,128)(2,1)} %bitcast.131), custom_call_target="tpu_custom_call" | custom-call | flops 4294967296 | bytes 16777216 | tf_op jit(solution)/shard_map/ffn_hidden_back/pallas_call | solution.py:399
  302.4 9.2 %weight_grad.3 = bf16[8,4,128,1024]{3,2,1,0:T(8,128)(2,1)} custom-call(bf16[1024,512]{1,0:T(8,128)(2,1)} %get-tuple-element.107.left_ref, bf16[512,4096]{1,0:T(8,128)(2,1)} %get-tuple-element.108.right_ref.g_ref), custom_call_target="tpu_custom_call" | custom-call | flops 4294967296 | bytes 13631488 | tf_op jit(solution)/shard_map/weight_grad/pallas_call | solution.py:399
  311.6 1.4 slice.303.wide_ref
  313.6 48.4 %middle_back.1 = (f32[512,1024]{1,0:T(8,128)}, bf16[512,1024]{1,0:T(8,128)(2,1)}, bf16[4,512,128]{2,1,0:T(8,128)(2,1)}, bf16[4,512,128]{2,1,0:T(8,128)(2,1)}, f3...) custom-call(bf16[512,4096]{1,0:T(8,128)(2,1)} %get-tuple-element.108, ...), custom_call_target="tpu_custom_call" | custom-call | flops 40000000000 | bytes 120000000 | tf_op jit(solution)/shard_map/middle_back/pallas_call | solution.py:1402
  362.0 80.9 %attend_bwd.1 = (bf16[512,3072]{1,0:T(8,128)(2,1)}, f32[128,128]{1,0:T(8,128)}, bf16[4,128,1024]{2,1,0:T(8,128)(2,1)}) custom-call(bf16[4,3,1024,128]{3,2,1,0:T(8,128)(2,1)} %get-tuple-element.91.heads_ref, bf16[8,1024,1024]{2,1,0:T(8,128)(2,1)} %get-tuple-element.92.p_ref, bf16[128,128]{1,0:T(8,128)(2,1)} %slice.303.wide_ref, ...), custom_call_target="tpu_custom_call" | custom-call | flops 49999998976 | bytes 150000000 | tf_op jit(solution)/shard_map/attend_bwd/pallas_call | solution.py:340
  443.0 186.6 %last.1 = (bf16[15,128,1024]{2,1,0:T(8,128)(2,1)}, bf16[4,128,1024]{2,1,0:T(8,128)(2,1)}, f32[64,128]{1,0:T(8,128)}, f32[128,128]{1,0:T(8,128)}, bf16[2,256,1024]{2,1,0:T(8,128)(2,1)}) custom-call(f32[2,1024]{1,0:T(2,128)} %slice_bitcast_fusion.10.gain_ref, f32[128,128]{1,0:T(8,128)} %get-tuple-element.116.table_ref, ...), custom_call_target="tpu_custom_call" | custom-call | flops 99999997952 | bytes 400000000 | tf_op jit(solution)/shard_map/last/pallas_call | solution.py:1910
  629.6 9.1 %finish.1 = (f32[2,128,4096]{2,1,0:T(8,128)}, f32[2,4,128,1024]{3,2,1,0:T(8,128)}, f32[3,128,1024]{2,1,0:T(8,128)}, f32[128,1024]{1,0:T(8,128)}, f32[128,2048]{1...) custom-call(bf16[15,128,1024]{2,1,0:T(8,128)(2,1)} %get-tuple-elemen, ...), custom_call_target="tpu_custom_call" | custom-call | bytes 18000000 | tf_op jit(solution)/shard_map/finish/pallas_call | solution.py:2052
  638.7 1.5 copy.35
  (77 shorter events, 17.7 us)
Async XLA Ops:
  7.2 2.8 copy-start.3
  7.2 113.0 %all-gather.7.cloned.1.call-start = ((), (), s32[]{:S(2)}) async-start(), calls=%async_computation.4 | async-start | bytes 16515072 | tf_op jit(solution)/shard_map/all_gather | solution.py:2162
  10.0 2.3 copy-start.2
  11.4 200.7 %all-gather.9.cloned.1.call-start = ((), (), s32[]{:S(2)}) async-start(), calls=%async_computation.5 | async-start | bytes 18874368 | tf_op jit(solution)/shard_map/all_gather | solution.py:2188
  13.6 82.6 %copy-start = (bf16[2,256,1024]{2,1,0:T(8,128)(2,1)S(1)}, bf16[2,256,1024]{2,1,0:T(8,128)(2,1)}, u32[]{:S(2)}) copy-start(bf16[2,256,1024]{2,1,0:T(8,128)(2,1)} %param.27) | copy-start | bytes 3145732
  96.2 2.8 copy-start.5
  96.2 2.8 copy-start.4
  97.2 2.8 copy-start.6
  97.2 2.8 collective-permute-start
  98.8 14.7 %collective-permute-start.1 = (bf16[256,1024]{1,0:T(8,128)(2,1)}, bf16[256,1024]{1,0:T(8,128)(2,1)}, u32[]{:S(2)}, u32[]{:S(2)}) collective-permute-start(bf16[256,1024]{1,0:T(8,128)(2,1)} %get-tuple-element.205), channel_id=1, source_target_pairs={{0,16},{8,0},{16,24},{24,8},{1,17},{9,1},{17,25},{25,9},{2,18},{10... | collective-permute-start | bytes 1572872 | tf_op jit(solution)/shard_map/ppermute | solution.py:2109
  100.0 15.9 %copy-start.1 = (bf16[8,128,1024]{2,1,0:T(8,128)(2,1)}, bf16[8,128,1024]{2,1,0:T(8,128)(2,1)S(1)}, u32[]{:S(2)}) copy-start(bf16[8,128,1024]{2,1,0:T(8,128)(2,1)S(1)} %bitcast_dynamic-update-slice_fusion) | copy-start | bytes 6291460
  114.9 5.4 copy-start.10
  114.9 7.3 %copy-start.8 = (bf16[73,64]{0,1:T(8,128)(2,1)S(1)}, bf16[73,64]{0,1:T(8,128)(2,1)}, u32[]{:S(2)}) copy-start(bf16[73,64]{0,1:T(8,128)(2,1)} %param.26) | copy-start | bytes 28036
  114.9 7.6 %copy-start.7 = (bf16[8,64,128]{2,1,0:T(8,128)(2,1)S(1)}, bf16[8,64,128]{2,1,0:T(8,128)(2,1)}, u32[]{:S(2)}) copy-start(bf16[8,64,128]{2,1,0:T(8,128)(2,1)} %get-tuple-element.86) | copy-start | bytes 393220
  120.2 148.8 %all-gather.11.cloned.1.call-start = ((), (), s32[]{:S(2)}) async-start(), calls=%async_computation.6 | async-start | bytes 9437184 | tf_op jit(solution)/shard_map/all_gather | solution.py:2193
  212.1 149.9 %reduce-scatter.3.cloned.1.call-start = ((), (), s32[]{:S(2)}) async-start(), calls=%async_computation.2 | async-start | bytes 9437184 | tf_op jit(solution)/shard_map/reduce_scatter | solution.py:2206
  227.8 5.3 collective-permute-start.2
  233.1 0.6 copy-start.9
  290.6 152.4 %reduce-scatter.5.cloned.1.call-start = ((), (), s32[]{:S(2)}) async-start(), calls=%async_computation.3 | async-start | bytes 9437184 | tf_op jit(solution)/shard_map/reduce_scatter | solution.py:2209
Sparse Core Ops, SparseCore 0:
  11.5 108.6 all-gather.6
  122.7 89.4 all-gather.8
  214.6 54.3 all-gather.10
  290.7 71.2 reduce-scatter.2
  365.7 71.2 reduce-scatter.4

commit v6 on v5

--- a/solution.py
+++ b/solution.py
@@ -2156,8 +2156,6 @@
 
     shard_a = jnp.stack(chunks(ffn_in[0]))
     shard_b = jnp.concatenate([ffn_out[0].reshape(4, r, width), qkv], axis=0)
-    shard_c = jnp.stack(chunks(ffn_in[1]) + [attn_out] + chunks(conv_in) + [conv_out])
-    shard_d = ffn_out[1].reshape(4, r, width)
     if cubed:
         w_b = lax.all_gather(shard_b, "fsdp", axis=0)
         inner_a, act_a, act_t_a, unit_t_a, tokens, small, w_a = first_forward(
@@ -2185,7 +2183,12 @@
 
     if not cubed:
         inner_a, act_a, act_t_a, unit_t_a = ffn_in_forward(tokens, jnp.stack([gain[0], shift[0]]), bias[0], w_a, 0)
-    w_c = lax.all_gather(after(shard_c, w_b, cotangent, act_a), "fsdp", axis=0)
+    later_in, later_out, attn_out, conv_in, conv_out, _ = lax.optimization_barrier(
+        (ffn_in, ffn_out, attn_out, conv_in, conv_out, act_a)
+    )
+    shard_c = jnp.stack(chunks(later_in[1]) + [attn_out] + chunks(conv_in) + [conv_out])
+    shard_d = later_out[1].reshape(4, r, width)
+    w_c = lax.all_gather(after(shard_c, w_b, cotangent), "fsdp", axis=0)
     first, unit_t_1, mine, other = out_qkv_forward(
         odd_word, tokens, act_a, w_b, jnp.stack([shift[6], gain[1], shift[1], shift[8], shift[9]])
     )

time: 656 us -> 653 us (level)
  transfers between devices with their start and end apart: 8 -> 8, of which waited for: 6 -> 5; matrix products, arithmetic and copies ran while one was open for 2% -> 3% of each run, Pallas kernels for 53% -> 53%
where the time goes in v6:
time: 653 us; the launch traced here: 644 us
  Pallas kernels  559 us (86%)
  waiting for transfers between devices  41 us (6%)
  between operations  15.8 us (2%)
  local copies, waits for them, and re-layouts  14.3 us (2%)
  other arithmetic  9.15 us (1%)
    pallas_call x1, Pallas kernels, last_reduced(): pl.pallas_call(last_kernel, in_specs=[vmem] * 8 + [anywhere] * 20, out_sp...  187 us
    pallas_call x8, Pallas kernels, call(): pl.pallas_call(kernel, grid=grid, in_specs=[spec(a.shape, b, w) for a, b,...  97.3 us
    pallas_call x1, Pallas kernels, first_forward(): pl.pallas_call(first_kernel, grid=(k,), in_specs=[anywhere] * 2 + [whole(...  81.8 us
    pallas_call x1, Pallas kernels, attend_back(): pl.pallas_call(functools.partial(bwd_kernel, with_part), grid=(pairs, STE...  80.9 us
    pallas_call x1, Pallas kernels, attend(): pl.pallas_call(fwd_kernel, grid=(pairs, STEPS), in_specs=[pl.BlockSpec(me...  54.4 us
    pallas_call x1, Pallas kernels, middle_back(): pl.pallas_call(middle_kernel, grid=(7,), in_specs=[pl.BlockSpec((t, d), l...  48.4 us
    all_gather x1, waiting for transfers between devices, on_device(): w_c = lax.all_gather(after(shard_c, w_b, cotangent), 'fsdp', axis=0)  13.4 us
  transfers between devices with their start and end apart: 8, of which 5 were waited for; matrix products, arithmetic and copies ran while one was open for 3% of the time, Pallas kernels for 53%

profile of v6, /device:TPU:0, one launch (start us, length us, event | category | flops | bytes accessed | tf_op | source)
XLA Modules:
  0.0 644.2 jit_solution(8914958351716323112)
XLA Ops:
  8.6 1.4 pad_maximum_fusion
  12.2 81.8 %first.1 = (bf16[512,4096]{1,0:T(8,128)(2,1)}, bf16[512,4096]{1,0:T(8,128)(2,1)}, bf16[4096,512]{1,0:T(8,128)(2,1)}, bf16[1024,512]{1,0:T(8,128)(2,1)}, bf16[512...) custom-call(bf16[2,256,1024]{2,1,0:T(8,128)(2,1)} %x_ref.1, ...), custom_call_target="tpu_custom_call" | custom-call | flops 30000001024 | bytes 100000000 | tf_op jit(solution)/shard_map/first/pallas_call | solution.py:1182
  95.1 1.5 collective-permute-start
  98.8 12.5 %collective-permute-done.1 = bf16[256,1024]{1,0:T(8,128)(2,1)} collective-permute-done((bf16[256,1024]{1,0:T(8,128)(2,1)}, bf16[256,1024]{1,0:T(8,128)(2,1)}, u32[]{:S(2)}, u32[]{:S(2)}) %collective-permute-start.1) | collective-permute-done | bytes 524320 | tf_op jit(solution)/shard_map/ppermute | solution.py:2109
  111.3 1.3 bitcast_select_fusion.3
  113.7 4.9 all-gather.7.cloned.1.call-done
  124.2 17.7 %out_qkv.1 = (f32[512,1024]{1,0:T(8,128)}, bf16[1024,512]{1,0:T(8,128)(2,1)}, bf16[4,3,512,128]{3,2,1,0:T(8,128)(2,1)}, bf16[4,3,512,128]{3,2,1,0:T(8,128)(2,1)}) custom-call(s32[1]{0:T(128)} %bitcast.12.odd_ref, bf16[512,1024]{1,0:T(8,128)(2,1)} %get-tuple-element.92.x_ref, bf16[512,4096]{1,0:T(8,128)(2,1)} %get-tuple-element.93.act_ref, ...), custom_call_target="tpu_custom_call" | custom-call | flops 7516192768 | bytes 25165824 | tf_op jit(solution)/shard_map/out_qkv/pallas_call | solution.py:399
  141.9 54.4 %attend_fwd.1 = (bf16[8,1024,1024]{2,1,0:T(8,128)(2,1)}, bf16[4,3,1024,128]{3,2,1,0:T(8,128)(2,1)}, bf16[512,1024]{1,0:T(8,128)(2,1)}) custom-call(s32[1]{0:T(128)} %bitcast.10.len_ref, bf16[128,512]{1,0:T(8,128)(2,1)} %maximum_maximum_fusion.wide_ref, bf16[128,128]{1,0:T(8,128)(2,1)} %pad_maximum_fusion.3.ends_ref, ...), custom_call_target="tpu_custom_call" | custom-call | flops 40000000000 | bytes 120000000 | tf_op jit(solution)/shard_map/attend_fwd/pallas_call | solution.py:321
  196.4 13.4 %all-gather.9.cloned.1.call-done = bf16[64,128,1024]{2,1,0:T(8,128)(2,1)} async-done(((bf16[8,128,1024]{2,1,0:T(8,128)(2,1)}), bf16[64,128,1024]{2,1,0:T(8,128)(2,1)}) %all-gather.9.cloned.1.call-update) | async-done | bytes 16777232 | tf_op jit(solution)/shard_map/all_gather | solution.py:2191
  213.5 11.2 %mid.1 = (f32[512,1024]{1,0:T(8,128)}, bf16[1024,512]{1,0:T(8,128)(2,1)}, bf16[1024,512]{1,0:T(8,128)(2,1)}, bf16[512,1024]{1,0:T(8,128)(2,1)}, bf16[512,1024]{1,0:T(8,128)(2,1)}, /*index=5*/bf16[512,1024]{1,0:T(8,128)(2,1)}) custom-call(f32[512,1024]{1,0:T(8,128)} %get-tuple-element.98.first_ref, bf16[512,1024]{1,0:T(8,128)(2,1)} %get-tuple-element.99.mixed_ref, ...), custom_call_target="tpu_custom_call" | custom-call | flops 3221225472 | bytes 16777216 | tf_op jit(solution)/shard_map/mid/pallas_call | solution.py:399
  225.5 3.4 collective-permute-start.2
  231.4 13.3 %conv.1 = (f32[512,1024]{1,0:T(8,128)}, bf16[1024,512]{1,0:T(8,128)(2,1)}, f32[512,1024]{1,0:T(8,128)}) custom-call(bf16[512,1024]{1,0:T(8,128)(2,1)} %get-tuple-element.106.gated_ref, bf16[32,1024]{1,0:T(8,128)(2,1)} %copy-done.10, f32[31,1024]{1,0:T(8,128)} %bitcast.124, f32[4,1024]{1,0:T(4,128)} %get-tuple-element.238.vec_ref, ...), custom_call_target="tpu_custom_call" | custom-call | flops 1073741824 | bytes 10485760 | tf_op jit(solution)/shard_map/conv/pallas_call | solution.py:399
  244.7 12.6 %ffn_in.1 = (bf16[512,4096]{1,0:T(8,128)(2,1)}, bf16[512,4096]{1,0:T(8,128)(2,1)}, bf16[4096,512]{1,0:T(8,128)(2,1)}, bf16[1024,512]{1,0:T(8,128)(2,1)}) custom-call(f32[512,1024]{1,0:T(8,128)} %get-tuple-element.108.x_ref.third_in, f32[2,1024]{1,0:T(2,128)} %pad_maximum_fusion.9.vec_ref, f32[4,1,1024]{2,1,0:T(1,128)} %reshape_squeeze.10.bias_ref, ...), custom_call_target="tpu_custom_call" | custom-call | flops 4294967296 | bytes 20971520 | tf_op jit(solution)/shard_map/ffn_in/pallas_call | solution.py:399
  257.3 8.8 %all-gather.11.cloned.1.call-done = bf16[32,128,1024]{2,1,0:T(8,128)(2,1)} async-done(((bf16[4,128,1024]{2,1,0:T(8,128)(2,1)}), bf16[32,128,1024]{2,1,0:T(8,128)(2,1)}) %all-gather.11.cloned.1.call-update) | async-done | bytes 8388624 | tf_op jit(solution)/shard_map/all_gather | solution.py:2196
  266.1 12.8 %out_last.1 = (bf16[512,1024]{1,0:T(8,128)(2,1)}, f32[512,1024]{1,0:T(8,128)}, bf16[512,1024]{1,0:T(8,128)(2,1)}, f32[8,1024]{1,0:T(8,128)}) custom-call(f32[512,1024]{1,0:T(8,128)} %get-tuple-element.108.x_ref.third_in, bf16[512,4096]{1,0:T(8,128)(2,1)} %get-tuple-element.109.act_ref, bf16[8,4,128,1024]{3,2,1,0:T(8,128)(2,1)} %bitcast.130, ...), custom_call_target="tpu_custom_call" | custom-call | flops 4294967296 | bytes 18874368 | tf_op jit(solution)/shard_map/out_last/pallas_call | solution.py:399
  278.9 8.8 %weight_grad.2 = bf16[8,4,128,1024]{3,2,1,0:T(8,128)(2,1)} custom-call(bf16[4096,512]{1,0:T(8,128)(2,1)} %get-tuple-element.113.left_ref, bf16[512,1024]{1,0:T(8,128)(2,1)} %get-tuple-element.114.right_ref.d_ref), custom_call_target="tpu_custom_call" | custom-call | flops 4294967296 | bytes 13631488 | tf_op jit(solution)/shard_map/weight_grad/pallas_call | solution.py:399
  287.8 11.7 %ffn_hidden_back.1 = (bf16[512,4096]{1,0:T(8,128)(2,1)}, bf16[512,1024]{1,0:T(8,128)(2,1)}, f32[4,1,1024]{2,1,0:T(1,128)}, f32[8,1024]{1,0:T(8,128)}) custom-call(bf16[512,1024]{1,0:T(8,128)(2,1)} %get-tuple-element.114.right_ref.d_ref, bf16[512,4096]{1,0:T(8,128)(2,1)} %get-tuple-element.115.inner_ref, bf16[8,4,128,1024]{3,2,1,0:T(8,128)(2,1)} %bitcast.131), custom_call_target="tpu_custom_call" | custom-call | flops 4294967296 | bytes 16777216 | tf_op jit(solution)/shard_map/ffn_hidden_back/pallas_call | solution.py:399
  299.5 9.2 %weight_grad.3 = bf16[8,4,128,1024]{3,2,1,0:T(8,128)(2,1)} custom-call(bf16[1024,512]{1,0:T(8,128)(2,1)} %get-tuple-element.117.left_ref, bf16[512,4096]{1,0:T(8,128)(2,1)} %get-tuple-element.118.right_ref.g_ref), custom_call_target="tpu_custom_call" | custom-call | flops 4294967296 | bytes 13631488 | tf_op jit(solution)/shard_map/weight_grad/pallas_call | solution.py:399
  308.7 1.4 slice.303.wide_ref
  310.7 48.4 %middle_back.1 = (f32[512,1024]{1,0:T(8,128)}, bf16[512,1024]{1,0:T(8,128)(2,1)}, bf16[4,512,128]{2,1,0:T(8,128)(2,1)}, bf16[4,512,128]{2,1,0:T(8,128)(2,1)}, f3...) custom-call(bf16[512,4096]{1,0:T(8,128)(2,1)} %get-tuple-element.118, ...), custom_call_target="tpu_custom_call" | custom-call | flops 40000000000 | bytes 120000000 | tf_op jit(solution)/shard_map/middle_back/pallas_call | solution.py:1402
  359.2 80.9 %attend_bwd.1 = (bf16[512,3072]{1,0:T(8,128)(2,1)}, f32[128,128]{1,0:T(8,128)}, bf16[4,128,1024]{2,1,0:T(8,128)(2,1)}) custom-call(bf16[4,3,1024,128]{3,2,1,0:T(8,128)(2,1)} %get-tuple-element.96.heads_ref, bf16[8,1024,1024]{2,1,0:T(8,128)(2,1)} %get-tuple-element.97.p_ref, bf16[128,128]{1,0:T(8,128)(2,1)} %slice.303.wide_ref, ...), custom_call_target="tpu_custom_call" | custom-call | flops 49999998976 | bytes 150000000 | tf_op jit(solution)/shard_map/attend_bwd/pallas_call | solution.py:340
  440.1 186.6 %last.1 = (bf16[15,128,1024]{2,1,0:T(8,128)(2,1)}, bf16[4,128,1024]{2,1,0:T(8,128)(2,1)}, f32[64,128]{1,0:T(8,128)}, f32[128,128]{1,0:T(8,128)}, bf16[2,256,1024]{2,1,0:T(8,128)(2,1)}) custom-call(f32[2,1024]{1,0:T(2,128)} %slice_bitcast_fusion.10.gain_ref, f32[128,128]{1,0:T(8,128)} %get-tuple-element.126.table_ref, ...), custom_call_target="tpu_custom_call" | custom-call | flops 99999997952 | bytes 400000000 | tf_op jit(solution)/shard_map/last/pallas_call | solution.py:1910
  626.7 9.1 %finish.1 = (f32[2,128,4096]{2,1,0:T(8,128)}, f32[2,4,128,1024]{3,2,1,0:T(8,128)}, f32[3,128,1024]{2,1,0:T(8,128)}, f32[128,1024]{1,0:T(8,128)}, f32[128,2048]{1...) custom-call(bf16[15,128,1024]{2,1,0:T(8,128)(2,1)} %get-tuple-elemen, ...), custom_call_target="tpu_custom_call" | custom-call | bytes 18000000 | tf_op jit(solution)/shard_map/finish/pallas_call | solution.py:2052
  635.8 1.5 copy.35
  (82 shorter events, 19.7 us)
Async XLA Ops:
  7.2 1.2 slice-start
  7.2 111.3 %all-gather.7.cloned.1.call-start = ((), (), s32[]{:S(2)}) async-start(), calls=%async_computation.4 | async-start | bytes 16515072 | tf_op jit(solution)/shard_map/all_gather | solution.py:2160
  7.2 1.4 copy-start.4
  8.6 2.3 copy-start.3
  10.1 199.7 %all-gather.9.cloned.1.call-start = ((), (), s32[]{:S(2)}) async-start(), calls=%async_computation.5 | async-start | bytes 18874368 | tf_op jit(solution)/shard_map/all_gather | solution.py:2191
  12.2 81.9 %copy-start.1 = (bf16[2,256,1024]{2,1,0:T(8,128)(2,1)S(1)}, bf16[2,256,1024]{2,1,0:T(8,128)(2,1)}, u32[]{:S(2)}) copy-start(bf16[2,256,1024]{2,1,0:T(8,128)(2,1)} %param.27) | copy-start | bytes 3145732
  95.1 3.7 collective-permute-start
  96.6 0.9 copy-start.6
  96.6 1.1 copy-start.5
  96.6 14.7 %collective-permute-start.1 = (bf16[256,1024]{1,0:T(8,128)(2,1)}, bf16[256,1024]{1,0:T(8,128)(2,1)}, u32[]{:S(2)}, u32[]{:S(2)}) collective-permute-start(bf16[256,1024]{1,0:T(8,128)(2,1)} %get-tuple-element.211), channel_id=1, source_target_pairs={{0,16},{8,0},{16,24},{24,8},{1,17},{9,1},{17,25},{25,9},{2,18},{10... | collective-permute-start | bytes 1572872 | tf_op jit(solution)/shard_map/ppermute | solution.py:2109
  96.7 2.0 copy-start.7
  98.7 13.8 %copy-start.2 = (bf16[8,128,1024]{2,1,0:T(8,128)(2,1)}, bf16[8,128,1024]{2,1,0:T(8,128)(2,1)S(1)}, u32[]{:S(2)}) copy-start(bf16[8,128,1024]{2,1,0:T(8,128)(2,1)S(1)} %bitcast_dynamic-update-slice_fusion) | copy-start | bytes 6291460
  112.6 6.0 copy-start
  118.5 1.2 copy-start.11
  118.5 3.0 copy-start.9
  118.5 3.3 copy-start.8
  118.6 147.5 %all-gather.11.cloned.1.call-start = ((), (), s32[]{:S(2)}) async-start(), calls=%async_computation.6 | async-start | bytes 9437184 | tf_op jit(solution)/shard_map/all_gather | solution.py:2196
  209.8 149.3 %reduce-scatter.3.cloned.1.call-start = ((), (), s32[]{:S(2)}) async-start(), calls=%async_computation.2 | async-start | bytes 9437184 | tf_op jit(solution)/shard_map/reduce_scatter | solution.py:2209
  225.5 5.3 collective-permute-start.2
  230.8 0.6 copy-start.10
  287.7 152.4 %reduce-scatter.5.cloned.1.call-start = ((), (), s32[]{:S(2)}) async-start(), calls=%async_computation.3 | async-start | bytes 9437184 | tf_op jit(solution)/shard_map/reduce_scatter | solution.py:2212
Sparse Core Ops, SparseCore 0:
  10.5 108.0 all-gather.6
  121.0 88.7 all-gather.8
  211.7 54.3 all-gather.10
  287.8 71.2 reduce-scatter.2
  362.9 71.3 reduce-scatter.4
